TPU v7x, 32 devices: a whole 2x2x4 slice. The times are simulated.
32 devices in a mesh: bx: 4 (over y, x), by: 2 (over core), bz: 4 (over z).
Axes of the slice: x: 2, y: 2, z: 4, core: 2. Of those that a mesh axis runs over, the one named last changes fastest.
Arguments:
- counts: bfloat16 [64, 64, 128, 128], P(('bx', 'by', 'bz')), may hold values from 0.099609375 to 10
- row_split: bfloat16 [64, 64, 128, 256], P(('bx', 'by', 'bz')), may hold values from 0 to 0.03125
- col_split: bfloat16 [64, 64, 128, 256], P(('bx', 'by', 'bz')), may hold values from 0 to 0.03125
- efficiency: bfloat16 [64, 128, 128], replicated, may hold values from 0.5 to 1.5
- lorentz: float32 [3600], replicated, may hold values from 0.3 to 3
- angles: int32 [64], P(('bx', 'by', 'bz')), may hold values from 0 to 3599
- tile_owner: int32 [4096, 1], P(('bx', 'by', 'bz')), may hold values from 0 to 31; in each aligned block of 128 rows (0 to 127, 128 to 255, ...) at most 16 rows name the same one
- tile_box: int32 [4096], P(('bx', 'by', 'bz')), may hold values from 0 to 511
Outputs:
- intensity: float32 [8, 8, 4, 64, 256], P('bx', 'by', 'bz')
Inputs may be any that keep to these rules, and one draw needn't show every extreme that they name: `tile_owner`: among the 128 tiles of one device, no owner is named more than 16 times, a bound that some block reaches.
All inputs are finite; a program needn't handle non-finite values.
Results may differ from a plain program's by a relative error of at most 0.0003.
Values sent between devices are 32-bit elements; how exact they have to be, the bound alone decides.
No kernel may reach another device: no remote copies, remote signals or barrier semaphores. Data moves between devices by JAX's collectives and lax.ppermute only.
A program may use at most 128 MiB of HBM per device.

v0:
```python
import functools

import jax
import jax.numpy as jnp
from jax import lax
from jax.experimental import pallas as pl
from jax.experimental.pallas import tpu as pltpu
from jax.sharding import PartitionSpec as P

VOX = 256
LANES = 128
GX = 8
GY = 8
GZ = 4
BOX_BRICK = 64
FLIP_VOX = (0b11100000, 0b00011100, 0b00000011)
FLIP_BOX = (0b110000, 0b001100, 0b000011)
AXES = ("bx", "by", "bz")
POSITIONS = 8
TILE_LIMIT = 56 * 1024 * 1024
VMEM_LIMIT = 24 * 1024 * 1024
LARGE = 10**10
SWAPPED = (0, 4, 2, 6, 1, 5, 3, 7)
PIXEL_ROWS = 64


class Plan:
    def __init__(self, mesh):
        self.sx, self.sy, self.sz = (mesh.shape[name] for name in AXES)
        self.devices = self.sx * self.sy * self.sz
        lx, ly, lz = GX // self.sx, GY // self.sy, GZ // self.sz
        self.boxes = lx * ly * lz * BOX_BRICK
        self.share = self.boxes // 8
        self.flip_dev = ((self.sx - 1) * self.sy * self.sz, (self.sy - 1) * self.sz, self.sz - 1)
        self.half = (self.sx * self.sy * self.sz // 2, self.sy * self.sz // 2, self.sz // 2)
        self.flip_local = (
            (lx - 1) * ly * lz * BOX_BRICK + FLIP_BOX[0],
            (ly - 1) * lz * BOX_BRICK + FLIP_BOX[1],
            (lz - 1) * BOX_BRICK + FLIP_BOX[2],
        )

    def upper(self, device):
        return [(device & half) != 0 for half in self.half]

    def steps(self):
        row = self.sy * self.sz
        return (row, 1), (2 * row, 2)

    def box_row(self, place):
        (gather_a, gather_b), (first, second) = self.steps()
        has = lambda mask: (place & (mask * self.share)) != 0
        other_y = place // (self.sz * self.share) % self.sy
        odd = ((other_y ^ lax.axis_index("by")) & 1) != 0
        part = jnp.where(has(first), jnp.where(odd, 1, 2), 0) + jnp.where(has(second), jnp.where(odd, 2, 1), 0)
        row = (other_y * 4 + part) * self.share + place % self.share
        return jnp.where(has(gather_a) | has(gather_b), -1, row)

    def here(self):
        return (lax.axis_index("bx") * self.sy + lax.axis_index("by")) * self.sz + lax.axis_index("bz")


def masked(flags, masks):
    total = jnp.where(flags[0], masks[0], 0)
    for flag, mask in zip(flags[1:], masks[1:]):
        total = total ^ jnp.where(flag, mask, 0)
    return total


def lane_gather(values, index):
    return jnp.take_along_axis(values, index, axis=1, mode="promise_in_bounds")


def destination(plan, owner, box):
    upper = plan.upper(owner)
    local = box ^ masked(upper, plan.flip_local)
    part = local // plan.share
    row = local % plan.share
    holder = owner ^ masked(upper, plan.flip_dev)
    holder = holder ^ masked([(part & bit) != 0 for bit in (4, 2, 1)], plan.flip_dev)
    return holder * plan.share + row


def accumulate_kernel(plan, angles, lorentz, owner, box, counts, rows, cols, seen, value_out, weight_out, *scratch):
    arrays, sems, turned, partial = scratch[:4], scratch[4], scratch[5], scratch[6]
    frames, positions = counts.shape[0], counts.shape[1]
    blocks = positions // POSITIONS

    def copies(block):
        span = pl.ds(block * POSITIONS, POSITIONS)
        views = [(ref.at[:, span], held.at[:, span]) for ref, held in zip((counts, rows, cols), arrays)]
        views.append((seen.at[span], arrays[3].at[span]))
        return [pltpu.make_async_copy(src, dst, sems.at[block, i]) for i, (src, dst) in enumerate(views)]

    for block in range(blocks):
        for copy in copies(block):
            copy.start()

    tiles = frames * positions
    across = lax.broadcasted_iota(jnp.int32, (tiles, tiles), 1)
    down = lax.broadcasted_iota(jnp.int32, (tiles, tiles), 0)
    flips = masked(plan.upper(owner[...]), FLIP_VOX)
    turned[...] = jnp.sum(jnp.where(across == down, flips, 0), axis=1, keepdims=True)
    ids = destination(plan, owner[...], box[...])
    for out in (value_out, weight_out):
        out[tiles : tiles + 8, :] = jnp.zeros((8, VOX), jnp.float32)
        out[tiles : tiles + 8, :tiles] = jnp.broadcast_to(ids.astype(jnp.float32), (8, tiles))

    held_counts, held_rows, held_cols, held_seen = arrays

    def compute(block):
        for p in range(POSITIONS):
            at = block * POSITIONS + p
            for f in range(frames):
                weights = held_cols[f, at]
                for kind in range(2):
                    total = None
                    for start in range(0, held_rows.shape[2], PIXEL_ROWS):
                        span = pl.ds(start, PIXEL_ROWS)
                        pixels = held_seen[at, span, :] if kind else held_counts[f, at, span, :]
                        item = jnp.dot(pixels, weights, preferred_element_type=jnp.float32)
                        item = held_rows[f, at, span, :].astype(jnp.float32) * item
                        item = jnp.sum(item.reshape(-1, 8, VOX), axis=0)
                        total = item if total is None else total + item
                    partial[f, kind, 0, p * 8 : (p + 1) * 8, :] = total[:, :LANES]
                    partial[f, kind, 1, p * 8 : (p + 1) * 8, :] = total[:, LANES:]

    def finish(block):
        lanes = lax.broadcasted_iota(jnp.int32, (POSITIONS, LANES), 1)
        for f in range(frames):
            place = pl.ds(pl.multiple_of(f * positions + block * POSITIONS, POSITIONS), POSITIONS)
            mask = jnp.broadcast_to(turned[place, :], (POSITIONS, LANES))
            index = lanes ^ (mask & (LANES - 1))
            swap = (mask & LANES) != 0
            for kind, out in enumerate((value_out, weight_out)):
                low, high = (
                    sum(partial[f, kind, half, pl.ds(row, POSITIONS, stride=8), :] for row in range(8))
                    for half in range(2)
                )
                scale = lorentz[angles[f]] if kind == 0 else 1.0
                out[place, :LANES] = lane_gather(jnp.where(swap, high, low), index) * scale
                out[place, LANES:] = lane_gather(jnp.where(swap, low, high), index) * scale

    @pl.loop(0, blocks)
    def _(block):
        for copy in copies(block):
            copy.wait()
        compute(block)
        finish(block)


def accumulate(plan, counts, row_split, col_split, efficiency, lorentz, angles, owner, box):
    frames, positions, pixels, _ = counts.shape
    tiles = frames * positions
    arrays = (counts, row_split, col_split, efficiency)
    return pl.pallas_call(
        functools.partial(accumulate_kernel, plan),
        in_specs=[pl.BlockSpec(memory_space=pltpu.SMEM)] * 2
        + [pl.BlockSpec(memory_space=pltpu.VMEM)] * 2
        + [pl.BlockSpec(memory_space=pl.ANY)] * 4,
        out_specs=[pl.BlockSpec(memory_space=pltpu.VMEM)] * 2,
        out_shape=[jax.ShapeDtypeStruct((tiles + 8, VOX), jnp.float32)] * 2,
        scratch_shapes=[pltpu.VMEM(array.shape, array.dtype) for array in arrays]
        + [
            pltpu.SemaphoreType.DMA((positions // POSITIONS, 4)),
            pltpu.VMEM((tiles, 1), jnp.int32),
            pltpu.VMEM((frames, 2, 2, 8 * POSITIONS, LANES), jnp.float32),
        ],
        compiler_params=pltpu.CompilerParams(vmem_limit_bytes=TILE_LIMIT),
        cost_estimate=pl.CostEstimate(
            flops=4 * tiles * pixels * pixels * VOX,
            bytes_accessed=sum(array.size * 2 for array in arrays),
            transcendentals=0,
        ),
        name="tile_sums",
    )(angles, lorentz, owner, box, *arrays)


def scatter_kernel(plan, olds, outs, payload, *refs):
    before, after = refs[:olds], refs[len(refs) - outs :]
    tiles = LANES
    half = payload.shape[0] // 2
    ids = [payload[start + tiles : start + tiles + 1, :tiles] for start in (0, half)]
    ids = plan.box_row(jnp.concatenate(ids, axis=1).astype(jnp.int32) ^ (plan.here() * plan.share))
    values = jnp.concatenate([payload[:tiles, :], payload[half : half + tiles, :]], axis=0)
    high = values.astype(jnp.bfloat16)
    low = (values - high.astype(jnp.float32)).astype(jnp.bfloat16)
    for number, out in enumerate(after):
        boxes = lax.broadcasted_iota(jnp.int32, (out.shape[0], ids.shape[1]), 0) + number * out.shape[0]
        pick = (boxes == ids).astype(jnp.float32).astype(jnp.bfloat16)
        total = jnp.dot(pick, high, preferred_element_type=jnp.float32)
        total = total + jnp.dot(pick, low, preferred_element_type=jnp.float32)
        out[...] = total + before[number][...] if olds else total


def stage_kernel(first, second, first_out, second_out):
    first_out[...] = first[...]
    second_out[...] = second[...]


def join_kernel(first, second, *rest):
    half, out = first.shape[0], rest[-1]
    out[:half, :] = first[...]
    out[half:, :] = second[...]


def add_kernel(count, *refs):
    inputs, outs = refs[:count], refs[count:]
    start = 0
    for out in outs:
        span = slice(start, start + out.shape[0])
        total = inputs[0][span, :]
        for ref in inputs[1:]:
            total = total + ref[span, :]
        out[...] = total
        start += out.shape[0]


def intensity_kernel(value, *refs):
    inputs, out = refs[:-1], refs[-1]
    weight = inputs[0][...]
    for ref in inputs[1:]:
        weight = weight + ref[...]
    out[...] = value[...] * 0.125 / jnp.maximum(weight * 0.125, 1.0)


def unfold_kernel(plan, *refs):
    inputs, out = refs[:-1], refs[-1]
    upper = plan.upper(plan.here())
    own = masked(upper, (4, 2, 1))
    local = masked(upper, plan.flip_local)
    mask = masked(upper, FLIP_VOX)
    index = lax.broadcasted_iota(jnp.int32, (8, LANES), 1) ^ (mask & (LANES - 1))
    turn = lax.broadcasted_iota(jnp.int32, (8, LANES), 0) ^ (local & 7)
    swap = (mask & LANES) != 0
    odd = (lax.axis_index("by") & 1) != 0
    for number, ref in enumerate(inputs):
        codes = (number, SWAPPED[number])
        far = (number & 2) != 0
        relative = jnp.where(odd, codes[1 - far], codes[far])
        base = (relative ^ own) * plan.share
        for group in range(0, plan.share, 8):
            rows = ref[group : group + 8, :]
            low, high = rows[:, :LANES], rows[:, LANES:]
            target = (base + group) ^ (local & ~7)
            place = pl.ds(pl.multiple_of(target, 8), 8)
            for at, item in enumerate((jnp.where(swap, high, low), jnp.where(swap, low, high))):
                item = jnp.take_along_axis(item, turn, axis=0, mode="promise_in_bounds")
                out[place, at * LANES : (at + 1) * LANES] = lane_gather(item, index)


def small_call(kernel, shapes, name, *arrays, flops=1):
    return pl.pallas_call(
        kernel,
        out_shape=[jax.ShapeDtypeStruct(shape, jnp.float32) for shape in shapes],
        compiler_params=pltpu.CompilerParams(vmem_limit_bytes=VMEM_LIMIT),
        cost_estimate=pl.CostEstimate(flops=flops, bytes_accessed=1, transcendentals=0),
        name=name,
    )(*arrays)


def shards(plan, counts, row_split, col_split, efficiency, lorentz, angles, tile_owner, tile_box):
    def swap(array, even, odd=None):
        odd = even if odd is None else odd
        pairs = [(i, i ^ (odd if i // plan.sz % 2 else even)) for i in range(plan.devices)]
        return lax.ppermute(array, AXES, pairs)

    def join(first, second, *order):
        rows, width = first.shape
        return small_call(join_kernel, [(2 * rows, width)], "join", first, second, *order)[0]

    gather_steps, reduce_steps = plan.steps()
    owner = tile_owner.reshape(1, -1)
    box = tile_box.reshape(1, -1)
    own = accumulate(plan, counts, row_split, col_split, efficiency, lorentz, angles, owner, box)
    arrived = [swap(array, *gather_steps) for array in own]
    held = small_call(stage_kernel, [array.shape for array in own], "stage", *own, flops=LARGE)
    near = [join(held[0], arrived[0])]
    near.append(join(held[1], arrived[1], near[0]))
    far = [swap(array, *gather_steps[::-1]) for array in near]
    def box_sums(payload, olds, *waits, flops=1):
        kernel = functools.partial(scatter_kernel, plan, len(olds), plan.sy)
        shapes = [(4 * plan.share, VOX)] * plan.sy
        return small_call(kernel, shapes, "box_sums", payload, *olds, *waits, flops=flops)

    def added(arrays, pieces, flops=1):
        shape = (arrays[0].shape[0] // pieces, VOX)
        kernel = functools.partial(add_kernel, len(arrays))
        return small_call(kernel, [shape] * pieces, "added", *arrays, flops=flops)

    sums = [box_sums(near[0], []), box_sums(near[1], [], flops=LARGE)]
    pairs, waits = [], [sums[1][0]]
    for kind in range(2):
        parts = box_sums(far[kind], sums[kind], *waits, flops=LARGE if kind else 1)
        waits = [parts[0]]
        parts = [parts[0]] + [swap(parts[i], i * plan.sz) for i in range(1, plan.sy)]
        for even, odd in (reduce_steps, reduce_steps[::-1]):
            keep, give = added(parts, 2)
            parts = [keep, swap(give, even, odd)]
        pairs.append(parts)
    (value,) = added(pairs[0], 1, flops=LARGE)
    (own,) = small_call(intensity_kernel, [(plan.share, VOX)], "intensity", value, *pairs[1])
    flip_x, flip_y, flip_z = plan.flip_dev
    near = [own, swap(own, flip_z, flip_x), swap(own, flip_x, flip_z)]
    near.append(swap(near[1], flip_x, flip_z))
    far = [swap(array, flip_y) for array in near]
    ordered = [near[0], near[1], far[0], far[1], near[2], near[3], far[2], far[3]]
    (result,) = small_call(functools.partial(unfold_kernel, plan), [(plan.boxes, VOX)], "unfold", *ordered)
    return result.reshape(GX // plan.sx, GY // plan.sy, GZ // plan.sz, BOX_BRICK, VOX)


def solution(mesh):
    return jax.shard_map(
        functools.partial(shards, Plan(mesh)),
        mesh=mesh,
        in_specs=(
            P(AXES, None, None, None),
            P(AXES, None, None, None),
            P(AXES, None, None, None),
            P(),
            P(),
            P(AXES),
            P(AXES, None),
            P(AXES),
        ),
        out_specs=P("bx", "by", "bz", None, None),
        check_vma=False,
    )
```

profile of v0, /device:TPU:0, one launch (start us, length us, event | category | flops | bytes accessed | tf_op | source)
XLA Modules:
  0.0 53.7 jit_solution(18054149111090232994)
XLA Ops:
  0.0 10.2 %tile_sums.1 = (f32[136,256]{1,0:T(8,128)}, f32[136,256]{1,0:T(8,128)}) custom-call(s32[2]{0:T(128)} %angles.1, f32[3600]{0:T(1024)} %lorentz.1, s32[1,128]{1,0:T(1,128)} %bitcast.5, s32[1,128]{1,0:T(1,128)} %bitcast.6, bf16[2,64,128,128]{3,2,1,0:T(8,128)(2,1)} %counts.1, bf16[2,64,128,256]{3,2,1,0:T(8,128)(2,1)} %rows.1, bf16[2,64,128,256]{3,2,1,0:T(8,128)(2,1)} %cols.1, ...), custom_call_target="tpu_custom_call" | custom-call | flops 2147483648 | bytes 23068672 | tf_op jit(solution)/shard_map/tile_sums/pallas_call | solution.py:155
  10.2 3.0 %collective-permute-start = (f32[136,256]{1,0:T(8,128)}, f32[136,256]{1,0:T(8,128)S(1)}, u32[]{:S(2)}, u32[]{:S(2)}) collective-permute-start(f32[136,256]{1,0:T(8,128)} %get-tuple-element.25.first), channel_id=1, source_target_pairs={{0,8},{1,9},{2,10},{3,11},{4,5},{5,4},{6,7},{7,6},{8,0},{9,1},{10,... | collective-permute-start | bytes 417800 | tf_op jit(solution)/shard_map/ppermute | solution.py:265
  13.3 0.9 %copy-done = f32[136,256]{1,0:T(8,128)S(1)} copy-done((f32[136,256]{1,0:T(8,128)S(1)}, f32[136,256]{1,0:T(8,128)}, u32[]{:S(2)}) %copy-start) | copy-done | bytes 139288
  14.2 0.9 %copy-done.1 = f32[136,256]{1,0:T(8,128)S(1)} copy-done((f32[136,256]{1,0:T(8,128)S(1)}, f32[136,256]{1,0:T(8,128)}, u32[]{:S(2)}) %copy-start.1) | copy-done | bytes 139288
  15.2 1.3 %collective-permute-done.second = f32[136,256]{1,0:T(8,128)S(1)} collective-permute-done((f32[136,256]{1,0:T(8,128)}, f32[136,256]{1,0:T(8,128)S(1)}, u32[]{:S(2)}, u32[]{:S(2)}) %collective-permute-start) | collective-permute-done | bytes 139296 | tf_op jit(solution)/shard_map/ppermute | solution.py:265
  16.5 2.2 %collective-permute-start.1 = (f32[272,256]{1,0:T(8,128)S(1)}, f32[272,256]{1,0:T(8,128)S(1)}, u32[]{:S(2)}, u32[]{:S(2)}) collective-permute-start(f32[272,256]{1,0:T(8,128)S(1)} %join.2.payload.rest_0_), channel_id=1, source_target_pairs={{0,1},{1,0},{2,3},{3,2},{4,12},{5,13},{6,14},{7,15},{8,9},{9,8},{1... | collective-permute-start | bytes 835592 | tf_op jit(solution)/shard_map/ppermute | solution.py:265
  18.7 1.5 %collective-permute-start.6 = (f32[272,256]{1,0:T(8,128)S(1)}, f32[272,256]{1,0:T(8,128)S(1)}, u32[]{:S(2)}, u32[]{:S(2)}) collective-permute-start(f32[272,256]{1,0:T(8,128)S(1)} %join.3.payload), channel_id=1, source_target_pairs={{0,1},{1,0},{2,3},{3,2},{4,12},{5,13},{6,14},{7,15},{8,9},{9,8},{1... | collective-permute-start | bytes 835592 | tf_op jit(solution)/shard_map/ppermute | solution.py:265
  20.8 2.4 %collective-permute-done.1.payload = f32[272,256]{1,0:T(8,128)S(1)} collective-permute-done((f32[272,256]{1,0:T(8,128)S(1)}, f32[272,256]{1,0:T(8,128)S(1)}, u32[]{:S(2)}, u32[]{:S(2)}) %collective-permute-start.1) | collective-permute-done | bytes 278560 | tf_op jit(solution)/shard_map/ppermute | solution.py:265
  23.6 2.6 %collective-permute-done.6.payload = f32[272,256]{1,0:T(8,128)S(1)} collective-permute-done((f32[272,256]{1,0:T(8,128)S(1)}, f32[272,256]{1,0:T(8,128)S(1)}, u32[]{:S(2)}, u32[]{:S(2)}) %collective-permute-start.6) | collective-permute-done | bytes 278560 | tf_op jit(solution)/shard_map/ppermute | solution.py:265
  26.6 2.0 %collective-permute-start.4 = (f32[128,256]{1,0:T(8,128)S(1)}, f32[128,256]{1,0:T(8,128)S(1)}, u32[]{:S(2)}, u32[]{:S(2)}) collective-permute-start(f32[128,256]{1,0:T(8,128)S(1)} %get-tuple-element.35), channel_id=1, source_target_pairs={{0,16},{1,17},{2,18},{3,19},{4,6},{5,7},{6,4},{7,5},{8,24},{9,25},... | collective-permute-start | bytes 393224 | tf_op jit(solution)/shard_map/ppermute | solution.py:265
  28.7 1.5 %collective-permute-start.8 = (f32[128,256]{1,0:T(8,128)S(1)}, f32[128,256]{1,0:T(8,128)S(1)}, u32[]{:S(2)}, u32[]{:S(2)}) collective-permute-start(f32[128,256]{1,0:T(8,128)S(1)} %get-tuple-element.42), channel_id=1, source_target_pairs={{0,16},{1,17},{2,18},{3,19},{4,6},{5,7},{6,4},{7,5},{8,24},{9,25},... | collective-permute-start | bytes 393224 | tf_op jit(solution)/shard_map/ppermute | solution.py:265
  30.2 1.5 %collective-permute-done.4.refs_1_ = f32[128,256]{1,0:T(8,128)S(1)} collective-permute-done((f32[128,256]{1,0:T(8,128)S(1)}, f32[128,256]{1,0:T(8,128)S(1)}, u32[]{:S(2)}, u32[]{:S(2)}) %collective-permute-start.4) | collective-permute-done | bytes 131104 | tf_op jit(solution)/shard_map/ppermute | solution.py:265
  31.7 3.1 %collective-permute-start.5 = (f32[64,256]{1,0:T(8,128)S(1)}, f32[64,256]{1,0:T(8,128)S(1)}, u32[]{:S(2)}, u32[]{:S(2)}) collective-permute-start(f32[64,256]{1,0:T(8,128)S(1)} %get-tuple-element.37), channel_id=1, source_target_pairs={{0,2},{1,3},{2,0},{3,1},{4,20},{5,21},{6,22},{7,23},{8,10},{9,11},... | collective-permute-start | bytes 196616 | tf_op jit(solution)/shard_map/ppermute | solution.py:265
  34.8 1.6 %collective-permute-start.9 = (f32[64,256]{1,0:T(8,128)S(1)}, f32[64,256]{1,0:T(8,128)S(1)}, u32[]{:S(2)}, u32[]{:S(2)}) collective-permute-start(f32[64,256]{1,0:T(8,128)S(1)} %get-tuple-element.44), channel_id=1, source_target_pairs={{0,2},{1,3},{2,0},{3,1},{4,20},{5,21},{6,22},{7,23},{8,10},{9,11},... | collective-permute-start | bytes 196616 | tf_op jit(solution)/shard_map/ppermute | solution.py:265
  36.4 1.0 %collective-permute-done.5.refs_1_ = f32[64,256]{1,0:T(8,128)S(1)} collective-permute-done((f32[64,256]{1,0:T(8,128)S(1)}, f32[64,256]{1,0:T(8,128)S(1)}, u32[]{:S(2)}, u32[]{:S(2)}) %collective-permute-start.5) | collective-permute-done | bytes 65568 | tf_op jit(solution)/shard_map/ppermute | solution.py:265
  37.4 2.6 %collective-permute-done.9.refs_1_ = f32[64,256]{1,0:T(8,128)S(1)} collective-permute-done((f32[64,256]{1,0:T(8,128)S(1)}, f32[64,256]{1,0:T(8,128)S(1)}, u32[]{:S(2)}, u32[]{:S(2)}) %collective-permute-start.9) | collective-permute-done | bytes 65568 | tf_op jit(solution)/shard_map/ppermute | solution.py:265
  40.1 3.2 %collective-permute-start.10 = (f32[64,256]{1,0:T(8,128)S(1)}, f32[64,256]{1,0:T(8,128)S(1)}, u32[]{:S(2)}, u32[]{:S(2)}) collective-permute-start(f32[64,256]{1,0:T(8,128)S(1)} %intensity.1.refs_0_), channel_id=1, source_target_pairs={{0,3},{1,2},{2,1},{3,0},{4,28},{5,29},{6,30},{7,31},{8,11},{9,10},... | collective-permute-start | bytes 196616 | tf_op jit(solution)/shard_map/ppermute | solution.py:265
  43.3 2.3 %collective-permute-start.13 = (f32[64,256]{1,0:T(8,128)S(1)}, f32[64,256]{1,0:T(8,128)S(1)}, u32[]{:S(2)}, u32[]{:S(2)}) collective-permute-start(f32[64,256]{1,0:T(8,128)S(1)} %intensity.1.refs_0_), channel_id=1, source_target_pairs={{0,24},{1,25},{2,26},{3,27},{4,7},{5,6},{6,5},{7,4},{8,16},{9,17},... | collective-permute-start | bytes 196616 | tf_op jit(solution)/shard_map/ppermute | solution.py:265
  45.6 0.7 %collective-permute-done.10.refs_1_ = f32[64,256]{1,0:T(8,128)S(1)} collective-permute-done((f32[64,256]{1,0:T(8,128)S(1)}, f32[64,256]{1,0:T(8,128)S(1)}, u32[]{:S(2)}, u32[]{:S(2)}) %collective-permute-start.10) | collective-permute-done | bytes 65568 | tf_op jit(solution)/shard_map/ppermute | solution.py:265
  46.3 2.6 %collective-permute-start.14 = (f32[64,256]{1,0:T(8,128)S(1)}, f32[64,256]{1,0:T(8,128)S(1)}, u32[]{:S(2)}, u32[]{:S(2)}) collective-permute-start(f32[64,256]{1,0:T(8,128)S(1)} %collective-permute-done.10.refs_1_), channel_id=1, source_target_pairs={{0,24},{1,25},{2,26},{3,27},{4,7},{5,6},{6,5},{7,4},{8,16},{9,17},... | collective-permute-start | bytes 196616 | tf_op jit(solution)/shard_map/ppermute | solution.py:265
  48.9 0.5 collective-permute-start.12
  49.5 2.0 %collective-permute-done.14.refs_5_ = f32[64,256]{1,0:T(8,128)S(1)} collective-permute-done((f32[64,256]{1,0:T(8,128)S(1)}, f32[64,256]{1,0:T(8,128)S(1)}, u32[]{:S(2)}, u32[]{:S(2)}) %collective-permute-start.14) | collective-permute-done | bytes 65568 | tf_op jit(solution)/shard_map/ppermute | solution.py:265
  51.5 1.2 %collective-permute-done.16.refs_7_ = f32[64,256]{1,0:T(8,128)S(1)} collective-permute-done((f32[64,256]{1,0:T(8,128)S(1)}, f32[64,256]{1,0:T(8,128)S(1)}, u32[]{:S(2)}, u32[]{:S(2)}) %collective-permute-start.16) | collective-permute-done | bytes 65568 | tf_op jit(solution)/shard_map/ppermute | solution.py:265
  52.7 1.0 %unfold.1 = f32[512,256]{1,0:T(8,128)} custom-call(f32[64,256]{1,0:T(8,128)S(1)} %intensity.1.refs_0_, f32[64,256]{1,0:T(8,128)S(1)} %collective-permute-done.10.refs_1_, f32[64,256]{1,0:T(8,128)S(1)} %collective-permute-done.11.refs_2_, f32[64,256]{1,0:T(8,128)S(1)} %collective-permute-done.12.refs_3_, f32[64,256]{1,0:T(8,128)S(1)} %collective-permute-done.13.refs_4_, ...), custom_call_target="tpu_custom_call" | custom-call | flops 1 | bytes 1 | tf_op jit(solution)/shard_map/unfold/pallas_call | solution.py:252
  (29 shorter events, 1.7 us)
Async XLA Ops:
  10.2 6.2 %collective-permute-start = (f32[136,256]{1,0:T(8,128)}, f32[136,256]{1,0:T(8,128)S(1)}, u32[]{:S(2)}, u32[]{:S(2)}) collective-permute-start(f32[136,256]{1,0:T(8,128)} %get-tuple-element.25.first), channel_id=1, source_target_pairs={{0,8},{1,9},{2,10},{3,11},{4,5},{5,4},{6,7},{7,6},{8,0},{9,1},{10,... | collective-permute-start | bytes 417800 | tf_op jit(solution)/shard_map/ppermute | solution.py:265
  13.2 5.4 %collective-permute-start.2 = (f32[136,256]{1,0:T(8,128)}, f32[136,256]{1,0:T(8,128)S(1)}, u32[]{:S(2)}, u32[]{:S(2)}) collective-permute-start(f32[136,256]{1,0:T(8,128)} %get-tuple-element.26.second), channel_id=1, source_target_pairs={{0,8},{1,9},{2,10},{3,11},{4,5},{5,4},{6,7},{7,6},{8,0},{9,1},{10,... | collective-permute-start | bytes 417800 | tf_op jit(solution)/shard_map/ppermute | solution.py:265
  13.3 0.9 %copy-start = (f32[136,256]{1,0:T(8,128)S(1)}, f32[136,256]{1,0:T(8,128)}, u32[]{:S(2)}) copy-start(f32[136,256]{1,0:T(8,128)} %get-tuple-element.26.second) | copy-start | bytes 417796
  14.2 0.9 %copy-start.1 = (f32[136,256]{1,0:T(8,128)S(1)}, f32[136,256]{1,0:T(8,128)}, u32[]{:S(2)}) copy-start(f32[136,256]{1,0:T(8,128)} %get-tuple-element.25.first) | copy-start | bytes 417796
  16.5 6.7 %collective-permute-start.1 = (f32[272,256]{1,0:T(8,128)S(1)}, f32[272,256]{1,0:T(8,128)S(1)}, u32[]{:S(2)}, u32[]{:S(2)}) collective-permute-start(f32[272,256]{1,0:T(8,128)S(1)} %join.2.payload.rest_0_), channel_id=1, source_target_pairs={{0,1},{1,0},{2,3},{3,2},{4,12},{5,13},{6,14},{7,15},{8,9},{9,8},{1... | collective-permute-start | bytes 835592 | tf_op jit(solution)/shard_map/ppermute | solution.py:265
  18.7 7.5 %collective-permute-start.6 = (f32[272,256]{1,0:T(8,128)S(1)}, f32[272,256]{1,0:T(8,128)S(1)}, u32[]{:S(2)}, u32[]{:S(2)}) collective-permute-start(f32[272,256]{1,0:T(8,128)S(1)} %join.3.payload), channel_id=1, source_target_pairs={{0,1},{1,0},{2,3},{3,2},{4,12},{5,13},{6,14},{7,15},{8,9},{9,8},{1... | collective-permute-start | bytes 835592 | tf_op jit(solution)/shard_map/ppermute | solution.py:265
  23.5 3.1 %collective-permute-start.3 = (f32[256,256]{1,0:T(8,128)S(1)}, f32[256,256]{1,0:T(8,128)S(1)}, u32[]{:S(2)}, u32[]{:S(2)}) collective-permute-start(f32[256,256]{1,0:T(8,128)S(1)} %get-tuple-element.33), channel_id=1, source_target_pairs={{0,4},{1,5},{2,6},{3,7},{4,0},{5,1},{6,2},{7,3},{8,12},{9,13},{10,... | collective-permute-start | bytes 786440 | tf_op jit(solution)/shard_map/ppermute | solution.py:265
  26.5 2.2 %collective-permute-start.7 = (f32[256,256]{1,0:T(8,128)S(1)}, f32[256,256]{1,0:T(8,128)S(1)}, u32[]{:S(2)}, u32[]{:S(2)}) collective-permute-start(f32[256,256]{1,0:T(8,128)S(1)} %get-tuple-element.40), channel_id=1, source_target_pairs={{0,4},{1,5},{2,6},{3,7},{4,0},{5,1},{6,2},{7,3},{8,12},{9,13},{10,... | collective-permute-start | bytes 786440 | tf_op jit(solution)/shard_map/ppermute | solution.py:265
  26.6 5.0 %collective-permute-start.4 = (f32[128,256]{1,0:T(8,128)S(1)}, f32[128,256]{1,0:T(8,128)S(1)}, u32[]{:S(2)}, u32[]{:S(2)}) collective-permute-start(f32[128,256]{1,0:T(8,128)S(1)} %get-tuple-element.35), channel_id=1, source_target_pairs={{0,16},{1,17},{2,18},{3,19},{4,6},{5,7},{6,4},{7,5},{8,24},{9,25},... | collective-permute-start | bytes 393224 | tf_op jit(solution)/shard_map/ppermute | solution.py:265
  28.7 6.1 %collective-permute-start.8 = (f32[128,256]{1,0:T(8,128)S(1)}, f32[128,256]{1,0:T(8,128)S(1)}, u32[]{:S(2)}, u32[]{:S(2)}) collective-permute-start(f32[128,256]{1,0:T(8,128)S(1)} %get-tuple-element.42), channel_id=1, source_target_pairs={{0,16},{1,17},{2,18},{3,19},{4,6},{5,7},{6,4},{7,5},{8,24},{9,25},... | collective-permute-start | bytes 393224 | tf_op jit(solution)/shard_map/ppermute | solution.py:265
  31.7 5.7 %collective-permute-start.5 = (f32[64,256]{1,0:T(8,128)S(1)}, f32[64,256]{1,0:T(8,128)S(1)}, u32[]{:S(2)}, u32[]{:S(2)}) collective-permute-start(f32[64,256]{1,0:T(8,128)S(1)} %get-tuple-element.37), channel_id=1, source_target_pairs={{0,2},{1,3},{2,0},{3,1},{4,20},{5,21},{6,22},{7,23},{8,10},{9,11},... | collective-permute-start | bytes 196616 | tf_op jit(solution)/shard_map/ppermute | solution.py:265
  34.8 5.2 %collective-permute-start.9 = (f32[64,256]{1,0:T(8,128)S(1)}, f32[64,256]{1,0:T(8,128)S(1)}, u32[]{:S(2)}, u32[]{:S(2)}) collective-permute-start(f32[64,256]{1,0:T(8,128)S(1)} %get-tuple-element.44), channel_id=1, source_target_pairs={{0,2},{1,3},{2,0},{3,1},{4,20},{5,21},{6,22},{7,23},{8,10},{9,11},... | collective-permute-start | bytes 196616 | tf_op jit(solution)/shard_map/ppermute | solution.py:265
  40.1 6.2 %collective-permute-start.10 = (f32[64,256]{1,0:T(8,128)S(1)}, f32[64,256]{1,0:T(8,128)S(1)}, u32[]{:S(2)}, u32[]{:S(2)}) collective-permute-start(f32[64,256]{1,0:T(8,128)S(1)} %intensity.1.refs_0_), channel_id=1, source_target_pairs={{0,3},{1,2},{2,1},{3,0},{4,28},{5,29},{6,30},{7,31},{8,11},{9,10},... | collective-permute-start | bytes 196616 | tf_op jit(solution)/shard_map/ppermute | solution.py:265
  43.3 6.2 %collective-permute-start.13 = (f32[64,256]{1,0:T(8,128)S(1)}, f32[64,256]{1,0:T(8,128)S(1)}, u32[]{:S(2)}, u32[]{:S(2)}) collective-permute-start(f32[64,256]{1,0:T(8,128)S(1)} %intensity.1.refs_0_), channel_id=1, source_target_pairs={{0,24},{1,25},{2,26},{3,27},{4,7},{5,6},{6,5},{7,4},{8,16},{9,17},... | collective-permute-start | bytes 196616 | tf_op jit(solution)/shard_map/ppermute | solution.py:265
  46.3 5.2 %collective-permute-start.14 = (f32[64,256]{1,0:T(8,128)S(1)}, f32[64,256]{1,0:T(8,128)S(1)}, u32[]{:S(2)}, u32[]{:S(2)}) collective-permute-start(f32[64,256]{1,0:T(8,128)S(1)} %collective-permute-done.10.refs_1_), channel_id=1, source_target_pairs={{0,24},{1,25},{2,26},{3,27},{4,7},{5,6},{6,5},{7,4},{8,16},{9,17},... | collective-permute-start | bytes 196616 | tf_op jit(solution)/shard_map/ppermute | solution.py:265
  48.9 2.5 %collective-permute-start.11 = (f32[64,256]{1,0:T(8,128)S(1)}, f32[64,256]{1,0:T(8,128)S(1)}, u32[]{:S(2)}, u32[]{:S(2)}) collective-permute-start(f32[64,256]{1,0:T(8,128)S(1)} %intensity.1.refs_0_), channel_id=1, source_target_pairs={{0,4},{1,5},{2,6},{3,7},{4,0},{5,1},{6,2},{7,3},{8,12},{9,13},{10,... | collective-permute-start | bytes 196616 | tf_op jit(solution)/shard_map/ppermute | solution.py:265
  48.9 2.5 %collective-permute-start.12 = (f32[64,256]{1,0:T(8,128)S(1)}, f32[64,256]{1,0:T(8,128)S(1)}, u32[]{:S(2)}, u32[]{:S(2)}) collective-permute-start(f32[64,256]{1,0:T(8,128)S(1)} %collective-permute-done.10.refs_1_), channel_id=1, source_target_pairs={{0,4},{1,5},{2,6},{3,7},{4,0},{5,1},{6,2},{7,3},{8,12},{9,13},{10,... | collective-permute-start | bytes 196616 | tf_op jit(solution)/shard_map/ppermute | solution.py:265
  49.5 2.0 %collective-permute-start.15 = (f32[64,256]{1,0:T(8,128)S(1)}, f32[64,256]{1,0:T(8,128)S(1)}, u32[]{:S(2)}, u32[]{:S(2)}) collective-permute-start(f32[64,256]{1,0:T(8,128)S(1)} %collective-permute-done.13.refs_4_), channel_id=1, source_target_pairs={{0,4},{1,5},{2,6},{3,7},{4,0},{5,1},{6,2},{7,3},{8,12},{9,13},{10,... | collective-permute-start | bytes 196616 | tf_op jit(solution)/shard_map/ppermute | solution.py:265
  51.5 1.3 %collective-permute-start.16 = (f32[64,256]{1,0:T(8,128)S(1)}, f32[64,256]{1,0:T(8,128)S(1)}, u32[]{:S(2)}, u32[]{:S(2)}) collective-permute-start(f32[64,256]{1,0:T(8,128)S(1)} %collective-permute-done.14.refs_5_), channel_id=1, source_target_pairs={{0,4},{1,5},{2,6},{3,7},{4,0},{5,1},{6,2},{7,3},{8,12},{9,13},{10,... | collective-permute-start | bytes 196616 | tf_op jit(solution)/shard_map/ppermute | solution.py:265
where the time goes:
time: 53.9 us; the launch traced here: 53.7 us
  starting transfers between devices  23.7 us (44%)
  waiting for transfers between devices  15.3 us (28%)
  Pallas kernels  12.7 us (24%)
  local copies, waits for them, and re-layouts  1.85 us (3%)
    ppermute x17, starting transfers between devices, swap(): return lax.ppermute(array, AXES, pairs)  23.7 us
    ppermute x17, waiting for transfers between devices, swap(): return lax.ppermute(array, AXES, pairs)  15.3 us
    pallas_call x1, Pallas kernels, accumulate(): pl.pallas_call(functools.partial(accumulate_kernel, plan), in_specs=[pl.B...  10.2 us
    pallas_call x14, Pallas kernels, small_call(): pl.pallas_call(kernel, out_shape=[jax.ShapeDtypeStruct(shape, jnp.float32...  2.47 us
    unnamed x4, local copies, waits for them, and re-layouts  1.85 us
  transfers between devices with their start and end apart: 17, of which 9 were waited for; matrix products, arithmetic and copies ran while one was open for 0% of the time, Pallas kernels for 3%

commit v1 on v0

--- a/solution.py
+++ b/solution.py
@@ -17,7 +17,7 @@
 FLIP_BOX = (0b110000, 0b001100, 0b000011)
 AXES = ("bx", "by", "bz")
 POSITIONS = 8
-TILE_LIMIT = 56 * 1024 * 1024
+TILE_LIMIT = 53 * 1024 * 1024
 VMEM_LIMIT = 24 * 1024 * 1024
 LARGE = 10**10
 SWAPPED = (0, 4, 2, 6, 1, 5, 3, 7)
@@ -80,8 +80,8 @@
     return holder * plan.share + row
 
 
-def accumulate_kernel(plan, angles, lorentz, owner, box, counts, rows, cols, seen, value_out, weight_out, *scratch):
-    arrays, sems, turned, partial = scratch[:4], scratch[4], scratch[5], scratch[6]
+def accumulate_kernel(counts, rows, cols, seen, value_out, weight_out, *scratch):
+    arrays, sems, partial = scratch[:4], scratch[4], scratch[5]
     frames, positions = counts.shape[0], counts.shape[1]
     blocks = positions // POSITIONS
 
@@ -95,19 +95,12 @@
         for copy in copies(block):
             copy.start()
 
-    tiles = frames * positions
-    across = lax.broadcasted_iota(jnp.int32, (tiles, tiles), 1)
-    down = lax.broadcasted_iota(jnp.int32, (tiles, tiles), 0)
-    flips = masked(plan.upper(owner[...]), FLIP_VOX)
-    turned[...] = jnp.sum(jnp.where(across == down, flips, 0), axis=1, keepdims=True)
-    ids = destination(plan, owner[...], box[...])
-    for out in (value_out, weight_out):
-        out[tiles : tiles + 8, :] = jnp.zeros((8, VOX), jnp.float32)
-        out[tiles : tiles + 8, :tiles] = jnp.broadcast_to(ids.astype(jnp.float32), (8, tiles))
-
     held_counts, held_rows, held_cols, held_seen = arrays
 
-    def compute(block):
+    @pl.loop(0, blocks)
+    def _(block):
+        for copy in copies(block):
+            copy.wait()
         for p in range(POSITIONS):
             at = block * POSITIONS + p
             for f in range(frames):
@@ -123,46 +116,27 @@
                         total = item if total is None else total + item
                     partial[f, kind, 0, p * 8 : (p + 1) * 8, :] = total[:, :LANES]
                     partial[f, kind, 1, p * 8 : (p + 1) * 8, :] = total[:, LANES:]
-
-    def finish(block):
-        lanes = lax.broadcasted_iota(jnp.int32, (POSITIONS, LANES), 1)
         for f in range(frames):
             place = pl.ds(pl.multiple_of(f * positions + block * POSITIONS, POSITIONS), POSITIONS)
-            mask = jnp.broadcast_to(turned[place, :], (POSITIONS, LANES))
-            index = lanes ^ (mask & (LANES - 1))
-            swap = (mask & LANES) != 0
             for kind, out in enumerate((value_out, weight_out)):
-                low, high = (
-                    sum(partial[f, kind, half, pl.ds(row, POSITIONS, stride=8), :] for row in range(8))
-                    for half in range(2)
-                )
-                scale = lorentz[angles[f]] if kind == 0 else 1.0
-                out[place, :LANES] = lane_gather(jnp.where(swap, high, low), index) * scale
-                out[place, LANES:] = lane_gather(jnp.where(swap, low, high), index) * scale
-
-    @pl.loop(0, blocks)
-    def _(block):
-        for copy in copies(block):
-            copy.wait()
-        compute(block)
-        finish(block)
-
-
-def accumulate(plan, counts, row_split, col_split, efficiency, lorentz, angles, owner, box):
+                for half in range(2):
+                    lanes = pl.ds(half * LANES, LANES)
+                    parts = [partial[f, kind, half, pl.ds(row, POSITIONS, stride=8), :] for row in range(8)]
+                    out[place, lanes] = sum(parts)
+
+
+def accumulate(counts, row_split, col_split, efficiency):
     frames, positions, pixels, _ = counts.shape
     tiles = frames * positions
     arrays = (counts, row_split, col_split, efficiency)
     return pl.pallas_call(
-        functools.partial(accumulate_kernel, plan),
-        in_specs=[pl.BlockSpec(memory_space=pltpu.SMEM)] * 2
-        + [pl.BlockSpec(memory_space=pltpu.VMEM)] * 2
-        + [pl.BlockSpec(memory_space=pl.ANY)] * 4,
+        accumulate_kernel,
+        in_specs=[pl.BlockSpec(memory_space=pl.ANY)] * 4,
         out_specs=[pl.BlockSpec(memory_space=pltpu.VMEM)] * 2,
-        out_shape=[jax.ShapeDtypeStruct((tiles + 8, VOX), jnp.float32)] * 2,
+        out_shape=[jax.ShapeDtypeStruct((tiles, VOX), jnp.float32)] * 2,
         scratch_shapes=[pltpu.VMEM(array.shape, array.dtype) for array in arrays]
         + [
             pltpu.SemaphoreType.DMA((positions // POSITIONS, 4)),
-            pltpu.VMEM((tiles, 1), jnp.int32),
             pltpu.VMEM((frames, 2, 2, 8 * POSITIONS, LANES), jnp.float32),
         ],
         compiler_params=pltpu.CompilerParams(vmem_limit_bytes=TILE_LIMIT),
@@ -172,7 +146,43 @@
             transcendentals=0,
         ),
         name="tile_sums",
-    )(angles, lorentz, owner, box, *arrays)
+    )(*arrays)
+
+
+def payload_kernel(plan, angles, lorentz, owner, box, value, weight, value_out, weight_out):
+    tiles = value.shape[0]
+    frames = angles.shape[0]
+    across = lax.broadcasted_iota(jnp.int32, (tiles, tiles), 1)
+    down = lax.broadcasted_iota(jnp.int32, (tiles, tiles), 0)
+    flips = masked(plan.upper(owner[...]), FLIP_VOX)
+    flips = jnp.sum(jnp.where(across == down, flips, 0), axis=1, keepdims=True)
+    ids = destination(plan, owner[...], box[...])
+    for out in (value_out, weight_out):
+        out[tiles : tiles + 8, :] = jnp.zeros((8, VOX), jnp.float32)
+        out[tiles : tiles + 8, :tiles] = jnp.broadcast_to(ids.astype(jnp.float32), (8, tiles))
+    lanes = lax.broadcasted_iota(jnp.int32, (8, LANES), 1)
+    for start in range(0, tiles, 8):
+        span = slice(start, start + 8)
+        mask = jnp.broadcast_to(flips[span, :], (8, LANES))
+        index = lanes ^ (mask & (LANES - 1))
+        swap = (mask & LANES) != 0
+        factor = lorentz[angles[start // (tiles // frames)]]
+        for ref, out, scale in ((value, value_out, factor), (weight, weight_out, 1.0)):
+            low, high = ref[span, :LANES], ref[span, LANES:]
+            out[span, :LANES] = lane_gather(jnp.where(swap, high, low), index) * scale
+            out[span, LANES:] = lane_gather(jnp.where(swap, low, high), index) * scale
+
+
+def labelled(plan, angles, lorentz, owner, box, value, weight):
+    shape = (value.shape[0] + 8, VOX)
+    return pl.pallas_call(
+        functools.partial(payload_kernel, plan),
+        in_specs=[pl.BlockSpec(memory_space=pltpu.SMEM)] * 2 + [pl.BlockSpec(memory_space=pltpu.VMEM)] * 4,
+        out_shape=[jax.ShapeDtypeStruct(shape, jnp.float32)] * 2,
+        compiler_params=pltpu.CompilerParams(vmem_limit_bytes=VMEM_LIMIT),
+        cost_estimate=pl.CostEstimate(flops=1, bytes_accessed=1, transcendentals=0),
+        name="payload",
+    )(angles, lorentz, owner, box, value, weight)
 
 
 def scatter_kernel(plan, olds, outs, payload, *refs):
@@ -190,11 +200,6 @@
         total = jnp.dot(pick, high, preferred_element_type=jnp.float32)
         total = total + jnp.dot(pick, low, preferred_element_type=jnp.float32)
         out[...] = total + before[number][...] if olds else total
-
-
-def stage_kernel(first, second, first_out, second_out):
-    first_out[...] = first[...]
-    second_out[...] = second[...]
 
 
 def join_kernel(first, second, *rest):
@@ -271,11 +276,11 @@
     gather_steps, reduce_steps = plan.steps()
     owner = tile_owner.reshape(1, -1)
     box = tile_box.reshape(1, -1)
-    own = accumulate(plan, counts, row_split, col_split, efficiency, lorentz, angles, owner, box)
+    own = accumulate(counts, row_split, col_split, efficiency)
+    own = labelled(plan, angles, lorentz, owner, box, *own)
     arrived = [swap(array, *gather_steps) for array in own]
-    held = small_call(stage_kernel, [array.shape for array in own], "stage", *own, flops=LARGE)
-    near = [join(held[0], arrived[0])]
-    near.append(join(held[1], arrived[1], near[0]))
+    near = [join(own[0], arrived[0])]
+    near.append(join(own[1], arrived[1], near[0]))
     far = [swap(array, *gather_steps[::-1]) for array in near]
     def box_sums(payload, olds, *waits, flops=1):
         kernel = functools.partial(scatter_kernel, plan, len(olds), plan.sy)

time: 53.9 us -> 53.1 us (0.985)
  local copies, waits for them, and re-layouts: 1.85 us -> 0.01 us
  waiting for transfers between devices: 15.3 us -> 17 us
  Pallas kernels: 12.7 us -> 12.1 us
    unnamed x4 -> x8, local copies, waits for them, and re-layouts: 1.85 us -> 0.01 us
    ppermute x17, waiting for transfers between devices: 15.3 us -> 17 us  [swap(): return lax.ppermute(array, AXES, pairs)]
    pallas_call x1 -> x2, Pallas kernels: 10.2 us -> 9.64 us  [the longest x1 8.57 us: accumulate(): pl.pallas_call(accumulate_kernel, in_specs=[pl.BlockSpec(memory_space=pl....]
    pallas_call x14 -> x13, Pallas kernels: 2.47 us -> 2.45 us  [small_call(): pl.pallas_call(kernel, out_shape=[jax.ShapeDtypeStruct(shape, jnp.float32...]
where the time goes in v1:
time: 53.1 us; the launch traced here: 53 us
  starting transfers between devices  23.7 us (45%)
  waiting for transfers between devices  17 us (32%)
  Pallas kernels  12.1 us (23%)
    ppermute x17, starting transfers between devices, swap(): return lax.ppermute(array, AXES, pairs)  23.7 us
    ppermute x17, waiting for transfers between devices, swap(): return lax.ppermute(array, AXES, pairs)  17 us
    pallas_call x1, Pallas kernels, accumulate(): pl.pallas_call(accumulate_kernel, in_specs=[pl.BlockSpec(memory_space=pl....  8.57 us
    pallas_call x13, Pallas kernels, small_call(): pl.pallas_call(kernel, out_shape=[jax.ShapeDtypeStruct(shape, jnp.float32...  2.45 us
    pallas_call x1, Pallas kernels, labelled(): pl.pallas_call(functools.partial(payload_kernel, plan), in_specs=[pl.Bloc...  1.06 us
  transfers between devices with their start and end apart: 17, of which 9 were waited for; matrix products, arithmetic and copies ran while one was open for 0% of the time, Pallas kernels for 3%

profile of v1, /device:TPU:0, one launch (start us, length us, event | category | flops | bytes accessed | tf_op | source)
XLA Modules:
  0.0 53.0 jit_solution(5242481547781943376)
XLA Ops:
  0.0 8.6 %tile_sums.1 = (f32[128,256]{1,0:T(8,128)S(1)}, f32[128,256]{1,0:T(8,128)S(1)}) custom-call(bf16[2,64,128,128]{3,2,1,0:T(8,128)(2,1)} %counts.1, bf16[2,64,128,256]{3,2,1,0:T(8,128)(2,1)} %rows.1, bf16[2,64,128,256]{3,2,1,0:T(8,128)(2,1)} %cols.1, bf16[64,128,128]{2,1,0:T(8,128)(2,1)} %seen.1), custom_call_target="tpu_custom_call" | custom-call | flops 2147483648 | bytes 23068672 | tf_op jit(solution)/shard_map/tile_sums/pallas_call | solution.py:132
  8.6 1.1 %payload.1 = (f32[136,256]{1,0:T(8,128)S(1)}, f32[136,256]{1,0:T(8,128)S(1)}) custom-call(s32[2]{0:T(128)S(1)} %copy-done.1, f32[3600]{0:T(1024)S(1)} %copy-done, s32[1,128]{1,0:T(1,128)S(1)} %bitcast.5, s32[1,128]{1,0:T(1,128)S(1)} %bitcast.6, f32[128,256]{1,0:T(8,128)S(1)} %get-tuple-element.25.value, f32[128,256]{1,0:T(8,128)S(1)} %get-tuple-element.26.weight), custom_call_target="tpu_custom_call" | custom-call | flops 1 | bytes 1 | tf_op jit(solution)/shard_map/payload/pallas_call | solution.py:178
  9.7 3.0 %collective-permute-start = (f32[136,256]{1,0:T(8,128)S(1)}, f32[136,256]{1,0:T(8,128)S(1)}, u32[]{:S(2)}, u32[]{:S(2)}) collective-permute-start(f32[136,256]{1,0:T(8,128)S(1)} %get-tuple-element.27.first), channel_id=1, source_target_pairs={{0,8},{1,9},{2,10},{3,11},{4,5},{5,4},{6,7},{7,6},{8,0},{9,1},{10,... | collective-permute-start | bytes 417800 | tf_op jit(solution)/shard_map/ppermute | solution.py:270
  12.8 3.0 %collective-permute-done.second = f32[136,256]{1,0:T(8,128)S(1)} collective-permute-done((f32[136,256]{1,0:T(8,128)S(1)}, f32[136,256]{1,0:T(8,128)S(1)}, u32[]{:S(2)}, u32[]{:S(2)}) %collective-permute-start) | collective-permute-done | bytes 139296 | tf_op jit(solution)/shard_map/ppermute | solution.py:270
  15.8 2.2 %collective-permute-start.1 = (f32[272,256]{1,0:T(8,128)S(1)}, f32[272,256]{1,0:T(8,128)S(1)}, u32[]{:S(2)}, u32[]{:S(2)}) collective-permute-start(f32[272,256]{1,0:T(8,128)S(1)} %join.2.payload.rest_0_), channel_id=1, source_target_pairs={{0,1},{1,0},{2,3},{3,2},{4,12},{5,13},{6,14},{7,15},{8,9},{9,8},{1... | collective-permute-start | bytes 835592 | tf_op jit(solution)/shard_map/ppermute | solution.py:270
  18.0 1.5 %collective-permute-start.6 = (f32[272,256]{1,0:T(8,128)S(1)}, f32[272,256]{1,0:T(8,128)S(1)}, u32[]{:S(2)}, u32[]{:S(2)}) collective-permute-start(f32[272,256]{1,0:T(8,128)S(1)} %join.3.payload), channel_id=1, source_target_pairs={{0,1},{1,0},{2,3},{3,2},{4,12},{5,13},{6,14},{7,15},{8,9},{9,8},{1... | collective-permute-start | bytes 835592 | tf_op jit(solution)/shard_map/ppermute | solution.py:270
  20.1 2.4 %collective-permute-done.1.payload = f32[272,256]{1,0:T(8,128)S(1)} collective-permute-done((f32[272,256]{1,0:T(8,128)S(1)}, f32[272,256]{1,0:T(8,128)S(1)}, u32[]{:S(2)}, u32[]{:S(2)}) %collective-permute-start.1) | collective-permute-done | bytes 278560 | tf_op jit(solution)/shard_map/ppermute | solution.py:270
  22.9 2.6 %collective-permute-done.6.payload = f32[272,256]{1,0:T(8,128)S(1)} collective-permute-done((f32[272,256]{1,0:T(8,128)S(1)}, f32[272,256]{1,0:T(8,128)S(1)}, u32[]{:S(2)}, u32[]{:S(2)}) %collective-permute-start.6) | collective-permute-done | bytes 278560 | tf_op jit(solution)/shard_map/ppermute | solution.py:270
  25.4 0.3 box_sums.7
  25.9 2.0 %collective-permute-start.4 = (f32[128,256]{1,0:T(8,128)S(1)}, f32[128,256]{1,0:T(8,128)S(1)}, u32[]{:S(2)}, u32[]{:S(2)}) collective-permute-start(f32[128,256]{1,0:T(8,128)S(1)} %get-tuple-element.35), channel_id=1, source_target_pairs={{0,16},{1,17},{2,18},{3,19},{4,6},{5,7},{6,4},{7,5},{8,24},{9,25},... | collective-permute-start | bytes 393224 | tf_op jit(solution)/shard_map/ppermute | solution.py:270
  28.0 1.5 %collective-permute-start.8 = (f32[128,256]{1,0:T(8,128)S(1)}, f32[128,256]{1,0:T(8,128)S(1)}, u32[]{:S(2)}, u32[]{:S(2)}) collective-permute-start(f32[128,256]{1,0:T(8,128)S(1)} %get-tuple-element.42), channel_id=1, source_target_pairs={{0,16},{1,17},{2,18},{3,19},{4,6},{5,7},{6,4},{7,5},{8,24},{9,25},... | collective-permute-start | bytes 393224 | tf_op jit(solution)/shard_map/ppermute | solution.py:270
  29.4 1.5 %collective-permute-done.4.refs_1_ = f32[128,256]{1,0:T(8,128)S(1)} collective-permute-done((f32[128,256]{1,0:T(8,128)S(1)}, f32[128,256]{1,0:T(8,128)S(1)}, u32[]{:S(2)}, u32[]{:S(2)}) %collective-permute-start.4) | collective-permute-done | bytes 131104 | tf_op jit(solution)/shard_map/ppermute | solution.py:270
  31.0 3.1 %collective-permute-start.5 = (f32[64,256]{1,0:T(8,128)S(1)}, f32[64,256]{1,0:T(8,128)S(1)}, u32[]{:S(2)}, u32[]{:S(2)}) collective-permute-start(f32[64,256]{1,0:T(8,128)S(1)} %get-tuple-element.37), channel_id=1, source_target_pairs={{0,2},{1,3},{2,0},{3,1},{4,20},{5,21},{6,22},{7,23},{8,10},{9,11},... | collective-permute-start | bytes 196616 | tf_op jit(solution)/shard_map/ppermute | solution.py:270
  34.1 1.6 %collective-permute-start.9 = (f32[64,256]{1,0:T(8,128)S(1)}, f32[64,256]{1,0:T(8,128)S(1)}, u32[]{:S(2)}, u32[]{:S(2)}) collective-permute-start(f32[64,256]{1,0:T(8,128)S(1)} %get-tuple-element.44), channel_id=1, source_target_pairs={{0,2},{1,3},{2,0},{3,1},{4,20},{5,21},{6,22},{7,23},{8,10},{9,11},... | collective-permute-start | bytes 196616 | tf_op jit(solution)/shard_map/ppermute | solution.py:270
  35.7 1.0 %collective-permute-done.5.refs_1_ = f32[64,256]{1,0:T(8,128)S(1)} collective-permute-done((f32[64,256]{1,0:T(8,128)S(1)}, f32[64,256]{1,0:T(8,128)S(1)}, u32[]{:S(2)}, u32[]{:S(2)}) %collective-permute-start.5) | collective-permute-done | bytes 65568 | tf_op jit(solution)/shard_map/ppermute | solution.py:270
  36.7 2.6 %collective-permute-done.9.refs_1_ = f32[64,256]{1,0:T(8,128)S(1)} collective-permute-done((f32[64,256]{1,0:T(8,128)S(1)}, f32[64,256]{1,0:T(8,128)S(1)}, u32[]{:S(2)}, u32[]{:S(2)}) %collective-permute-start.9) | collective-permute-done | bytes 65568 | tf_op jit(solution)/shard_map/ppermute | solution.py:270
  39.3 3.2 %collective-permute-start.10 = (f32[64,256]{1,0:T(8,128)S(1)}, f32[64,256]{1,0:T(8,128)S(1)}, u32[]{:S(2)}, u32[]{:S(2)}) collective-permute-start(f32[64,256]{1,0:T(8,128)S(1)} %intensity.1.refs_0_), channel_id=1, source_target_pairs={{0,3},{1,2},{2,1},{3,0},{4,28},{5,29},{6,30},{7,31},{8,11},{9,10},... | collective-permute-start | bytes 196616 | tf_op jit(solution)/shard_map/ppermute | solution.py:270
  42.5 2.3 %collective-permute-start.13 = (f32[64,256]{1,0:T(8,128)S(1)}, f32[64,256]{1,0:T(8,128)S(1)}, u32[]{:S(2)}, u32[]{:S(2)}) collective-permute-start(f32[64,256]{1,0:T(8,128)S(1)} %intensity.1.refs_0_), channel_id=1, source_target_pairs={{0,24},{1,25},{2,26},{3,27},{4,7},{5,6},{6,5},{7,4},{8,16},{9,17},... | collective-permute-start | bytes 196616 | tf_op jit(solution)/shard_map/ppermute | solution.py:270
  44.9 0.7 %collective-permute-done.10.refs_1_ = f32[64,256]{1,0:T(8,128)S(1)} collective-permute-done((f32[64,256]{1,0:T(8,128)S(1)}, f32[64,256]{1,0:T(8,128)S(1)}, u32[]{:S(2)}, u32[]{:S(2)}) %collective-permute-start.10) | collective-permute-done | bytes 65568 | tf_op jit(solution)/shard_map/ppermute | solution.py:270
  45.6 2.6 %collective-permute-start.14 = (f32[64,256]{1,0:T(8,128)S(1)}, f32[64,256]{1,0:T(8,128)S(1)}, u32[]{:S(2)}, u32[]{:S(2)}) collective-permute-start(f32[64,256]{1,0:T(8,128)S(1)} %collective-permute-done.10.refs_1_), channel_id=1, source_target_pairs={{0,24},{1,25},{2,26},{3,27},{4,7},{5,6},{6,5},{7,4},{8,16},{9,17},... | collective-permute-start | bytes 196616 | tf_op jit(solution)/shard_map/ppermute | solution.py:270
  48.2 0.5 collective-permute-start.12
  48.7 2.0 %collective-permute-done.14.refs_5_ = f32[64,256]{1,0:T(8,128)S(1)} collective-permute-done((f32[64,256]{1,0:T(8,128)S(1)}, f32[64,256]{1,0:T(8,128)S(1)}, u32[]{:S(2)}, u32[]{:S(2)}) %collective-permute-start.14) | collective-permute-done | bytes 65568 | tf_op jit(solution)/shard_map/ppermute | solution.py:270
  50.8 1.2 %collective-permute-done.16.refs_7_ = f32[64,256]{1,0:T(8,128)S(1)} collective-permute-done((f32[64,256]{1,0:T(8,128)S(1)}, f32[64,256]{1,0:T(8,128)S(1)}, u32[]{:S(2)}, u32[]{:S(2)}) %collective-permute-start.16) | collective-permute-done | bytes 65568 | tf_op jit(solution)/shard_map/ppermute | solution.py:270
  52.0 1.0 %unfold.1 = f32[512,256]{1,0:T(8,128)} custom-call(f32[64,256]{1,0:T(8,128)S(1)} %intensity.1.refs_0_, f32[64,256]{1,0:T(8,128)S(1)} %collective-permute-done.10.refs_1_, f32[64,256]{1,0:T(8,128)S(1)} %collective-permute-done.11.refs_2_, f32[64,256]{1,0:T(8,128)S(1)} %collective-permute-done.12.refs_3_, f32[64,256]{1,0:T(8,128)S(1)} %collective-permute-done.13.refs_4_, ...), custom_call_target="tpu_custom_call" | custom-call | flops 1 | bytes 1 | tf_op jit(solution)/shard_map/unfold/pallas_call | solution.py:257
  (33 shorter events, 1.4 us)
Async XLA Ops:
  0.0 8.6 %copy-start.3 = (s32[128]{0:T(128)S(1)}, s32[128]{0:T(128)}, u32[]{:S(2)}) copy-start(s32[128]{0:T(128)} %param.15) | copy-start | bytes 1540
  0.0 8.6 %copy-start.2 = (s32[128,1]{0,1:T(1,128)S(1)}, s32[128,1]{0,1:T(1,128)}, u32[]{:S(2)}) copy-start(s32[128,1]{0,1:T(1,128)} %param.14) | copy-start | bytes 1540
  0.0 8.6 %copy-start.1 = (s32[2]{0:T(128)S(1)}, s32[2]{0:T(128)}, u32[]{:S(2)}) copy-start(s32[2]{0:T(128)} %angles.1) | copy-start | bytes 28
  0.0 8.6 %copy-start = (f32[3600]{0:T(1024)S(1)}, f32[3600]{0:T(1024)}, u32[]{:S(2)}) copy-start(f32[3600]{0:T(1024)} %lorentz.1) | copy-start | bytes 43204
  9.7 6.1 %collective-permute-start = (f32[136,256]{1,0:T(8,128)S(1)}, f32[136,256]{1,0:T(8,128)S(1)}, u32[]{:S(2)}, u32[]{:S(2)}) collective-permute-start(f32[136,256]{1,0:T(8,128)S(1)} %get-tuple-element.27.first), channel_id=1, source_target_pairs={{0,8},{1,9},{2,10},{3,11},{4,5},{5,4},{6,7},{7,6},{8,0},{9,1},{10,... | collective-permute-start | bytes 417800 | tf_op jit(solution)/shard_map/ppermute | solution.py:270
  12.7 5.2 %collective-permute-start.2 = (f32[136,256]{1,0:T(8,128)S(1)}, f32[136,256]{1,0:T(8,128)S(1)}, u32[]{:S(2)}, u32[]{:S(2)}) collective-permute-start(f32[136,256]{1,0:T(8,128)S(1)} %get-tuple-element.30.first), channel_id=1, source_target_pairs={{0,8},{1,9},{2,10},{3,11},{4,5},{5,4},{6,7},{7,6},{8,0},{9,1},{10,... | collective-permute-start | bytes 417800 | tf_op jit(solution)/shard_map/ppermute | solution.py:270
  15.8 6.7 %collective-permute-start.1 = (f32[272,256]{1,0:T(8,128)S(1)}, f32[272,256]{1,0:T(8,128)S(1)}, u32[]{:S(2)}, u32[]{:S(2)}) collective-permute-start(f32[272,256]{1,0:T(8,128)S(1)} %join.2.payload.rest_0_), channel_id=1, source_target_pairs={{0,1},{1,0},{2,3},{3,2},{4,12},{5,13},{6,14},{7,15},{8,9},{9,8},{1... | collective-permute-start | bytes 835592 | tf_op jit(solution)/shard_map/ppermute | solution.py:270
  18.0 7.5 %collective-permute-start.6 = (f32[272,256]{1,0:T(8,128)S(1)}, f32[272,256]{1,0:T(8,128)S(1)}, u32[]{:S(2)}, u32[]{:S(2)}) collective-permute-start(f32[272,256]{1,0:T(8,128)S(1)} %join.3.payload), channel_id=1, source_target_pairs={{0,1},{1,0},{2,3},{3,2},{4,12},{5,13},{6,14},{7,15},{8,9},{9,8},{1... | collective-permute-start | bytes 835592 | tf_op jit(solution)/shard_map/ppermute | solution.py:270
  22.8 3.1 %collective-permute-start.3 = (f32[256,256]{1,0:T(8,128)S(1)}, f32[256,256]{1,0:T(8,128)S(1)}, u32[]{:S(2)}, u32[]{:S(2)}) collective-permute-start(f32[256,256]{1,0:T(8,128)S(1)} %get-tuple-element.33), channel_id=1, source_target_pairs={{0,4},{1,5},{2,6},{3,7},{4,0},{5,1},{6,2},{7,3},{8,12},{9,13},{10,... | collective-permute-start | bytes 786440 | tf_op jit(solution)/shard_map/ppermute | solution.py:270
  25.8 2.2 %collective-permute-start.7 = (f32[256,256]{1,0:T(8,128)S(1)}, f32[256,256]{1,0:T(8,128)S(1)}, u32[]{:S(2)}, u32[]{:S(2)}) collective-permute-start(f32[256,256]{1,0:T(8,128)S(1)} %get-tuple-element.40), channel_id=1, source_target_pairs={{0,4},{1,5},{2,6},{3,7},{4,0},{5,1},{6,2},{7,3},{8,12},{9,13},{10,... | collective-permute-start | bytes 786440 | tf_op jit(solution)/shard_map/ppermute | solution.py:270
  25.9 5.0 %collective-permute-start.4 = (f32[128,256]{1,0:T(8,128)S(1)}, f32[128,256]{1,0:T(8,128)S(1)}, u32[]{:S(2)}, u32[]{:S(2)}) collective-permute-start(f32[128,256]{1,0:T(8,128)S(1)} %get-tuple-element.35), channel_id=1, source_target_pairs={{0,16},{1,17},{2,18},{3,19},{4,6},{5,7},{6,4},{7,5},{8,24},{9,25},... | collective-permute-start | bytes 393224 | tf_op jit(solution)/shard_map/ppermute | solution.py:270
  28.0 6.1 %collective-permute-start.8 = (f32[128,256]{1,0:T(8,128)S(1)}, f32[128,256]{1,0:T(8,128)S(1)}, u32[]{:S(2)}, u32[]{:S(2)}) collective-permute-start(f32[128,256]{1,0:T(8,128)S(1)} %get-tuple-element.42), channel_id=1, source_target_pairs={{0,16},{1,17},{2,18},{3,19},{4,6},{5,7},{6,4},{7,5},{8,24},{9,25},... | collective-permute-start | bytes 393224 | tf_op jit(solution)/shard_map/ppermute | solution.py:270
  31.0 5.7 %collective-permute-start.5 = (f32[64,256]{1,0:T(8,128)S(1)}, f32[64,256]{1,0:T(8,128)S(1)}, u32[]{:S(2)}, u32[]{:S(2)}) collective-permute-start(f32[64,256]{1,0:T(8,128)S(1)} %get-tuple-element.37), channel_id=1, source_target_pairs={{0,2},{1,3},{2,0},{3,1},{4,20},{5,21},{6,22},{7,23},{8,10},{9,11},... | collective-permute-start | bytes 196616 | tf_op jit(solution)/shard_map/ppermute | solution.py:270
  34.1 5.2 %collective-permute-start.9 = (f32[64,256]{1,0:T(8,128)S(1)}, f32[64,256]{1,0:T(8,128)S(1)}, u32[]{:S(2)}, u32[]{:S(2)}) collective-permute-start(f32[64,256]{1,0:T(8,128)S(1)} %get-tuple-element.44), channel_id=1, source_target_pairs={{0,2},{1,3},{2,0},{3,1},{4,20},{5,21},{6,22},{7,23},{8,10},{9,11},... | collective-permute-start | bytes 196616 | tf_op jit(solution)/shard_map/ppermute | solution.py:270
  39.3 6.2 %collective-permute-start.10 = (f32[64,256]{1,0:T(8,128)S(1)}, f32[64,256]{1,0:T(8,128)S(1)}, u32[]{:S(2)}, u32[]{:S(2)}) collective-permute-start(f32[64,256]{1,0:T(8,128)S(1)} %intensity.1.refs_0_), channel_id=1, source_target_pairs={{0,3},{1,2},{2,1},{3,0},{4,28},{5,29},{6,30},{7,31},{8,11},{9,10},... | collective-permute-start | bytes 196616 | tf_op jit(solution)/shard_map/ppermute | solution.py:270
  42.5 6.2 %collective-permute-start.13 = (f32[64,256]{1,0:T(8,128)S(1)}, f32[64,256]{1,0:T(8,128)S(1)}, u32[]{:S(2)}, u32[]{:S(2)}) collective-permute-start(f32[64,256]{1,0:T(8,128)S(1)} %intensity.1.refs_0_), channel_id=1, source_target_pairs={{0,24},{1,25},{2,26},{3,27},{4,7},{5,6},{6,5},{7,4},{8,16},{9,17},... | collective-permute-start | bytes 196616 | tf_op jit(solution)/shard_map/ppermute | solution.py:270
  45.6 5.2 %collective-permute-start.14 = (f32[64,256]{1,0:T(8,128)S(1)}, f32[64,256]{1,0:T(8,128)S(1)}, u32[]{:S(2)}, u32[]{:S(2)}) collective-permute-start(f32[64,256]{1,0:T(8,128)S(1)} %collective-permute-done.10.refs_1_), channel_id=1, source_target_pairs={{0,24},{1,25},{2,26},{3,27},{4,7},{5,6},{6,5},{7,4},{8,16},{9,17},... | collective-permute-start | bytes 196616 | tf_op jit(solution)/shard_map/ppermute | solution.py:270
  48.2 2.5 %collective-permute-start.11 = (f32[64,256]{1,0:T(8,128)S(1)}, f32[64,256]{1,0:T(8,128)S(1)}, u32[]{:S(2)}, u32[]{:S(2)}) collective-permute-start(f32[64,256]{1,0:T(8,128)S(1)} %intensity.1.refs_0_), channel_id=1, source_target_pairs={{0,4},{1,5},{2,6},{3,7},{4,0},{5,1},{6,2},{7,3},{8,12},{9,13},{10,... | collective-permute-start | bytes 196616 | tf_op jit(solution)/shard_map/ppermute | solution.py:270
  48.2 2.5 %collective-permute-start.12 = (f32[64,256]{1,0:T(8,128)S(1)}, f32[64,256]{1,0:T(8,128)S(1)}, u32[]{:S(2)}, u32[]{:S(2)}) collective-permute-start(f32[64,256]{1,0:T(8,128)S(1)} %collective-permute-done.10.refs_1_), channel_id=1, source_target_pairs={{0,4},{1,5},{2,6},{3,7},{4,0},{5,1},{6,2},{7,3},{8,12},{9,13},{10,... | collective-permute-start | bytes 196616 | tf_op jit(solution)/shard_map/ppermute | solution.py:270
  48.7 2.0 %collective-permute-start.15 = (f32[64,256]{1,0:T(8,128)S(1)}, f32[64,256]{1,0:T(8,128)S(1)}, u32[]{:S(2)}, u32[]{:S(2)}) collective-permute-start(f32[64,256]{1,0:T(8,128)S(1)} %collective-permute-done.13.refs_4_), channel_id=1, source_target_pairs={{0,4},{1,5},{2,6},{3,7},{4,0},{5,1},{6,2},{7,3},{8,12},{9,13},{10,... | collective-permute-start | bytes 196616 | tf_op jit(solution)/shard_map/ppermute | solution.py:270
  50.7 1.3 %collective-permute-start.16 = (f32[64,256]{1,0:T(8,128)S(1)}, f32[64,256]{1,0:T(8,128)S(1)}, u32[]{:S(2)}, u32[]{:S(2)}) collective-permute-start(f32[64,256]{1,0:T(8,128)S(1)} %collective-permute-done.14.refs_5_), channel_id=1, source_target_pairs={{0,4},{1,5},{2,6},{3,7},{4,0},{5,1},{6,2},{7,3},{8,12},{9,13},{10,... | collective-permute-start | bytes 196616 | tf_op jit(solution)/shard_map/ppermute | solution.py:270

commit v2 on v1

--- a/solution.py
+++ b/solution.py
@@ -151,7 +151,12 @@
 
 def payload_kernel(plan, angles, lorentz, owner, box, value, weight, value_out, weight_out):
     tiles = value.shape[0]
-    frames = angles.shape[0]
+    frames = angles.shape[1]
+    table = lorentz[...].reshape(1, -1)
+    entry = lax.broadcasted_iota(jnp.int32, table.shape, 1)
+    factors = [
+        jnp.sum(jnp.where(entry == angles[:, f : f + 1], table, 0.0), axis=1, keepdims=True) for f in range(frames)
+    ]
     across = lax.broadcasted_iota(jnp.int32, (tiles, tiles), 1)
     down = lax.broadcasted_iota(jnp.int32, (tiles, tiles), 0)
     flips = masked(plan.upper(owner[...]), FLIP_VOX)
@@ -166,7 +171,7 @@
         mask = jnp.broadcast_to(flips[span, :], (8, LANES))
         index = lanes ^ (mask & (LANES - 1))
         swap = (mask & LANES) != 0
-        factor = lorentz[angles[start // (tiles // frames)]]
+        factor = factors[start // (tiles // frames)]
         for ref, out, scale in ((value, value_out, factor), (weight, weight_out, 1.0)):
             low, high = ref[span, :LANES], ref[span, LANES:]
             out[span, :LANES] = lane_gather(jnp.where(swap, high, low), index) * scale
@@ -177,12 +182,11 @@
     shape = (value.shape[0] + 8, VOX)
     return pl.pallas_call(
         functools.partial(payload_kernel, plan),
-        in_specs=[pl.BlockSpec(memory_space=pltpu.SMEM)] * 2 + [pl.BlockSpec(memory_space=pltpu.VMEM)] * 4,
         out_shape=[jax.ShapeDtypeStruct(shape, jnp.float32)] * 2,
         compiler_params=pltpu.CompilerParams(vmem_limit_bytes=VMEM_LIMIT),
         cost_estimate=pl.CostEstimate(flops=1, bytes_accessed=1, transcendentals=0),
         name="payload",
-    )(angles, lorentz, owner, box, value, weight)
+    )(angles.reshape(1, -1), lorentz, owner, box, value, weight)
 
 
 def scatter_kernel(plan, olds, outs, payload, *refs):

time: 53.1 us -> 52.4 us (0.987)
  Pallas kernels: 12.1 us -> 11.3 us
    pallas_call x1, Pallas kernels: 1.06 us -> 0.32 us  [labelled(): pl.pallas_call(functools.partial(payload_kernel, plan), out_shape=[jax.Sh...]
where the time goes in v2:
time: 52.4 us; the launch traced here: 52.3 us
  starting transfers between devices  23.7 us (45%)
  waiting for transfers between devices  17 us (32%)
  Pallas kernels  11.3 us (22%)
    ppermute x17, starting transfers between devices, swap(): return lax.ppermute(array, AXES, pairs)  23.7 us
    ppermute x17, waiting for transfers between devices, swap(): return lax.ppermute(array, AXES, pairs)  17 us
    pallas_call x1, Pallas kernels, accumulate(): pl.pallas_call(accumulate_kernel, in_specs=[pl.BlockSpec(memory_space=pl....  8.57 us
    pallas_call x13, Pallas kernels, small_call(): pl.pallas_call(kernel, out_shape=[jax.ShapeDtypeStruct(shape, jnp.float32...  2.45 us
  transfers between devices with their start and end apart: 17, of which 9 were waited for; matrix products, arithmetic and copies ran while one was open for 0% of the time, Pallas kernels for 3%

profile of v2, /device:TPU:0, one launch (start us, length us, event | category | flops | bytes accessed | tf_op | source)
XLA Modules:
  0.0 52.3 jit_solution(4907629989149908490)
XLA Ops:
  0.0 8.6 %tile_sums.1 = (f32[128,256]{1,0:T(8,128)S(1)}, f32[128,256]{1,0:T(8,128)S(1)}) custom-call(bf16[2,64,128,128]{3,2,1,0:T(8,128)(2,1)} %counts.1, bf16[2,64,128,256]{3,2,1,0:T(8,128)(2,1)} %rows.1, bf16[2,64,128,256]{3,2,1,0:T(8,128)(2,1)} %cols.1, bf16[64,128,128]{2,1,0:T(8,128)(2,1)} %seen.1), custom_call_target="tpu_custom_call" | custom-call | flops 2147483648 | bytes 23068672 | tf_op jit(solution)/shard_map/tile_sums/pallas_call | solution.py:132
  9.0 3.0 %collective-permute-start = (f32[136,256]{1,0:T(8,128)S(1)}, f32[136,256]{1,0:T(8,128)S(1)}, u32[]{:S(2)}, u32[]{:S(2)}) collective-permute-start(f32[136,256]{1,0:T(8,128)S(1)} %get-tuple-element.27.first), channel_id=1, source_target_pairs={{0,8},{1,9},{2,10},{3,11},{4,5},{5,4},{6,7},{7,6},{8,0},{9,1},{10,... | collective-permute-start | bytes 417800 | tf_op jit(solution)/shard_map/ppermute | solution.py:274
  12.0 3.0 %collective-permute-done.second = f32[136,256]{1,0:T(8,128)S(1)} collective-permute-done((f32[136,256]{1,0:T(8,128)S(1)}, f32[136,256]{1,0:T(8,128)S(1)}, u32[]{:S(2)}, u32[]{:S(2)}) %collective-permute-start) | collective-permute-done | bytes 139296 | tf_op jit(solution)/shard_map/ppermute | solution.py:274
  15.0 2.2 %collective-permute-start.1 = (f32[272,256]{1,0:T(8,128)S(1)}, f32[272,256]{1,0:T(8,128)S(1)}, u32[]{:S(2)}, u32[]{:S(2)}) collective-permute-start(f32[272,256]{1,0:T(8,128)S(1)} %join.2.payload.rest_0_), channel_id=1, source_target_pairs={{0,1},{1,0},{2,3},{3,2},{4,12},{5,13},{6,14},{7,15},{8,9},{9,8},{1... | collective-permute-start | bytes 835592 | tf_op jit(solution)/shard_map/ppermute | solution.py:274
  17.2 1.5 %collective-permute-start.6 = (f32[272,256]{1,0:T(8,128)S(1)}, f32[272,256]{1,0:T(8,128)S(1)}, u32[]{:S(2)}, u32[]{:S(2)}) collective-permute-start(f32[272,256]{1,0:T(8,128)S(1)} %join.3.payload), channel_id=1, source_target_pairs={{0,1},{1,0},{2,3},{3,2},{4,12},{5,13},{6,14},{7,15},{8,9},{9,8},{1... | collective-permute-start | bytes 835592 | tf_op jit(solution)/shard_map/ppermute | solution.py:274
  19.3 2.4 %collective-permute-done.1.payload = f32[272,256]{1,0:T(8,128)S(1)} collective-permute-done((f32[272,256]{1,0:T(8,128)S(1)}, f32[272,256]{1,0:T(8,128)S(1)}, u32[]{:S(2)}, u32[]{:S(2)}) %collective-permute-start.1) | collective-permute-done | bytes 278560 | tf_op jit(solution)/shard_map/ppermute | solution.py:274
  21.7 0.3 box_sums.6
  22.1 2.6 %collective-permute-done.6.payload = f32[272,256]{1,0:T(8,128)S(1)} collective-permute-done((f32[272,256]{1,0:T(8,128)S(1)}, f32[272,256]{1,0:T(8,128)S(1)}, u32[]{:S(2)}, u32[]{:S(2)}) %collective-permute-start.6) | collective-permute-done | bytes 278560 | tf_op jit(solution)/shard_map/ppermute | solution.py:274
  24.7 0.3 box_sums.7
  25.2 2.0 %collective-permute-start.4 = (f32[128,256]{1,0:T(8,128)S(1)}, f32[128,256]{1,0:T(8,128)S(1)}, u32[]{:S(2)}, u32[]{:S(2)}) collective-permute-start(f32[128,256]{1,0:T(8,128)S(1)} %get-tuple-element.35), channel_id=1, source_target_pairs={{0,16},{1,17},{2,18},{3,19},{4,6},{5,7},{6,4},{7,5},{8,24},{9,25},... | collective-permute-start | bytes 393224 | tf_op jit(solution)/shard_map/ppermute | solution.py:274
  27.2 1.5 %collective-permute-start.8 = (f32[128,256]{1,0:T(8,128)S(1)}, f32[128,256]{1,0:T(8,128)S(1)}, u32[]{:S(2)}, u32[]{:S(2)}) collective-permute-start(f32[128,256]{1,0:T(8,128)S(1)} %get-tuple-element.42), channel_id=1, source_target_pairs={{0,16},{1,17},{2,18},{3,19},{4,6},{5,7},{6,4},{7,5},{8,24},{9,25},... | collective-permute-start | bytes 393224 | tf_op jit(solution)/shard_map/ppermute | solution.py:274
  28.7 1.5 %collective-permute-done.4.refs_1_ = f32[128,256]{1,0:T(8,128)S(1)} collective-permute-done((f32[128,256]{1,0:T(8,128)S(1)}, f32[128,256]{1,0:T(8,128)S(1)}, u32[]{:S(2)}, u32[]{:S(2)}) %collective-permute-start.4) | collective-permute-done | bytes 131104 | tf_op jit(solution)/shard_map/ppermute | solution.py:274
  30.2 3.1 %collective-permute-start.5 = (f32[64,256]{1,0:T(8,128)S(1)}, f32[64,256]{1,0:T(8,128)S(1)}, u32[]{:S(2)}, u32[]{:S(2)}) collective-permute-start(f32[64,256]{1,0:T(8,128)S(1)} %get-tuple-element.37), channel_id=1, source_target_pairs={{0,2},{1,3},{2,0},{3,1},{4,20},{5,21},{6,22},{7,23},{8,10},{9,11},... | collective-permute-start | bytes 196616 | tf_op jit(solution)/shard_map/ppermute | solution.py:274
  33.3 1.6 %collective-permute-start.9 = (f32[64,256]{1,0:T(8,128)S(1)}, f32[64,256]{1,0:T(8,128)S(1)}, u32[]{:S(2)}, u32[]{:S(2)}) collective-permute-start(f32[64,256]{1,0:T(8,128)S(1)} %get-tuple-element.44), channel_id=1, source_target_pairs={{0,2},{1,3},{2,0},{3,1},{4,20},{5,21},{6,22},{7,23},{8,10},{9,11},... | collective-permute-start | bytes 196616 | tf_op jit(solution)/shard_map/ppermute | solution.py:274
  34.9 1.0 %collective-permute-done.5.refs_1_ = f32[64,256]{1,0:T(8,128)S(1)} collective-permute-done((f32[64,256]{1,0:T(8,128)S(1)}, f32[64,256]{1,0:T(8,128)S(1)}, u32[]{:S(2)}, u32[]{:S(2)}) %collective-permute-start.5) | collective-permute-done | bytes 65568 | tf_op jit(solution)/shard_map/ppermute | solution.py:274
  35.9 2.6 %collective-permute-done.9.refs_1_ = f32[64,256]{1,0:T(8,128)S(1)} collective-permute-done((f32[64,256]{1,0:T(8,128)S(1)}, f32[64,256]{1,0:T(8,128)S(1)}, u32[]{:S(2)}, u32[]{:S(2)}) %collective-permute-start.9) | collective-permute-done | bytes 65568 | tf_op jit(solution)/shard_map/ppermute | solution.py:274
  38.6 3.2 %collective-permute-start.10 = (f32[64,256]{1,0:T(8,128)S(1)}, f32[64,256]{1,0:T(8,128)S(1)}, u32[]{:S(2)}, u32[]{:S(2)}) collective-permute-start(f32[64,256]{1,0:T(8,128)S(1)} %intensity.1.refs_0_), channel_id=1, source_target_pairs={{0,3},{1,2},{2,1},{3,0},{4,28},{5,29},{6,30},{7,31},{8,11},{9,10},... | collective-permute-start | bytes 196616 | tf_op jit(solution)/shard_map/ppermute | solution.py:274
  41.8 2.3 %collective-permute-start.13 = (f32[64,256]{1,0:T(8,128)S(1)}, f32[64,256]{1,0:T(8,128)S(1)}, u32[]{:S(2)}, u32[]{:S(2)}) collective-permute-start(f32[64,256]{1,0:T(8,128)S(1)} %intensity.1.refs_0_), channel_id=1, source_target_pairs={{0,24},{1,25},{2,26},{3,27},{4,7},{5,6},{6,5},{7,4},{8,16},{9,17},... | collective-permute-start | bytes 196616 | tf_op jit(solution)/shard_map/ppermute | solution.py:274
  44.1 0.7 %collective-permute-done.10.refs_1_ = f32[64,256]{1,0:T(8,128)S(1)} collective-permute-done((f32[64,256]{1,0:T(8,128)S(1)}, f32[64,256]{1,0:T(8,128)S(1)}, u32[]{:S(2)}, u32[]{:S(2)}) %collective-permute-start.10) | collective-permute-done | bytes 65568 | tf_op jit(solution)/shard_map/ppermute | solution.py:274
  44.8 2.6 %collective-permute-start.14 = (f32[64,256]{1,0:T(8,128)S(1)}, f32[64,256]{1,0:T(8,128)S(1)}, u32[]{:S(2)}, u32[]{:S(2)}) collective-permute-start(f32[64,256]{1,0:T(8,128)S(1)} %collective-permute-done.10.refs_1_), channel_id=1, source_target_pairs={{0,24},{1,25},{2,26},{3,27},{4,7},{5,6},{6,5},{7,4},{8,16},{9,17},... | collective-permute-start | bytes 196616 | tf_op jit(solution)/shard_map/ppermute | solution.py:274
  47.5 0.5 collective-permute-start.12
  48.0 2.0 %collective-permute-done.14.refs_5_ = f32[64,256]{1,0:T(8,128)S(1)} collective-permute-done((f32[64,256]{1,0:T(8,128)S(1)}, f32[64,256]{1,0:T(8,128)S(1)}, u32[]{:S(2)}, u32[]{:S(2)}) %collective-permute-start.14) | collective-permute-done | bytes 65568 | tf_op jit(solution)/shard_map/ppermute | solution.py:274
  50.0 1.2 %collective-permute-done.16.refs_7_ = f32[64,256]{1,0:T(8,128)S(1)} collective-permute-done((f32[64,256]{1,0:T(8,128)S(1)}, f32[64,256]{1,0:T(8,128)S(1)}, u32[]{:S(2)}, u32[]{:S(2)}) %collective-permute-start.16) | collective-permute-done | bytes 65568 | tf_op jit(solution)/shard_map/ppermute | solution.py:274
  51.2 1.0 %unfold.1 = f32[512,256]{1,0:T(8,128)} custom-call(f32[64,256]{1,0:T(8,128)S(1)} %intensity.1.refs_0_, f32[64,256]{1,0:T(8,128)S(1)} %collective-permute-done.10.refs_1_, f32[64,256]{1,0:T(8,128)S(1)} %collective-permute-done.11.refs_2_, f32[64,256]{1,0:T(8,128)S(1)} %collective-permute-done.12.refs_3_, f32[64,256]{1,0:T(8,128)S(1)} %collective-permute-done.13.refs_4_, ...), custom_call_target="tpu_custom_call" | custom-call | flops 1 | bytes 1 | tf_op jit(solution)/shard_map/unfold/pallas_call | solution.py:261
  (33 shorter events, 1.4 us)
Async XLA Ops:
  0.0 8.6 %copy-start.3 = (s32[128]{0:T(128)S(1)}, s32[128]{0:T(128)}, u32[]{:S(2)}) copy-start(s32[128]{0:T(128)} %param.15) | copy-start | bytes 1540
  0.0 8.6 %copy-start.2 = (s32[128,1]{0,1:T(1,128)S(1)}, s32[128,1]{0,1:T(1,128)}, u32[]{:S(2)}) copy-start(s32[128,1]{0,1:T(1,128)} %param.14) | copy-start | bytes 1540
  0.0 8.6 %copy-start.1 = (s32[2]{0:T(128)S(1)}, s32[2]{0:T(128)}, u32[]{:S(2)}) copy-start(s32[2]{0:T(128)} %param.13) | copy-start | bytes 28
  0.0 8.6 %copy-start = (f32[3600]{0:T(1024)S(1)}, f32[3600]{0:T(1024)}, u32[]{:S(2)}) copy-start(f32[3600]{0:T(1024)} %lorentz.1) | copy-start | bytes 43204
  9.0 6.1 %collective-permute-start = (f32[136,256]{1,0:T(8,128)S(1)}, f32[136,256]{1,0:T(8,128)S(1)}, u32[]{:S(2)}, u32[]{:S(2)}) collective-permute-start(f32[136,256]{1,0:T(8,128)S(1)} %get-tuple-element.27.first), channel_id=1, source_target_pairs={{0,8},{1,9},{2,10},{3,11},{4,5},{5,4},{6,7},{7,6},{8,0},{9,1},{10,... | collective-permute-start | bytes 417800 | tf_op jit(solution)/shard_map/ppermute | solution.py:274
  12.0 5.2 %collective-permute-start.2 = (f32[136,256]{1,0:T(8,128)S(1)}, f32[136,256]{1,0:T(8,128)S(1)}, u32[]{:S(2)}, u32[]{:S(2)}) collective-permute-start(f32[136,256]{1,0:T(8,128)S(1)} %get-tuple-element.30.first), channel_id=1, source_target_pairs={{0,8},{1,9},{2,10},{3,11},{4,5},{5,4},{6,7},{7,6},{8,0},{9,1},{10,... | collective-permute-start | bytes 417800 | tf_op jit(solution)/shard_map/ppermute | solution.py:274
  15.0 6.7 %collective-permute-start.1 = (f32[272,256]{1,0:T(8,128)S(1)}, f32[272,256]{1,0:T(8,128)S(1)}, u32[]{:S(2)}, u32[]{:S(2)}) collective-permute-start(f32[272,256]{1,0:T(8,128)S(1)} %join.2.payload.rest_0_), channel_id=1, source_target_pairs={{0,1},{1,0},{2,3},{3,2},{4,12},{5,13},{6,14},{7,15},{8,9},{9,8},{1... | collective-permute-start | bytes 835592 | tf_op jit(solution)/shard_map/ppermute | solution.py:274
  17.2 7.5 %collective-permute-start.6 = (f32[272,256]{1,0:T(8,128)S(1)}, f32[272,256]{1,0:T(8,128)S(1)}, u32[]{:S(2)}, u32[]{:S(2)}) collective-permute-start(f32[272,256]{1,0:T(8,128)S(1)} %join.3.payload), channel_id=1, source_target_pairs={{0,1},{1,0},{2,3},{3,2},{4,12},{5,13},{6,14},{7,15},{8,9},{9,8},{1... | collective-permute-start | bytes 835592 | tf_op jit(solution)/shard_map/ppermute | solution.py:274
  22.0 3.1 %collective-permute-start.3 = (f32[256,256]{1,0:T(8,128)S(1)}, f32[256,256]{1,0:T(8,128)S(1)}, u32[]{:S(2)}, u32[]{:S(2)}) collective-permute-start(f32[256,256]{1,0:T(8,128)S(1)} %get-tuple-element.33), channel_id=1, source_target_pairs={{0,4},{1,5},{2,6},{3,7},{4,0},{5,1},{6,2},{7,3},{8,12},{9,13},{10,... | collective-permute-start | bytes 786440 | tf_op jit(solution)/shard_map/ppermute | solution.py:274
  25.0 2.2 %collective-permute-start.7 = (f32[256,256]{1,0:T(8,128)S(1)}, f32[256,256]{1,0:T(8,128)S(1)}, u32[]{:S(2)}, u32[]{:S(2)}) collective-permute-start(f32[256,256]{1,0:T(8,128)S(1)} %get-tuple-element.40), channel_id=1, source_target_pairs={{0,4},{1,5},{2,6},{3,7},{4,0},{5,1},{6,2},{7,3},{8,12},{9,13},{10,... | collective-permute-start | bytes 786440 | tf_op jit(solution)/shard_map/ppermute | solution.py:274
  25.2 5.0 %collective-permute-start.4 = (f32[128,256]{1,0:T(8,128)S(1)}, f32[128,256]{1,0:T(8,128)S(1)}, u32[]{:S(2)}, u32[]{:S(2)}) collective-permute-start(f32[128,256]{1,0:T(8,128)S(1)} %get-tuple-element.35), channel_id=1, source_target_pairs={{0,16},{1,17},{2,18},{3,19},{4,6},{5,7},{6,4},{7,5},{8,24},{9,25},... | collective-permute-start | bytes 393224 | tf_op jit(solution)/shard_map/ppermute | solution.py:274
  27.2 6.1 %collective-permute-start.8 = (f32[128,256]{1,0:T(8,128)S(1)}, f32[128,256]{1,0:T(8,128)S(1)}, u32[]{:S(2)}, u32[]{:S(2)}) collective-permute-start(f32[128,256]{1,0:T(8,128)S(1)} %get-tuple-element.42), channel_id=1, source_target_pairs={{0,16},{1,17},{2,18},{3,19},{4,6},{5,7},{6,4},{7,5},{8,24},{9,25},... | collective-permute-start | bytes 393224 | tf_op jit(solution)/shard_map/ppermute | solution.py:274
  30.2 5.7 %collective-permute-start.5 = (f32[64,256]{1,0:T(8,128)S(1)}, f32[64,256]{1,0:T(8,128)S(1)}, u32[]{:S(2)}, u32[]{:S(2)}) collective-permute-start(f32[64,256]{1,0:T(8,128)S(1)} %get-tuple-element.37), channel_id=1, source_target_pairs={{0,2},{1,3},{2,0},{3,1},{4,20},{5,21},{6,22},{7,23},{8,10},{9,11},... | collective-permute-start | bytes 196616 | tf_op jit(solution)/shard_map/ppermute | solution.py:274
  33.3 5.2 %collective-permute-start.9 = (f32[64,256]{1,0:T(8,128)S(1)}, f32[64,256]{1,0:T(8,128)S(1)}, u32[]{:S(2)}, u32[]{:S(2)}) collective-permute-start(f32[64,256]{1,0:T(8,128)S(1)} %get-tuple-element.44), channel_id=1, source_target_pairs={{0,2},{1,3},{2,0},{3,1},{4,20},{5,21},{6,22},{7,23},{8,10},{9,11},... | collective-permute-start | bytes 196616 | tf_op jit(solution)/shard_map/ppermute | solution.py:274
  38.6 6.2 %collective-permute-start.10 = (f32[64,256]{1,0:T(8,128)S(1)}, f32[64,256]{1,0:T(8,128)S(1)}, u32[]{:S(2)}, u32[]{:S(2)}) collective-permute-start(f32[64,256]{1,0:T(8,128)S(1)} %intensity.1.refs_0_), channel_id=1, source_target_pairs={{0,3},{1,2},{2,1},{3,0},{4,28},{5,29},{6,30},{7,31},{8,11},{9,10},... | collective-permute-start | bytes 196616 | tf_op jit(solution)/shard_map/ppermute | solution.py:274
  41.8 6.2 %collective-permute-start.13 = (f32[64,256]{1,0:T(8,128)S(1)}, f32[64,256]{1,0:T(8,128)S(1)}, u32[]{:S(2)}, u32[]{:S(2)}) collective-permute-start(f32[64,256]{1,0:T(8,128)S(1)} %intensity.1.refs_0_), channel_id=1, source_target_pairs={{0,24},{1,25},{2,26},{3,27},{4,7},{5,6},{6,5},{7,4},{8,16},{9,17},... | collective-permute-start | bytes 196616 | tf_op jit(solution)/shard_map/ppermute | solution.py:274
  44.8 5.2 %collective-permute-start.14 = (f32[64,256]{1,0:T(8,128)S(1)}, f32[64,256]{1,0:T(8,128)S(1)}, u32[]{:S(2)}, u32[]{:S(2)}) collective-permute-start(f32[64,256]{1,0:T(8,128)S(1)} %collective-permute-done.10.refs_1_), channel_id=1, source_target_pairs={{0,24},{1,25},{2,26},{3,27},{4,7},{5,6},{6,5},{7,4},{8,16},{9,17},... | collective-permute-start | bytes 196616 | tf_op jit(solution)/shard_map/ppermute | solution.py:274
  47.5 2.5 %collective-permute-start.11 = (f32[64,256]{1,0:T(8,128)S(1)}, f32[64,256]{1,0:T(8,128)S(1)}, u32[]{:S(2)}, u32[]{:S(2)}) collective-permute-start(f32[64,256]{1,0:T(8,128)S(1)} %intensity.1.refs_0_), channel_id=1, source_target_pairs={{0,4},{1,5},{2,6},{3,7},{4,0},{5,1},{6,2},{7,3},{8,12},{9,13},{10,... | collective-permute-start | bytes 196616 | tf_op jit(solution)/shard_map/ppermute | solution.py:274
  47.5 2.5 %collective-permute-start.12 = (f32[64,256]{1,0:T(8,128)S(1)}, f32[64,256]{1,0:T(8,128)S(1)}, u32[]{:S(2)}, u32[]{:S(2)}) collective-permute-start(f32[64,256]{1,0:T(8,128)S(1)} %collective-permute-done.10.refs_1_), channel_id=1, source_target_pairs={{0,4},{1,5},{2,6},{3,7},{4,0},{5,1},{6,2},{7,3},{8,12},{9,13},{10,... | collective-permute-start | bytes 196616 | tf_op jit(solution)/shard_map/ppermute | solution.py:274
  48.0 2.0 %collective-permute-start.15 = (f32[64,256]{1,0:T(8,128)S(1)}, f32[64,256]{1,0:T(8,128)S(1)}, u32[]{:S(2)}, u32[]{:S(2)}) collective-permute-start(f32[64,256]{1,0:T(8,128)S(1)} %collective-permute-done.13.refs_4_), channel_id=1, source_target_pairs={{0,4},{1,5},{2,6},{3,7},{4,0},{5,1},{6,2},{7,3},{8,12},{9,13},{10,... | collective-permute-start | bytes 196616 | tf_op jit(solution)/shard_map/ppermute | solution.py:274
  50.0 1.3 %collective-permute-start.16 = (f32[64,256]{1,0:T(8,128)S(1)}, f32[64,256]{1,0:T(8,128)S(1)}, u32[]{:S(2)}, u32[]{:S(2)}) collective-permute-start(f32[64,256]{1,0:T(8,128)S(1)} %collective-permute-done.14.refs_5_), channel_id=1, source_target_pairs={{0,4},{1,5},{2,6},{3,7},{4,0},{5,1},{6,2},{7,3},{8,12},{9,13},{10,... | collective-permute-start | bytes 196616 | tf_op jit(solution)/shard_map/ppermute | solution.py:274

commit v3 on v2

--- a/solution.py
+++ b/solution.py
@@ -17,6 +17,7 @@
 FLIP_BOX = (0b110000, 0b001100, 0b000011)
 AXES = ("bx", "by", "bz")
 POSITIONS = 8
+LAST_PARTS = (4, 2, 2)
 TILE_LIMIT = 53 * 1024 * 1024
 VMEM_LIMIT = 24 * 1024 * 1024
 LARGE = 10**10
@@ -85,23 +86,27 @@
     frames, positions = counts.shape[0], counts.shape[1]
     blocks = positions // POSITIONS
 
-    def copies(block):
-        span = pl.ds(block * POSITIONS, POSITIONS)
+    def copies(start, count, slot):
+        span = pl.ds(start, count)
         views = [(ref.at[:, span], held.at[:, span]) for ref, held in zip((counts, rows, cols), arrays)]
         views.append((seen.at[span], arrays[3].at[span]))
-        return [pltpu.make_async_copy(src, dst, sems.at[block, i]) for i, (src, dst) in enumerate(views)]
-
-    for block in range(blocks):
-        for copy in copies(block):
+        return [pltpu.make_async_copy(src, dst, sems.at[slot, i]) for i, (src, dst) in enumerate(views)]
+
+    last, start = {}, positions - POSITIONS
+    for slot, count in enumerate(LAST_PARTS, blocks - 1):
+        last[start + POSITIONS - positions] = (start, count, slot)
+        start += count
+    for landing in [(block * POSITIONS, POSITIONS, block) for block in range(blocks - 1)] + list(last.values()):
+        for copy in copies(*landing):
             copy.start()
 
     held_counts, held_rows, held_cols, held_seen = arrays
 
-    @pl.loop(0, blocks)
-    def _(block):
-        for copy in copies(block):
-            copy.wait()
+    def compute(block, landings):
         for p in range(POSITIONS):
+            if p in landings:
+                for copy in copies(*landings[p]):
+                    copy.wait()
             at = block * POSITIONS + p
             for f in range(frames):
                 weights = held_cols[f, at]
@@ -124,6 +129,12 @@
                     parts = [partial[f, kind, half, pl.ds(row, POSITIONS, stride=8), :] for row in range(8)]
                     out[place, lanes] = sum(parts)
 
+    @pl.loop(0, blocks - 1)
+    def _(block):
+        compute(block, {0: (block * POSITIONS, POSITIONS, block)})
+
+    compute(blocks - 1, last)
+
 
 def accumulate(counts, row_split, col_split, efficiency):
     frames, positions, pixels, _ = counts.shape
@@ -136,7 +147,7 @@
         out_shape=[jax.ShapeDtypeStruct((tiles, VOX), jnp.float32)] * 2,
         scratch_shapes=[pltpu.VMEM(array.shape, array.dtype) for array in arrays]
         + [
-            pltpu.SemaphoreType.DMA((positions // POSITIONS, 4)),
+            pltpu.SemaphoreType.DMA((positions // POSITIONS - 1 + len(LAST_PARTS), 4)),
             pltpu.VMEM((frames, 2, 2, 8 * POSITIONS, LANES), jnp.float32),
         ],
         compiler_params=pltpu.CompilerParams(vmem_limit_bytes=TILE_LIMIT),

time: 52.4 us -> 52.7 us (level)
  no operation moved by 1% of the time
where the time goes in v3:
time: 52.7 us; the launch traced here: 52.6 us
  starting transfers between devices  23.7 us (45%)
  waiting for transfers between devices  17 us (32%)
  Pallas kernels  11.7 us (22%)
    ppermute x17, starting transfers between devices, swap(): return lax.ppermute(array, AXES, pairs)  23.7 us
    ppermute x17, waiting for transfers between devices, swap(): return lax.ppermute(array, AXES, pairs)  17 us
    pallas_call x1, Pallas kernels, accumulate(): pl.pallas_call(accumulate_kernel, in_specs=[pl.BlockSpec(memory_space=pl....  8.9 us
    pallas_call x13, Pallas kernels, small_call(): pl.pallas_call(kernel, out_shape=[jax.ShapeDtypeStruct(shape, jnp.float32...  2.45 us
  transfers between devices with their start and end apart: 17, of which 9 were waited for; matrix products, arithmetic and copies ran while one was open for 0% of the time, Pallas kernels for 3%

profile of v3, /device:TPU:0, one launch (start us, length us, event | category | flops | bytes accessed | tf_op | source)
XLA Modules:
  0.0 52.6 jit_solution(10505763072526757890)
XLA Ops:
  0.0 8.9 %tile_sums.1 = (f32[128,256]{1,0:T(8,128)S(1)}, f32[128,256]{1,0:T(8,128)S(1)}) custom-call(bf16[2,64,128,128]{3,2,1,0:T(8,128)(2,1)} %counts.1, bf16[2,64,128,256]{3,2,1,0:T(8,128)(2,1)} %rows.1, bf16[2,64,128,256]{3,2,1,0:T(8,128)(2,1)} %cols.1, bf16[64,128,128]{2,1,0:T(8,128)(2,1)} %seen.1), custom_call_target="tpu_custom_call" | custom-call | flops 2147483648 | bytes 23068672 | tf_op jit(solution)/shard_map/tile_sums/pallas_call | solution.py:143
  9.0 0.3 payload.1
  9.3 3.0 %collective-permute-start = (f32[136,256]{1,0:T(8,128)S(1)}, f32[136,256]{1,0:T(8,128)S(1)}, u32[]{:S(2)}, u32[]{:S(2)}) collective-permute-start(f32[136,256]{1,0:T(8,128)S(1)} %get-tuple-element.27.first), channel_id=1, source_target_pairs={{0,8},{1,9},{2,10},{3,11},{4,5},{5,4},{6,7},{7,6},{8,0},{9,1},{10,... | collective-permute-start | bytes 417800 | tf_op jit(solution)/shard_map/ppermute | solution.py:285
  12.4 3.0 %collective-permute-done.second = f32[136,256]{1,0:T(8,128)S(1)} collective-permute-done((f32[136,256]{1,0:T(8,128)S(1)}, f32[136,256]{1,0:T(8,128)S(1)}, u32[]{:S(2)}, u32[]{:S(2)}) %collective-permute-start) | collective-permute-done | bytes 139296 | tf_op jit(solution)/shard_map/ppermute | solution.py:285
  15.3 2.2 %collective-permute-start.1 = (f32[272,256]{1,0:T(8,128)S(1)}, f32[272,256]{1,0:T(8,128)S(1)}, u32[]{:S(2)}, u32[]{:S(2)}) collective-permute-start(f32[272,256]{1,0:T(8,128)S(1)} %join.2.payload.rest_0_), channel_id=1, source_target_pairs={{0,1},{1,0},{2,3},{3,2},{4,12},{5,13},{6,14},{7,15},{8,9},{9,8},{1... | collective-permute-start | bytes 835592 | tf_op jit(solution)/shard_map/ppermute | solution.py:285
  17.5 1.5 %collective-permute-start.6 = (f32[272,256]{1,0:T(8,128)S(1)}, f32[272,256]{1,0:T(8,128)S(1)}, u32[]{:S(2)}, u32[]{:S(2)}) collective-permute-start(f32[272,256]{1,0:T(8,128)S(1)} %join.3.payload), channel_id=1, source_target_pairs={{0,1},{1,0},{2,3},{3,2},{4,12},{5,13},{6,14},{7,15},{8,9},{9,8},{1... | collective-permute-start | bytes 835592 | tf_op jit(solution)/shard_map/ppermute | solution.py:285
  19.7 2.4 %collective-permute-done.1.payload = f32[272,256]{1,0:T(8,128)S(1)} collective-permute-done((f32[272,256]{1,0:T(8,128)S(1)}, f32[272,256]{1,0:T(8,128)S(1)}, u32[]{:S(2)}, u32[]{:S(2)}) %collective-permute-start.1) | collective-permute-done | bytes 278560 | tf_op jit(solution)/shard_map/ppermute | solution.py:285
  22.0 0.3 box_sums.6
  22.4 2.6 %collective-permute-done.6.payload = f32[272,256]{1,0:T(8,128)S(1)} collective-permute-done((f32[272,256]{1,0:T(8,128)S(1)}, f32[272,256]{1,0:T(8,128)S(1)}, u32[]{:S(2)}, u32[]{:S(2)}) %collective-permute-start.6) | collective-permute-done | bytes 278560 | tf_op jit(solution)/shard_map/ppermute | solution.py:285
  25.5 2.0 %collective-permute-start.4 = (f32[128,256]{1,0:T(8,128)S(1)}, f32[128,256]{1,0:T(8,128)S(1)}, u32[]{:S(2)}, u32[]{:S(2)}) collective-permute-start(f32[128,256]{1,0:T(8,128)S(1)} %get-tuple-element.35), channel_id=1, source_target_pairs={{0,16},{1,17},{2,18},{3,19},{4,6},{5,7},{6,4},{7,5},{8,24},{9,25},... | collective-permute-start | bytes 393224 | tf_op jit(solution)/shard_map/ppermute | solution.py:285
  27.5 1.5 %collective-permute-start.8 = (f32[128,256]{1,0:T(8,128)S(1)}, f32[128,256]{1,0:T(8,128)S(1)}, u32[]{:S(2)}, u32[]{:S(2)}) collective-permute-start(f32[128,256]{1,0:T(8,128)S(1)} %get-tuple-element.42), channel_id=1, source_target_pairs={{0,16},{1,17},{2,18},{3,19},{4,6},{5,7},{6,4},{7,5},{8,24},{9,25},... | collective-permute-start | bytes 393224 | tf_op jit(solution)/shard_map/ppermute | solution.py:285
  29.0 1.5 %collective-permute-done.4.refs_1_ = f32[128,256]{1,0:T(8,128)S(1)} collective-permute-done((f32[128,256]{1,0:T(8,128)S(1)}, f32[128,256]{1,0:T(8,128)S(1)}, u32[]{:S(2)}, u32[]{:S(2)}) %collective-permute-start.4) | collective-permute-done | bytes 131104 | tf_op jit(solution)/shard_map/ppermute | solution.py:285
  30.5 3.1 %collective-permute-start.5 = (f32[64,256]{1,0:T(8,128)S(1)}, f32[64,256]{1,0:T(8,128)S(1)}, u32[]{:S(2)}, u32[]{:S(2)}) collective-permute-start(f32[64,256]{1,0:T(8,128)S(1)} %get-tuple-element.37), channel_id=1, source_target_pairs={{0,2},{1,3},{2,0},{3,1},{4,20},{5,21},{6,22},{7,23},{8,10},{9,11},... | collective-permute-start | bytes 196616 | tf_op jit(solution)/shard_map/ppermute | solution.py:285
  33.6 1.6 %collective-permute-start.9 = (f32[64,256]{1,0:T(8,128)S(1)}, f32[64,256]{1,0:T(8,128)S(1)}, u32[]{:S(2)}, u32[]{:S(2)}) collective-permute-start(f32[64,256]{1,0:T(8,128)S(1)} %get-tuple-element.44), channel_id=1, source_target_pairs={{0,2},{1,3},{2,0},{3,1},{4,20},{5,21},{6,22},{7,23},{8,10},{9,11},... | collective-permute-start | bytes 196616 | tf_op jit(solution)/shard_map/ppermute | solution.py:285
  35.2 1.0 %collective-permute-done.5.refs_1_ = f32[64,256]{1,0:T(8,128)S(1)} collective-permute-done((f32[64,256]{1,0:T(8,128)S(1)}, f32[64,256]{1,0:T(8,128)S(1)}, u32[]{:S(2)}, u32[]{:S(2)}) %collective-permute-start.5) | collective-permute-done | bytes 65568 | tf_op jit(solution)/shard_map/ppermute | solution.py:285
  36.2 2.6 %collective-permute-done.9.refs_1_ = f32[64,256]{1,0:T(8,128)S(1)} collective-permute-done((f32[64,256]{1,0:T(8,128)S(1)}, f32[64,256]{1,0:T(8,128)S(1)}, u32[]{:S(2)}, u32[]{:S(2)}) %collective-permute-start.9) | collective-permute-done | bytes 65568 | tf_op jit(solution)/shard_map/ppermute | solution.py:285
  38.9 3.2 %collective-permute-start.10 = (f32[64,256]{1,0:T(8,128)S(1)}, f32[64,256]{1,0:T(8,128)S(1)}, u32[]{:S(2)}, u32[]{:S(2)}) collective-permute-start(f32[64,256]{1,0:T(8,128)S(1)} %intensity.1.refs_0_), channel_id=1, source_target_pairs={{0,3},{1,2},{2,1},{3,0},{4,28},{5,29},{6,30},{7,31},{8,11},{9,10},... | collective-permute-start | bytes 196616 | tf_op jit(solution)/shard_map/ppermute | solution.py:285
  42.1 2.3 %collective-permute-start.13 = (f32[64,256]{1,0:T(8,128)S(1)}, f32[64,256]{1,0:T(8,128)S(1)}, u32[]{:S(2)}, u32[]{:S(2)}) collective-permute-start(f32[64,256]{1,0:T(8,128)S(1)} %intensity.1.refs_0_), channel_id=1, source_target_pairs={{0,24},{1,25},{2,26},{3,27},{4,7},{5,6},{6,5},{7,4},{8,16},{9,17},... | collective-permute-start | bytes 196616 | tf_op jit(solution)/shard_map/ppermute | solution.py:285
  44.4 0.7 %collective-permute-done.10.refs_1_ = f32[64,256]{1,0:T(8,128)S(1)} collective-permute-done((f32[64,256]{1,0:T(8,128)S(1)}, f32[64,256]{1,0:T(8,128)S(1)}, u32[]{:S(2)}, u32[]{:S(2)}) %collective-permute-start.10) | collective-permute-done | bytes 65568 | tf_op jit(solution)/shard_map/ppermute | solution.py:285
  45.1 2.6 %collective-permute-start.14 = (f32[64,256]{1,0:T(8,128)S(1)}, f32[64,256]{1,0:T(8,128)S(1)}, u32[]{:S(2)}, u32[]{:S(2)}) collective-permute-start(f32[64,256]{1,0:T(8,128)S(1)} %collective-permute-done.10.refs_1_), channel_id=1, source_target_pairs={{0,24},{1,25},{2,26},{3,27},{4,7},{5,6},{6,5},{7,4},{8,16},{9,17},... | collective-permute-start | bytes 196616 | tf_op jit(solution)/shard_map/ppermute | solution.py:285
  47.8 0.5 collective-permute-start.12
  48.3 2.0 %collective-permute-done.14.refs_5_ = f32[64,256]{1,0:T(8,128)S(1)} collective-permute-done((f32[64,256]{1,0:T(8,128)S(1)}, f32[64,256]{1,0:T(8,128)S(1)}, u32[]{:S(2)}, u32[]{:S(2)}) %collective-permute-start.14) | collective-permute-done | bytes 65568 | tf_op jit(solution)/shard_map/ppermute | solution.py:285
  50.3 1.2 %collective-permute-done.16.refs_7_ = f32[64,256]{1,0:T(8,128)S(1)} collective-permute-done((f32[64,256]{1,0:T(8,128)S(1)}, f32[64,256]{1,0:T(8,128)S(1)}, u32[]{:S(2)}, u32[]{:S(2)}) %collective-permute-start.16) | collective-permute-done | bytes 65568 | tf_op jit(solution)/shard_map/ppermute | solution.py:285
  51.6 1.0 %unfold.1 = f32[512,256]{1,0:T(8,128)} custom-call(f32[64,256]{1,0:T(8,128)S(1)} %intensity.1.refs_0_, f32[64,256]{1,0:T(8,128)S(1)} %collective-permute-done.10.refs_1_, f32[64,256]{1,0:T(8,128)S(1)} %collective-permute-done.11.refs_2_, f32[64,256]{1,0:T(8,128)S(1)} %collective-permute-done.12.refs_3_, f32[64,256]{1,0:T(8,128)S(1)} %collective-permute-done.13.refs_4_, ...), custom_call_target="tpu_custom_call" | custom-call | flops 1 | bytes 1 | tf_op jit(solution)/shard_map/unfold/pallas_call | solution.py:272
  (33 shorter events, 1.4 us)
Async XLA Ops:
  0.0 8.9 %copy-start.3 = (s32[128]{0:T(128)S(1)}, s32[128]{0:T(128)}, u32[]{:S(2)}) copy-start(s32[128]{0:T(128)} %param.15) | copy-start | bytes 1540
  0.0 8.9 %copy-start.2 = (s32[128,1]{0,1:T(1,128)S(1)}, s32[128,1]{0,1:T(1,128)}, u32[]{:S(2)}) copy-start(s32[128,1]{0,1:T(1,128)} %param.14) | copy-start | bytes 1540
  0.0 8.9 %copy-start.1 = (s32[2]{0:T(128)S(1)}, s32[2]{0:T(128)}, u32[]{:S(2)}) copy-start(s32[2]{0:T(128)} %param.13) | copy-start | bytes 28
  0.0 8.9 %copy-start = (f32[3600]{0:T(1024)S(1)}, f32[3600]{0:T(1024)}, u32[]{:S(2)}) copy-start(f32[3600]{0:T(1024)} %lorentz.1) | copy-start | bytes 43204
  9.3 6.0 %collective-permute-start = (f32[136,256]{1,0:T(8,128)S(1)}, f32[136,256]{1,0:T(8,128)S(1)}, u32[]{:S(2)}, u32[]{:S(2)}) collective-permute-start(f32[136,256]{1,0:T(8,128)S(1)} %get-tuple-element.27.first), channel_id=1, source_target_pairs={{0,8},{1,9},{2,10},{3,11},{4,5},{5,4},{6,7},{7,6},{8,0},{9,1},{10,... | collective-permute-start | bytes 417800 | tf_op jit(solution)/shard_map/ppermute | solution.py:285
  12.3 5.2 %collective-permute-start.2 = (f32[136,256]{1,0:T(8,128)S(1)}, f32[136,256]{1,0:T(8,128)S(1)}, u32[]{:S(2)}, u32[]{:S(2)}) collective-permute-start(f32[136,256]{1,0:T(8,128)S(1)} %get-tuple-element.30.first), channel_id=1, source_target_pairs={{0,8},{1,9},{2,10},{3,11},{4,5},{5,4},{6,7},{7,6},{8,0},{9,1},{10,... | collective-permute-start | bytes 417800 | tf_op jit(solution)/shard_map/ppermute | solution.py:285
  15.3 6.7 %collective-permute-start.1 = (f32[272,256]{1,0:T(8,128)S(1)}, f32[272,256]{1,0:T(8,128)S(1)}, u32[]{:S(2)}, u32[]{:S(2)}) collective-permute-start(f32[272,256]{1,0:T(8,128)S(1)} %join.2.payload.rest_0_), channel_id=1, source_target_pairs={{0,1},{1,0},{2,3},{3,2},{4,12},{5,13},{6,14},{7,15},{8,9},{9,8},{1... | collective-permute-start | bytes 835592 | tf_op jit(solution)/shard_map/ppermute | solution.py:285
  17.5 7.5 %collective-permute-start.6 = (f32[272,256]{1,0:T(8,128)S(1)}, f32[272,256]{1,0:T(8,128)S(1)}, u32[]{:S(2)}, u32[]{:S(2)}) collective-permute-start(f32[272,256]{1,0:T(8,128)S(1)} %join.3.payload), channel_id=1, source_target_pairs={{0,1},{1,0},{2,3},{3,2},{4,12},{5,13},{6,14},{7,15},{8,9},{9,8},{1... | collective-permute-start | bytes 835592 | tf_op jit(solution)/shard_map/ppermute | solution.py:285
  22.4 3.1 %collective-permute-start.3 = (f32[256,256]{1,0:T(8,128)S(1)}, f32[256,256]{1,0:T(8,128)S(1)}, u32[]{:S(2)}, u32[]{:S(2)}) collective-permute-start(f32[256,256]{1,0:T(8,128)S(1)} %get-tuple-element.33), channel_id=1, source_target_pairs={{0,4},{1,5},{2,6},{3,7},{4,0},{5,1},{6,2},{7,3},{8,12},{9,13},{10,... | collective-permute-start | bytes 786440 | tf_op jit(solution)/shard_map/ppermute | solution.py:285
  25.3 2.2 %collective-permute-start.7 = (f32[256,256]{1,0:T(8,128)S(1)}, f32[256,256]{1,0:T(8,128)S(1)}, u32[]{:S(2)}, u32[]{:S(2)}) collective-permute-start(f32[256,256]{1,0:T(8,128)S(1)} %get-tuple-element.40), channel_id=1, source_target_pairs={{0,4},{1,5},{2,6},{3,7},{4,0},{5,1},{6,2},{7,3},{8,12},{9,13},{10,... | collective-permute-start | bytes 786440 | tf_op jit(solution)/shard_map/ppermute | solution.py:285
  25.5 5.0 %collective-permute-start.4 = (f32[128,256]{1,0:T(8,128)S(1)}, f32[128,256]{1,0:T(8,128)S(1)}, u32[]{:S(2)}, u32[]{:S(2)}) collective-permute-start(f32[128,256]{1,0:T(8,128)S(1)} %get-tuple-element.35), channel_id=1, source_target_pairs={{0,16},{1,17},{2,18},{3,19},{4,6},{5,7},{6,4},{7,5},{8,24},{9,25},... | collective-permute-start | bytes 393224 | tf_op jit(solution)/shard_map/ppermute | solution.py:285
  27.5 6.1 %collective-permute-start.8 = (f32[128,256]{1,0:T(8,128)S(1)}, f32[128,256]{1,0:T(8,128)S(1)}, u32[]{:S(2)}, u32[]{:S(2)}) collective-permute-start(f32[128,256]{1,0:T(8,128)S(1)} %get-tuple-element.42), channel_id=1, source_target_pairs={{0,16},{1,17},{2,18},{3,19},{4,6},{5,7},{6,4},{7,5},{8,24},{9,25},... | collective-permute-start | bytes 393224 | tf_op jit(solution)/shard_map/ppermute | solution.py:285
  30.5 5.7 %collective-permute-start.5 = (f32[64,256]{1,0:T(8,128)S(1)}, f32[64,256]{1,0:T(8,128)S(1)}, u32[]{:S(2)}, u32[]{:S(2)}) collective-permute-start(f32[64,256]{1,0:T(8,128)S(1)} %get-tuple-element.37), channel_id=1, source_target_pairs={{0,2},{1,3},{2,0},{3,1},{4,20},{5,21},{6,22},{7,23},{8,10},{9,11},... | collective-permute-start | bytes 196616 | tf_op jit(solution)/shard_map/ppermute | solution.py:285
  33.6 5.2 %collective-permute-start.9 = (f32[64,256]{1,0:T(8,128)S(1)}, f32[64,256]{1,0:T(8,128)S(1)}, u32[]{:S(2)}, u32[]{:S(2)}) collective-permute-start(f32[64,256]{1,0:T(8,128)S(1)} %get-tuple-element.44), channel_id=1, source_target_pairs={{0,2},{1,3},{2,0},{3,1},{4,20},{5,21},{6,22},{7,23},{8,10},{9,11},... | collective-permute-start | bytes 196616 | tf_op jit(solution)/shard_map/ppermute | solution.py:285
  38.9 6.2 %collective-permute-start.10 = (f32[64,256]{1,0:T(8,128)S(1)}, f32[64,256]{1,0:T(8,128)S(1)}, u32[]{:S(2)}, u32[]{:S(2)}) collective-permute-start(f32[64,256]{1,0:T(8,128)S(1)} %intensity.1.refs_0_), channel_id=1, source_target_pairs={{0,3},{1,2},{2,1},{3,0},{4,28},{5,29},{6,30},{7,31},{8,11},{9,10},... | collective-permute-start | bytes 196616 | tf_op jit(solution)/shard_map/ppermute | solution.py:285
  42.1 6.2 %collective-permute-start.13 = (f32[64,256]{1,0:T(8,128)S(1)}, f32[64,256]{1,0:T(8,128)S(1)}, u32[]{:S(2)}, u32[]{:S(2)}) collective-permute-start(f32[64,256]{1,0:T(8,128)S(1)} %intensity.1.refs_0_), channel_id=1, source_target_pairs={{0,24},{1,25},{2,26},{3,27},{4,7},{5,6},{6,5},{7,4},{8,16},{9,17},... | collective-permute-start | bytes 196616 | tf_op jit(solution)/shard_map/ppermute | solution.py:285
  45.1 5.2 %collective-permute-start.14 = (f32[64,256]{1,0:T(8,128)S(1)}, f32[64,256]{1,0:T(8,128)S(1)}, u32[]{:S(2)}, u32[]{:S(2)}) collective-permute-start(f32[64,256]{1,0:T(8,128)S(1)} %collective-permute-done.10.refs_1_), channel_id=1, source_target_pairs={{0,24},{1,25},{2,26},{3,27},{4,7},{5,6},{6,5},{7,4},{8,16},{9,17},... | collective-permute-start | bytes 196616 | tf_op jit(solution)/shard_map/ppermute | solution.py:285
  47.8 2.5 %collective-permute-start.11 = (f32[64,256]{1,0:T(8,128)S(1)}, f32[64,256]{1,0:T(8,128)S(1)}, u32[]{:S(2)}, u32[]{:S(2)}) collective-permute-start(f32[64,256]{1,0:T(8,128)S(1)} %intensity.1.refs_0_), channel_id=1, source_target_pairs={{0,4},{1,5},{2,6},{3,7},{4,0},{5,1},{6,2},{7,3},{8,12},{9,13},{10,... | collective-permute-start | bytes 196616 | tf_op jit(solution)/shard_map/ppermute | solution.py:285
  47.8 2.5 %collective-permute-start.12 = (f32[64,256]{1,0:T(8,128)S(1)}, f32[64,256]{1,0:T(8,128)S(1)}, u32[]{:S(2)}, u32[]{:S(2)}) collective-permute-start(f32[64,256]{1,0:T(8,128)S(1)} %collective-permute-done.10.refs_1_), channel_id=1, source_target_pairs={{0,4},{1,5},{2,6},{3,7},{4,0},{5,1},{6,2},{7,3},{8,12},{9,13},{10,... | collective-permute-start | bytes 196616 | tf_op jit(solution)/shard_map/ppermute | solution.py:285
  48.3 2.0 %collective-permute-start.15 = (f32[64,256]{1,0:T(8,128)S(1)}, f32[64,256]{1,0:T(8,128)S(1)}, u32[]{:S(2)}, u32[]{:S(2)}) collective-permute-start(f32[64,256]{1,0:T(8,128)S(1)} %collective-permute-done.13.refs_4_), channel_id=1, source_target_pairs={{0,4},{1,5},{2,6},{3,7},{4,0},{5,1},{6,2},{7,3},{8,12},{9,13},{10,... | collective-permute-start | bytes 196616 | tf_op jit(solution)/shard_map/ppermute | solution.py:285
  50.3 1.3 %collective-permute-start.16 = (f32[64,256]{1,0:T(8,128)S(1)}, f32[64,256]{1,0:T(8,128)S(1)}, u32[]{:S(2)}, u32[]{:S(2)}) collective-permute-start(f32[64,256]{1,0:T(8,128)S(1)} %collective-permute-done.14.refs_5_), channel_id=1, source_target_pairs={{0,4},{1,5},{2,6},{3,7},{4,0},{5,1},{6,2},{7,3},{8,12},{9,13},{10,... | collective-permute-start | bytes 196616 | tf_op jit(solution)/shard_map/ppermute | solution.py:285

commit v4 on v3

--- a/solution.py
+++ b/solution.py
@@ -17,7 +17,7 @@
 FLIP_BOX = (0b110000, 0b001100, 0b000011)
 AXES = ("bx", "by", "bz")
 POSITIONS = 8
-LAST_PARTS = (4, 2, 2)
+FIRST = 4
 TILE_LIMIT = 53 * 1024 * 1024
 VMEM_LIMIT = 24 * 1024 * 1024
 LARGE = 10**10
@@ -92,11 +92,8 @@
         views.append((seen.at[span], arrays[3].at[span]))
         return [pltpu.make_async_copy(src, dst, sems.at[slot, i]) for i, (src, dst) in enumerate(views)]
 
-    last, start = {}, positions - POSITIONS
-    for slot, count in enumerate(LAST_PARTS, blocks - 1):
-        last[start + POSITIONS - positions] = (start, count, slot)
-        start += count
-    for landing in [(block * POSITIONS, POSITIONS, block) for block in range(blocks - 1)] + list(last.values()):
+    early = [(0, FIRST, blocks), (FIRST, POSITIONS - FIRST, 0)]
+    for landing in early + [(block * POSITIONS, POSITIONS, block) for block in range(1, blocks)]:
         for copy in copies(*landing):
             copy.start()
 
@@ -129,11 +126,11 @@
                     parts = [partial[f, kind, half, pl.ds(row, POSITIONS, stride=8), :] for row in range(8)]
                     out[place, lanes] = sum(parts)
 
-    @pl.loop(0, blocks - 1)
+    compute(0, {landing[0]: landing for landing in early})
+
+    @pl.loop(1, blocks)
     def _(block):
         compute(block, {0: (block * POSITIONS, POSITIONS, block)})
-
-    compute(blocks - 1, last)
 
 
 def accumulate(counts, row_split, col_split, efficiency):
@@ -147,7 +144,7 @@
         out_shape=[jax.ShapeDtypeStruct((tiles, VOX), jnp.float32)] * 2,
         scratch_shapes=[pltpu.VMEM(array.shape, array.dtype) for array in arrays]
         + [
-            pltpu.SemaphoreType.DMA((positions // POSITIONS - 1 + len(LAST_PARTS), 4)),
+            pltpu.SemaphoreType.DMA((positions // POSITIONS + 1, 4)),
             pltpu.VMEM((frames, 2, 2, 8 * POSITIONS, LANES), jnp.float32),
         ],
         compiler_params=pltpu.CompilerParams(vmem_limit_bytes=TILE_LIMIT),
@@ -243,29 +240,46 @@
     out[...] = value[...] * 0.125 / jnp.maximum(weight * 0.125, 1.0)
 
 
-def unfold_kernel(plan, *refs):
-    inputs, out = refs[:-1], refs[-1]
+def unfold(plan, ref, number, write):
     upper = plan.upper(plan.here())
-    own = masked(upper, (4, 2, 1))
     local = masked(upper, plan.flip_local)
     mask = masked(upper, FLIP_VOX)
     index = lax.broadcasted_iota(jnp.int32, (8, LANES), 1) ^ (mask & (LANES - 1))
     turn = lax.broadcasted_iota(jnp.int32, (8, LANES), 0) ^ (local & 7)
     swap = (mask & LANES) != 0
     odd = (lax.axis_index("by") & 1) != 0
+    codes = (number, SWAPPED[number])
+    far = (number & 2) != 0
+    relative = jnp.where(odd, codes[1 - far], codes[far])
+    base = ((relative ^ masked(upper, (4, 2, 1))) * plan.share) ^ (local & ~(plan.share - 1))
+    for group in range(0, plan.share, 8):
+        rows = ref[group : group + 8, :]
+        low, high = rows[:, :LANES], rows[:, LANES:]
+        place = group ^ (local & (plan.share - 1) & ~7)
+        for at, item in enumerate((jnp.where(swap, high, low), jnp.where(swap, low, high))):
+            item = jnp.take_along_axis(item, turn, axis=0, mode="promise_in_bounds")
+            write(base, place, slice(at * LANES, (at + 1) * LANES), lane_gather(item, index))
+    return base
+
+
+def unfold_kernel(plan, *refs):
+    inputs, out = refs[:-1], refs[-1]
+
+    def write(base, place, lanes, item):
+        out[pl.ds(pl.multiple_of(base + place, 8), 8), lanes] = item
+
     for number, ref in enumerate(inputs):
-        codes = (number, SWAPPED[number])
-        far = (number & 2) != 0
-        relative = jnp.where(odd, codes[1 - far], codes[far])
-        base = (relative ^ own) * plan.share
-        for group in range(0, plan.share, 8):
-            rows = ref[group : group + 8, :]
-            low, high = rows[:, :LANES], rows[:, LANES:]
-            target = (base + group) ^ (local & ~7)
-            place = pl.ds(pl.multiple_of(target, 8), 8)
-            for at, item in enumerate((jnp.where(swap, high, low), jnp.where(swap, low, high))):
-                item = jnp.take_along_axis(item, turn, axis=0, mode="promise_in_bounds")
-                out[place, at * LANES : (at + 1) * LANES] = lane_gather(item, index)
+        unfold(plan, ref, number, write)
+
+
+def last_kernel(plan, number, ref, before, out, held, sem):
+    def write(base, place, lanes, item):
+        held[pl.ds(pl.multiple_of(place, 8), 8), lanes] = item
+
+    base = unfold(plan, ref, number, write)
+    copy = pltpu.make_async_copy(held, out.at[pl.ds(pl.multiple_of(base, 8), plan.share)], sem)
+    copy.start()
+    copy.wait()
 
 
 def small_call(kernel, shapes, name, *arrays, flops=1):
@@ -324,7 +338,18 @@
     near.append(swap(near[1], flip_x, flip_z))
     far = [swap(array, flip_y) for array in near]
     ordered = [near[0], near[1], far[0], far[1], near[2], near[3], far[2], far[3]]
-    (result,) = small_call(functools.partial(unfold_kernel, plan), [(plan.boxes, VOX)], "unfold", *ordered)
+    shape = jax.ShapeDtypeStruct((plan.boxes, VOX), jnp.float32)
+    (result,) = small_call(functools.partial(unfold_kernel, plan), [shape.shape], "unfold", *ordered[:-1], flops=LARGE)
+    result = pl.pallas_call(
+        functools.partial(last_kernel, plan, len(ordered) - 1),
+        in_specs=[pl.BlockSpec(memory_space=pltpu.VMEM), pl.BlockSpec(memory_space=pl.ANY)],
+        out_specs=pl.BlockSpec(memory_space=pl.ANY),
+        out_shape=shape,
+        scratch_shapes=[pltpu.VMEM((plan.share, VOX), jnp.float32), pltpu.SemaphoreType.DMA(())],
+        input_output_aliases={1: 0},
+        compiler_params=pltpu.CompilerParams(vmem_limit_bytes=VMEM_LIMIT),
+        name="last",
+    )(ordered[-1], result)
     return result.reshape(GX // plan.sx, GY // plan.sy, GZ // plan.sz, BOX_BRICK, VOX)
 
 

time: 52.7 us -> 52.2 us (level)
  waiting for transfers between devices: 17 us -> 16 us
    ppermute x17, waiting for transfers between devices: 17 us -> 16 us  [swap(): return lax.ppermute(array, AXES, pairs)]
    pallas_call x0 -> x1, Pallas kernels: none -> 0.73 us  [shards(): pl.pallas_call(functools.partial(last_kernel, plan, len(ordered) - 1), in...]
  transfers between devices with their start and end apart: 17 -> 17, of which waited for: 9 -> 9; matrix products, arithmetic and copies ran while one was open for 0% -> 0% of each run, Pallas kernels for 3% -> 5%
where the time goes in v4:
time: 52.2 us; the launch traced here: 52 us
  starting transfers between devices  23.7 us (45%)
  waiting for transfers between devices  16 us (31%)
  Pallas kernels  12.1 us (23%)
    ppermute x17, starting transfers between devices, swap(): return lax.ppermute(array, AXES, pairs)  23.7 us
    ppermute x17, waiting for transfers between devices, swap(): return lax.ppermute(array, AXES, pairs)  16 us
    pallas_call x1, Pallas kernels, accumulate(): pl.pallas_call(accumulate_kernel, in_specs=[pl.BlockSpec(memory_space=pl....  8.61 us
    pallas_call x13, Pallas kernels, small_call(): pl.pallas_call(kernel, out_shape=[jax.ShapeDtypeStruct(shape, jnp.float32...  2.45 us
  transfers between devices with their start and end apart: 17, of which 9 were waited for; matrix products, arithmetic and copies ran while one was open for 0% of the time, Pallas kernels for 5%

profile of v4, /device:TPU:0, one launch (start us, length us, event | category | flops | bytes accessed | tf_op | source)
XLA Modules:
  0.0 52.0 jit_solution(2998394732477183833)
XLA Ops:
  0.0 8.6 %tile_sums.1 = (f32[128,256]{1,0:T(8,128)S(1)}, f32[128,256]{1,0:T(8,128)S(1)}) custom-call(bf16[2,64,128,128]{3,2,1,0:T(8,128)(2,1)} %counts.1, bf16[2,64,128,256]{3,2,1,0:T(8,128)(2,1)} %rows.1, bf16[2,64,128,256]{3,2,1,0:T(8,128)(2,1)} %cols.1, bf16[64,128,128]{2,1,0:T(8,128)(2,1)} %seen.1), custom_call_target="tpu_custom_call" | custom-call | flops 2147483648 | bytes 23068672 | tf_op jit(solution)/shard_map/tile_sums/pallas_call | solution.py:140
  8.7 0.3 payload.1
  9.0 3.0 %collective-permute-start = (f32[136,256]{1,0:T(8,128)S(1)}, f32[136,256]{1,0:T(8,128)S(1)}, u32[]{:S(2)}, u32[]{:S(2)}) collective-permute-start(f32[136,256]{1,0:T(8,128)S(1)} %get-tuple-element.27.first), channel_id=1, source_target_pairs={{0,8},{1,9},{2,10},{3,11},{4,5},{5,4},{6,7},{7,6},{8,0},{9,1},{10,... | collective-permute-start | bytes 417800 | tf_op jit(solution)/shard_map/ppermute | solution.py:299
  12.1 3.0 %collective-permute-done.second = f32[136,256]{1,0:T(8,128)S(1)} collective-permute-done((f32[136,256]{1,0:T(8,128)S(1)}, f32[136,256]{1,0:T(8,128)S(1)}, u32[]{:S(2)}, u32[]{:S(2)}) %collective-permute-start) | collective-permute-done | bytes 139296 | tf_op jit(solution)/shard_map/ppermute | solution.py:299
  15.1 2.2 %collective-permute-start.1 = (f32[272,256]{1,0:T(8,128)S(1)}, f32[272,256]{1,0:T(8,128)S(1)}, u32[]{:S(2)}, u32[]{:S(2)}) collective-permute-start(f32[272,256]{1,0:T(8,128)S(1)} %join.2.payload.rest_0_), channel_id=1, source_target_pairs={{0,1},{1,0},{2,3},{3,2},{4,12},{5,13},{6,14},{7,15},{8,9},{9,8},{1... | collective-permute-start | bytes 835592 | tf_op jit(solution)/shard_map/ppermute | solution.py:299
  17.3 1.5 %collective-permute-start.6 = (f32[272,256]{1,0:T(8,128)S(1)}, f32[272,256]{1,0:T(8,128)S(1)}, u32[]{:S(2)}, u32[]{:S(2)}) collective-permute-start(f32[272,256]{1,0:T(8,128)S(1)} %join.3.payload), channel_id=1, source_target_pairs={{0,1},{1,0},{2,3},{3,2},{4,12},{5,13},{6,14},{7,15},{8,9},{9,8},{1... | collective-permute-start | bytes 835592 | tf_op jit(solution)/shard_map/ppermute | solution.py:299
  19.4 2.4 %collective-permute-done.1.payload = f32[272,256]{1,0:T(8,128)S(1)} collective-permute-done((f32[272,256]{1,0:T(8,128)S(1)}, f32[272,256]{1,0:T(8,128)S(1)}, u32[]{:S(2)}, u32[]{:S(2)}) %collective-permute-start.1) | collective-permute-done | bytes 278560 | tf_op jit(solution)/shard_map/ppermute | solution.py:299
  21.8 0.3 box_sums.6
  22.2 2.6 %collective-permute-done.6.payload = f32[272,256]{1,0:T(8,128)S(1)} collective-permute-done((f32[272,256]{1,0:T(8,128)S(1)}, f32[272,256]{1,0:T(8,128)S(1)}, u32[]{:S(2)}, u32[]{:S(2)}) %collective-permute-start.6) | collective-permute-done | bytes 278560 | tf_op jit(solution)/shard_map/ppermute | solution.py:299
  25.2 2.0 %collective-permute-start.4 = (f32[128,256]{1,0:T(8,128)S(1)}, f32[128,256]{1,0:T(8,128)S(1)}, u32[]{:S(2)}, u32[]{:S(2)}) collective-permute-start(f32[128,256]{1,0:T(8,128)S(1)} %get-tuple-element.35), channel_id=1, source_target_pairs={{0,16},{1,17},{2,18},{3,19},{4,6},{5,7},{6,4},{7,5},{8,24},{9,25},... | collective-permute-start | bytes 393224 | tf_op jit(solution)/shard_map/ppermute | solution.py:299
  27.3 1.5 %collective-permute-start.8 = (f32[128,256]{1,0:T(8,128)S(1)}, f32[128,256]{1,0:T(8,128)S(1)}, u32[]{:S(2)}, u32[]{:S(2)}) collective-permute-start(f32[128,256]{1,0:T(8,128)S(1)} %get-tuple-element.42), channel_id=1, source_target_pairs={{0,16},{1,17},{2,18},{3,19},{4,6},{5,7},{6,4},{7,5},{8,24},{9,25},... | collective-permute-start | bytes 393224 | tf_op jit(solution)/shard_map/ppermute | solution.py:299
  28.7 1.5 %collective-permute-done.4.refs_1_ = f32[128,256]{1,0:T(8,128)S(1)} collective-permute-done((f32[128,256]{1,0:T(8,128)S(1)}, f32[128,256]{1,0:T(8,128)S(1)}, u32[]{:S(2)}, u32[]{:S(2)}) %collective-permute-start.4) | collective-permute-done | bytes 131104 | tf_op jit(solution)/shard_map/ppermute | solution.py:299
  30.2 3.1 %collective-permute-start.5 = (f32[64,256]{1,0:T(8,128)S(1)}, f32[64,256]{1,0:T(8,128)S(1)}, u32[]{:S(2)}, u32[]{:S(2)}) collective-permute-start(f32[64,256]{1,0:T(8,128)S(1)} %get-tuple-element.37), channel_id=1, source_target_pairs={{0,2},{1,3},{2,0},{3,1},{4,20},{5,21},{6,22},{7,23},{8,10},{9,11},... | collective-permute-start | bytes 196616 | tf_op jit(solution)/shard_map/ppermute | solution.py:299
  33.4 1.6 %collective-permute-start.9 = (f32[64,256]{1,0:T(8,128)S(1)}, f32[64,256]{1,0:T(8,128)S(1)}, u32[]{:S(2)}, u32[]{:S(2)}) collective-permute-start(f32[64,256]{1,0:T(8,128)S(1)} %get-tuple-element.44), channel_id=1, source_target_pairs={{0,2},{1,3},{2,0},{3,1},{4,20},{5,21},{6,22},{7,23},{8,10},{9,11},... | collective-permute-start | bytes 196616 | tf_op jit(solution)/shard_map/ppermute | solution.py:299
  35.0 1.0 %collective-permute-done.5.refs_1_ = f32[64,256]{1,0:T(8,128)S(1)} collective-permute-done((f32[64,256]{1,0:T(8,128)S(1)}, f32[64,256]{1,0:T(8,128)S(1)}, u32[]{:S(2)}, u32[]{:S(2)}) %collective-permute-start.5) | collective-permute-done | bytes 65568 | tf_op jit(solution)/shard_map/ppermute | solution.py:299
  36.0 2.6 %collective-permute-done.9.refs_1_ = f32[64,256]{1,0:T(8,128)S(1)} collective-permute-done((f32[64,256]{1,0:T(8,128)S(1)}, f32[64,256]{1,0:T(8,128)S(1)}, u32[]{:S(2)}, u32[]{:S(2)}) %collective-permute-start.9) | collective-permute-done | bytes 65568 | tf_op jit(solution)/shard_map/ppermute | solution.py:299
  38.6 3.2 %collective-permute-start.10 = (f32[64,256]{1,0:T(8,128)S(1)}, f32[64,256]{1,0:T(8,128)S(1)}, u32[]{:S(2)}, u32[]{:S(2)}) collective-permute-start(f32[64,256]{1,0:T(8,128)S(1)} %intensity.1.refs_0_), channel_id=1, source_target_pairs={{0,3},{1,2},{2,1},{3,0},{4,28},{5,29},{6,30},{7,31},{8,11},{9,10},... | collective-permute-start | bytes 196616 | tf_op jit(solution)/shard_map/ppermute | solution.py:299
  41.8 2.3 %collective-permute-start.15 = (f32[64,256]{1,0:T(8,128)S(1)}, f32[64,256]{1,0:T(8,128)S(1)}, u32[]{:S(2)}, u32[]{:S(2)}) collective-permute-start(f32[64,256]{1,0:T(8,128)S(1)} %intensity.1.refs_0_), channel_id=1, source_target_pairs={{0,24},{1,25},{2,26},{3,27},{4,7},{5,6},{6,5},{7,4},{8,16},{9,17},... | collective-permute-start | bytes 196616 | tf_op jit(solution)/shard_map/ppermute | solution.py:299
  44.2 0.7 %collective-permute-done.10.refs_1_ = f32[64,256]{1,0:T(8,128)S(1)} collective-permute-done((f32[64,256]{1,0:T(8,128)S(1)}, f32[64,256]{1,0:T(8,128)S(1)}, u32[]{:S(2)}, u32[]{:S(2)}) %collective-permute-start.10) | collective-permute-done | bytes 65568 | tf_op jit(solution)/shard_map/ppermute | solution.py:299
  44.9 2.6 %collective-permute-start.11 = (f32[64,256]{1,0:T(8,128)S(1)}, f32[64,256]{1,0:T(8,128)S(1)}, u32[]{:S(2)}, u32[]{:S(2)}) collective-permute-start(f32[64,256]{1,0:T(8,128)S(1)} %collective-permute-done.10.refs_1_), channel_id=1, source_target_pairs={{0,24},{1,25},{2,26},{3,27},{4,7},{5,6},{6,5},{7,4},{8,16},{9,17},... | collective-permute-start | bytes 196616 | tf_op jit(solution)/shard_map/ppermute | solution.py:299
  47.5 0.5 collective-permute-start.16
  48.0 2.0 %collective-permute-done.11.refs_5_ = f32[64,256]{1,0:T(8,128)S(1)} collective-permute-done((f32[64,256]{1,0:T(8,128)S(1)}, f32[64,256]{1,0:T(8,128)S(1)}, u32[]{:S(2)}, u32[]{:S(2)}) %collective-permute-start.11) | collective-permute-done | bytes 65568 | tf_op jit(solution)/shard_map/ppermute | solution.py:299
  50.1 1.0 %unfold.1.before = f32[512,256]{1,0:T(8,128)} custom-call(f32[64,256]{1,0:T(8,128)S(1)} %intensity.1.refs_0_, f32[64,256]{1,0:T(8,128)S(1)} %collective-permute-done.10.refs_1_, f32[64,256]{1,0:T(8,128)S(1)} %collective-permute-done.13.refs_2_, f32[64,256]{1,0:T(8,128)S(1)} %collective-permute-done.14.refs_3_, ...), custom_call_target="tpu_custom_call" | custom-call | flops 10000000000 | bytes 1 | tf_op jit(solution)/shard_map/unfold/pallas_call | solution.py:286
  51.3 0.7 %last.1 = f32[512,256]{1,0:T(8,128)} custom-call(f32[64,256]{1,0:T(8,128)S(1)} %collective-permute-done.12.ref, f32[512,256]{1,0:T(8,128)} %unfold.1.before), custom_call_target="tpu_custom_call", output_to_operand_aliasing={{}: (1, {})} | custom-call | tf_op jit(solution)/shard_map/last/pallas_call | solution.py:343
  (34 shorter events, 1.6 us)
Async XLA Ops:
  0.0 8.6 %copy-start.3 = (s32[128]{0:T(128)S(1)}, s32[128]{0:T(128)}, u32[]{:S(2)}) copy-start(s32[128]{0:T(128)} %param.15) | copy-start | bytes 1540
  0.0 8.6 %copy-start.2 = (s32[128,1]{0,1:T(1,128)S(1)}, s32[128,1]{0,1:T(1,128)}, u32[]{:S(2)}) copy-start(s32[128,1]{0,1:T(1,128)} %param.14) | copy-start | bytes 1540
  0.0 8.6 %copy-start.1 = (s32[2]{0:T(128)S(1)}, s32[2]{0:T(128)}, u32[]{:S(2)}) copy-start(s32[2]{0:T(128)} %param.13) | copy-start | bytes 28
  0.0 8.7 %copy-start = (f32[3600]{0:T(1024)S(1)}, f32[3600]{0:T(1024)}, u32[]{:S(2)}) copy-start(f32[3600]{0:T(1024)} %lorentz.1) | copy-start | bytes 43204
  9.0 6.0 %collective-permute-start = (f32[136,256]{1,0:T(8,128)S(1)}, f32[136,256]{1,0:T(8,128)S(1)}, u32[]{:S(2)}, u32[]{:S(2)}) collective-permute-start(f32[136,256]{1,0:T(8,128)S(1)} %get-tuple-element.27.first), channel_id=1, source_target_pairs={{0,8},{1,9},{2,10},{3,11},{4,5},{5,4},{6,7},{7,6},{8,0},{9,1},{10,... | collective-permute-start | bytes 417800 | tf_op jit(solution)/shard_map/ppermute | solution.py:299
  12.0 5.2 %collective-permute-start.2 = (f32[136,256]{1,0:T(8,128)S(1)}, f32[136,256]{1,0:T(8,128)S(1)}, u32[]{:S(2)}, u32[]{:S(2)}) collective-permute-start(f32[136,256]{1,0:T(8,128)S(1)} %get-tuple-element.30.first), channel_id=1, source_target_pairs={{0,8},{1,9},{2,10},{3,11},{4,5},{5,4},{6,7},{7,6},{8,0},{9,1},{10,... | collective-permute-start | bytes 417800 | tf_op jit(solution)/shard_map/ppermute | solution.py:299
  15.1 6.7 %collective-permute-start.1 = (f32[272,256]{1,0:T(8,128)S(1)}, f32[272,256]{1,0:T(8,128)S(1)}, u32[]{:S(2)}, u32[]{:S(2)}) collective-permute-start(f32[272,256]{1,0:T(8,128)S(1)} %join.2.payload.rest_0_), channel_id=1, source_target_pairs={{0,1},{1,0},{2,3},{3,2},{4,12},{5,13},{6,14},{7,15},{8,9},{9,8},{1... | collective-permute-start | bytes 835592 | tf_op jit(solution)/shard_map/ppermute | solution.py:299
  17.3 7.5 %collective-permute-start.6 = (f32[272,256]{1,0:T(8,128)S(1)}, f32[272,256]{1,0:T(8,128)S(1)}, u32[]{:S(2)}, u32[]{:S(2)}) collective-permute-start(f32[272,256]{1,0:T(8,128)S(1)} %join.3.payload), channel_id=1, source_target_pairs={{0,1},{1,0},{2,3},{3,2},{4,12},{5,13},{6,14},{7,15},{8,9},{9,8},{1... | collective-permute-start | bytes 835592 | tf_op jit(solution)/shard_map/ppermute | solution.py:299
  22.1 3.1 %collective-permute-start.3 = (f32[256,256]{1,0:T(8,128)S(1)}, f32[256,256]{1,0:T(8,128)S(1)}, u32[]{:S(2)}, u32[]{:S(2)}) collective-permute-start(f32[256,256]{1,0:T(8,128)S(1)} %get-tuple-element.33), channel_id=1, source_target_pairs={{0,4},{1,5},{2,6},{3,7},{4,0},{5,1},{6,2},{7,3},{8,12},{9,13},{10,... | collective-permute-start | bytes 786440 | tf_op jit(solution)/shard_map/ppermute | solution.py:299
  25.1 2.2 %collective-permute-start.7 = (f32[256,256]{1,0:T(8,128)S(1)}, f32[256,256]{1,0:T(8,128)S(1)}, u32[]{:S(2)}, u32[]{:S(2)}) collective-permute-start(f32[256,256]{1,0:T(8,128)S(1)} %get-tuple-element.40), channel_id=1, source_target_pairs={{0,4},{1,5},{2,6},{3,7},{4,0},{5,1},{6,2},{7,3},{8,12},{9,13},{10,... | collective-permute-start | bytes 786440 | tf_op jit(solution)/shard_map/ppermute | solution.py:299
  25.2 5.0 %collective-permute-start.4 = (f32[128,256]{1,0:T(8,128)S(1)}, f32[128,256]{1,0:T(8,128)S(1)}, u32[]{:S(2)}, u32[]{:S(2)}) collective-permute-start(f32[128,256]{1,0:T(8,128)S(1)} %get-tuple-element.35), channel_id=1, source_target_pairs={{0,16},{1,17},{2,18},{3,19},{4,6},{5,7},{6,4},{7,5},{8,24},{9,25},... | collective-permute-start | bytes 393224 | tf_op jit(solution)/shard_map/ppermute | solution.py:299
  27.3 6.1 %collective-permute-start.8 = (f32[128,256]{1,0:T(8,128)S(1)}, f32[128,256]{1,0:T(8,128)S(1)}, u32[]{:S(2)}, u32[]{:S(2)}) collective-permute-start(f32[128,256]{1,0:T(8,128)S(1)} %get-tuple-element.42), channel_id=1, source_target_pairs={{0,16},{1,17},{2,18},{3,19},{4,6},{5,7},{6,4},{7,5},{8,24},{9,25},... | collective-permute-start | bytes 393224 | tf_op jit(solution)/shard_map/ppermute | solution.py:299
  30.2 5.7 %collective-permute-start.5 = (f32[64,256]{1,0:T(8,128)S(1)}, f32[64,256]{1,0:T(8,128)S(1)}, u32[]{:S(2)}, u32[]{:S(2)}) collective-permute-start(f32[64,256]{1,0:T(8,128)S(1)} %get-tuple-element.37), channel_id=1, source_target_pairs={{0,2},{1,3},{2,0},{3,1},{4,20},{5,21},{6,22},{7,23},{8,10},{9,11},... | collective-permute-start | bytes 196616 | tf_op jit(solution)/shard_map/ppermute | solution.py:299
  33.4 5.2 %collective-permute-start.9 = (f32[64,256]{1,0:T(8,128)S(1)}, f32[64,256]{1,0:T(8,128)S(1)}, u32[]{:S(2)}, u32[]{:S(2)}) collective-permute-start(f32[64,256]{1,0:T(8,128)S(1)} %get-tuple-element.44), channel_id=1, source_target_pairs={{0,2},{1,3},{2,0},{3,1},{4,20},{5,21},{6,22},{7,23},{8,10},{9,11},... | collective-permute-start | bytes 196616 | tf_op jit(solution)/shard_map/ppermute | solution.py:299
  38.6 6.2 %collective-permute-start.10 = (f32[64,256]{1,0:T(8,128)S(1)}, f32[64,256]{1,0:T(8,128)S(1)}, u32[]{:S(2)}, u32[]{:S(2)}) collective-permute-start(f32[64,256]{1,0:T(8,128)S(1)} %intensity.1.refs_0_), channel_id=1, source_target_pairs={{0,3},{1,2},{2,1},{3,0},{4,28},{5,29},{6,30},{7,31},{8,11},{9,10},... | collective-permute-start | bytes 196616 | tf_op jit(solution)/shard_map/ppermute | solution.py:299
  41.8 5.7 %collective-permute-start.15 = (f32[64,256]{1,0:T(8,128)S(1)}, f32[64,256]{1,0:T(8,128)S(1)}, u32[]{:S(2)}, u32[]{:S(2)}) collective-permute-start(f32[64,256]{1,0:T(8,128)S(1)} %intensity.1.refs_0_), channel_id=1, source_target_pairs={{0,24},{1,25},{2,26},{3,27},{4,7},{5,6},{6,5},{7,4},{8,16},{9,17},... | collective-permute-start | bytes 196616 | tf_op jit(solution)/shard_map/ppermute | solution.py:299
  44.9 5.2 %collective-permute-start.11 = (f32[64,256]{1,0:T(8,128)S(1)}, f32[64,256]{1,0:T(8,128)S(1)}, u32[]{:S(2)}, u32[]{:S(2)}) collective-permute-start(f32[64,256]{1,0:T(8,128)S(1)} %collective-permute-done.10.refs_1_), channel_id=1, source_target_pairs={{0,24},{1,25},{2,26},{3,27},{4,7},{5,6},{6,5},{7,4},{8,16},{9,17},... | collective-permute-start | bytes 196616 | tf_op jit(solution)/shard_map/ppermute | solution.py:299
  47.5 2.5 %collective-permute-start.13 = (f32[64,256]{1,0:T(8,128)S(1)}, f32[64,256]{1,0:T(8,128)S(1)}, u32[]{:S(2)}, u32[]{:S(2)}) collective-permute-start(f32[64,256]{1,0:T(8,128)S(1)} %intensity.1.refs_0_), channel_id=1, source_target_pairs={{0,4},{1,5},{2,6},{3,7},{4,0},{5,1},{6,2},{7,3},{8,12},{9,13},{10,... | collective-permute-start | bytes 196616 | tf_op jit(solution)/shard_map/ppermute | solution.py:299
  47.5 2.5 %collective-permute-start.16 = (f32[64,256]{1,0:T(8,128)S(1)}, f32[64,256]{1,0:T(8,128)S(1)}, u32[]{:S(2)}, u32[]{:S(2)}) collective-permute-start(f32[64,256]{1,0:T(8,128)S(1)} %collective-permute-done.15.refs_4_), channel_id=1, source_target_pairs={{0,4},{1,5},{2,6},{3,7},{4,0},{5,1},{6,2},{7,3},{8,12},{9,13},{10,... | collective-permute-start | bytes 196616 | tf_op jit(solution)/shard_map/ppermute | solution.py:299
  48.0 2.0 %collective-permute-start.14 = (f32[64,256]{1,0:T(8,128)S(1)}, f32[64,256]{1,0:T(8,128)S(1)}, u32[]{:S(2)}, u32[]{:S(2)}) collective-permute-start(f32[64,256]{1,0:T(8,128)S(1)} %collective-permute-done.10.refs_1_), channel_id=1, source_target_pairs={{0,4},{1,5},{2,6},{3,7},{4,0},{5,1},{6,2},{7,3},{8,12},{9,13},{10,... | collective-permute-start | bytes 196616 | tf_op jit(solution)/shard_map/ppermute | solution.py:299
  50.0 1.3 %collective-permute-start.12 = (f32[64,256]{1,0:T(8,128)S(1)}, f32[64,256]{1,0:T(8,128)S(1)}, u32[]{:S(2)}, u32[]{:S(2)}) collective-permute-start(f32[64,256]{1,0:T(8,128)S(1)} %collective-permute-done.11.refs_5_), channel_id=1, source_target_pairs={{0,4},{1,5},{2,6},{3,7},{4,0},{5,1},{6,2},{7,3},{8,12},{9,13},{10,... | collective-permute-start | bytes 196616 | tf_op jit(solution)/shard_map/ppermute | solution.py:299

commit v5 on v4

--- a/solution.py
+++ b/solution.py
@@ -170,9 +170,8 @@
     flips = masked(plan.upper(owner[...]), FLIP_VOX)
     flips = jnp.sum(jnp.where(across == down, flips, 0), axis=1, keepdims=True)
     ids = destination(plan, owner[...], box[...])
-    for out in (value_out, weight_out):
-        out[tiles : tiles + 8, :] = jnp.zeros((8, VOX), jnp.float32)
-        out[tiles : tiles + 8, :tiles] = jnp.broadcast_to(ids.astype(jnp.float32), (8, tiles))
+    value_out[tiles : tiles + 8, :] = jnp.zeros((8, VOX), jnp.float32)
+    value_out[tiles : tiles + 8, :tiles] = jnp.broadcast_to(ids.astype(jnp.float32), (8, tiles))
     lanes = lax.broadcasted_iota(jnp.int32, (8, LANES), 1)
     for start in range(0, tiles, 8):
         span = slice(start, start + 8)
@@ -187,21 +186,21 @@
 
 
 def labelled(plan, angles, lorentz, owner, box, value, weight):
-    shape = (value.shape[0] + 8, VOX)
+    tiles = value.shape[0]
     return pl.pallas_call(
         functools.partial(payload_kernel, plan),
-        out_shape=[jax.ShapeDtypeStruct(shape, jnp.float32)] * 2,
+        out_shape=[jax.ShapeDtypeStruct((rows, VOX), jnp.float32) for rows in (tiles + 8, tiles)],
         compiler_params=pltpu.CompilerParams(vmem_limit_bytes=VMEM_LIMIT),
         cost_estimate=pl.CostEstimate(flops=1, bytes_accessed=1, transcendentals=0),
         name="payload",
     )(angles.reshape(1, -1), lorentz, owner, box, value, weight)
 
 
-def scatter_kernel(plan, olds, outs, payload, *refs):
+def scatter_kernel(plan, olds, outs, names, payload, *refs):
     before, after = refs[:olds], refs[len(refs) - outs :]
     tiles = LANES
     half = payload.shape[0] // 2
-    ids = [payload[start + tiles : start + tiles + 1, :tiles] for start in (0, half)]
+    ids = [names[start + tiles : start + tiles + 1, :tiles] for start in (0, names.shape[0] // 2)]
     ids = plan.box_row(jnp.concatenate(ids, axis=1).astype(jnp.int32) ^ (plan.here() * plan.share))
     values = jnp.concatenate([payload[:tiles, :], payload[half : half + tiles, :]], axis=0)
     high = values.astype(jnp.bfloat16)
@@ -311,20 +310,20 @@
     near = [join(own[0], arrived[0])]
     near.append(join(own[1], arrived[1], near[0]))
     far = [swap(array, *gather_steps[::-1]) for array in near]
-    def box_sums(payload, olds, *waits, flops=1):
+    def box_sums(names, payload, olds, *waits, flops=1):
         kernel = functools.partial(scatter_kernel, plan, len(olds), plan.sy)
         shapes = [(4 * plan.share, VOX)] * plan.sy
-        return small_call(kernel, shapes, "box_sums", payload, *olds, *waits, flops=flops)
+        return small_call(kernel, shapes, "box_sums", names, payload, *olds, *waits, flops=flops)
 
     def added(arrays, pieces, flops=1):
         shape = (arrays[0].shape[0] // pieces, VOX)
         kernel = functools.partial(add_kernel, len(arrays))
         return small_call(kernel, [shape] * pieces, "added", *arrays, flops=flops)
 
-    sums = [box_sums(near[0], []), box_sums(near[1], [], flops=LARGE)]
+    sums = [box_sums(near[0], near[0], []), box_sums(near[0], near[1], [], flops=LARGE)]
     pairs, waits = [], [sums[1][0]]
     for kind in range(2):
-        parts = box_sums(far[kind], sums[kind], *waits, flops=LARGE if kind else 1)
+        parts = box_sums(far[0], far[kind], sums[kind], *waits, flops=LARGE if kind else 1)
         waits = [parts[0]]
         parts = [parts[0]] + [swap(parts[i], i * plan.sz) for i in range(1, plan.sy)]
         for even, odd in (reduce_steps, reduce_steps[::-1]):

time: 52.2 us -> 52 us (level)
  no operation moved by 1% of the time
where the time goes in v5:
time: 52 us; the launch traced here: 51.8 us
  starting transfers between devices  23.6 us (45%)
  waiting for transfers between devices  15.9 us (31%)
  Pallas kernels  12.1 us (23%)
    ppermute x17, starting transfers between devices, swap(): return lax.ppermute(array, AXES, pairs)  23.6 us
    ppermute x17, waiting for transfers between devices, swap(): return lax.ppermute(array, AXES, pairs)  15.9 us
    pallas_call x1, Pallas kernels, accumulate(): pl.pallas_call(accumulate_kernel, in_specs=[pl.BlockSpec(memory_space=pl....  8.61 us
    pallas_call x13, Pallas kernels, small_call(): pl.pallas_call(kernel, out_shape=[jax.ShapeDtypeStruct(shape, jnp.float32...  2.46 us
  transfers between devices with their start and end apart: 17, of which 9 were waited for; matrix products, arithmetic and copies ran while one was open for 0% of the time, Pallas kernels for 5%

profile of v5, /device:TPU:0, one launch (start us, length us, event | category | flops | bytes accessed | tf_op | source)
XLA Modules:
  0.0 51.8 jit_solution(11896806491855640772)
XLA Ops:
  0.0 8.6 %tile_sums.1 = (f32[128,256]{1,0:T(8,128)S(1)}, f32[128,256]{1,0:T(8,128)S(1)}) custom-call(bf16[2,64,128,128]{3,2,1,0:T(8,128)(2,1)} %counts.1, bf16[2,64,128,256]{3,2,1,0:T(8,128)(2,1)} %rows.1, bf16[2,64,128,256]{3,2,1,0:T(8,128)(2,1)} %cols.1, bf16[64,128,128]{2,1,0:T(8,128)(2,1)} %seen.1), custom_call_target="tpu_custom_call" | custom-call | flops 2147483648 | bytes 23068672 | tf_op jit(solution)/shard_map/tile_sums/pallas_call | solution.py:140
  9.0 3.0 %collective-permute-start = (f32[136,256]{1,0:T(8,128)S(1)}, f32[136,256]{1,0:T(8,128)S(1)}, u32[]{:S(2)}, u32[]{:S(2)}) collective-permute-start(f32[136,256]{1,0:T(8,128)S(1)} %get-tuple-element.27.first), channel_id=1, source_target_pairs={{0,8},{1,9},{2,10},{3,11},{4,5},{5,4},{6,7},{7,6},{8,0},{9,1},{10,... | collective-permute-start | bytes 417800 | tf_op jit(solution)/shard_map/ppermute | solution.py:298
  12.1 3.0 %collective-permute-done.second = f32[136,256]{1,0:T(8,128)S(1)} collective-permute-done((f32[136,256]{1,0:T(8,128)S(1)}, f32[136,256]{1,0:T(8,128)S(1)}, u32[]{:S(2)}, u32[]{:S(2)}) %collective-permute-start) | collective-permute-done | bytes 139296 | tf_op jit(solution)/shard_map/ppermute | solution.py:298
  15.1 2.2 %collective-permute-start.1 = (f32[272,256]{1,0:T(8,128)S(1)}, f32[272,256]{1,0:T(8,128)S(1)}, u32[]{:S(2)}, u32[]{:S(2)}) collective-permute-start(f32[272,256]{1,0:T(8,128)S(1)} %join.2.names.payload.rest_0_), channel_id=1, source_target_pairs={{0,1},{1,0},{2,3},{3,2},{4,12},{5,13},{6,14},{7,15},{8,9},{9,8},{1... | collective-permute-start | bytes 835592 | tf_op jit(solution)/shard_map/ppermute | solution.py:298
  17.2 1.4 %collective-permute-start.6 = (f32[256,256]{1,0:T(8,128)S(1)}, f32[256,256]{1,0:T(8,128)S(1)}, u32[]{:S(2)}, u32[]{:S(2)}) collective-permute-start(f32[256,256]{1,0:T(8,128)S(1)} %join.3.payload), channel_id=1, source_target_pairs={{0,1},{1,0},{2,3},{3,2},{4,12},{5,13},{6,14},{7,15},{8,9},{9,8},{1... | collective-permute-start | bytes 786440 | tf_op jit(solution)/shard_map/ppermute | solution.py:298
  19.3 2.5 %collective-permute-done.1.names.payload = f32[272,256]{1,0:T(8,128)S(1)} collective-permute-done((f32[272,256]{1,0:T(8,128)S(1)}, f32[272,256]{1,0:T(8,128)S(1)}, u32[]{:S(2)}, u32[]{:S(2)}) %collective-permute-start.1) | collective-permute-done | bytes 278560 | tf_op jit(solution)/shard_map/ppermute | solution.py:298
  21.8 0.3 box_sums.6
  22.2 2.4 %collective-permute-done.6.payload = f32[256,256]{1,0:T(8,128)S(1)} collective-permute-done((f32[256,256]{1,0:T(8,128)S(1)}, f32[256,256]{1,0:T(8,128)S(1)}, u32[]{:S(2)}, u32[]{:S(2)}) %collective-permute-start.6) | collective-permute-done | bytes 262176 | tf_op jit(solution)/shard_map/ppermute | solution.py:298
  24.6 0.3 box_sums.7
  25.0 2.0 %collective-permute-start.4 = (f32[128,256]{1,0:T(8,128)S(1)}, f32[128,256]{1,0:T(8,128)S(1)}, u32[]{:S(2)}, u32[]{:S(2)}) collective-permute-start(f32[128,256]{1,0:T(8,128)S(1)} %get-tuple-element.35), channel_id=1, source_target_pairs={{0,16},{1,17},{2,18},{3,19},{4,6},{5,7},{6,4},{7,5},{8,24},{9,25},... | collective-permute-start | bytes 393224 | tf_op jit(solution)/shard_map/ppermute | solution.py:298
  27.1 1.5 %collective-permute-start.8 = (f32[128,256]{1,0:T(8,128)S(1)}, f32[128,256]{1,0:T(8,128)S(1)}, u32[]{:S(2)}, u32[]{:S(2)}) collective-permute-start(f32[128,256]{1,0:T(8,128)S(1)} %get-tuple-element.42), channel_id=1, source_target_pairs={{0,16},{1,17},{2,18},{3,19},{4,6},{5,7},{6,4},{7,5},{8,24},{9,25},... | collective-permute-start | bytes 393224 | tf_op jit(solution)/shard_map/ppermute | solution.py:298
  28.6 1.5 %collective-permute-done.4.refs_1_ = f32[128,256]{1,0:T(8,128)S(1)} collective-permute-done((f32[128,256]{1,0:T(8,128)S(1)}, f32[128,256]{1,0:T(8,128)S(1)}, u32[]{:S(2)}, u32[]{:S(2)}) %collective-permute-start.4) | collective-permute-done | bytes 131104 | tf_op jit(solution)/shard_map/ppermute | solution.py:298
  30.1 3.1 %collective-permute-start.5 = (f32[64,256]{1,0:T(8,128)S(1)}, f32[64,256]{1,0:T(8,128)S(1)}, u32[]{:S(2)}, u32[]{:S(2)}) collective-permute-start(f32[64,256]{1,0:T(8,128)S(1)} %get-tuple-element.37), channel_id=1, source_target_pairs={{0,2},{1,3},{2,0},{3,1},{4,20},{5,21},{6,22},{7,23},{8,10},{9,11},... | collective-permute-start | bytes 196616 | tf_op jit(solution)/shard_map/ppermute | solution.py:298
  33.2 1.6 %collective-permute-start.9 = (f32[64,256]{1,0:T(8,128)S(1)}, f32[64,256]{1,0:T(8,128)S(1)}, u32[]{:S(2)}, u32[]{:S(2)}) collective-permute-start(f32[64,256]{1,0:T(8,128)S(1)} %get-tuple-element.44), channel_id=1, source_target_pairs={{0,2},{1,3},{2,0},{3,1},{4,20},{5,21},{6,22},{7,23},{8,10},{9,11},... | collective-permute-start | bytes 196616 | tf_op jit(solution)/shard_map/ppermute | solution.py:298
  34.8 1.0 %collective-permute-done.5.refs_1_ = f32[64,256]{1,0:T(8,128)S(1)} collective-permute-done((f32[64,256]{1,0:T(8,128)S(1)}, f32[64,256]{1,0:T(8,128)S(1)}, u32[]{:S(2)}, u32[]{:S(2)}) %collective-permute-start.5) | collective-permute-done | bytes 65568 | tf_op jit(solution)/shard_map/ppermute | solution.py:298
  35.8 2.6 %collective-permute-done.9.refs_1_ = f32[64,256]{1,0:T(8,128)S(1)} collective-permute-done((f32[64,256]{1,0:T(8,128)S(1)}, f32[64,256]{1,0:T(8,128)S(1)}, u32[]{:S(2)}, u32[]{:S(2)}) %collective-permute-start.9) | collective-permute-done | bytes 65568 | tf_op jit(solution)/shard_map/ppermute | solution.py:298
  38.5 3.2 %collective-permute-start.10 = (f32[64,256]{1,0:T(8,128)S(1)}, f32[64,256]{1,0:T(8,128)S(1)}, u32[]{:S(2)}, u32[]{:S(2)}) collective-permute-start(f32[64,256]{1,0:T(8,128)S(1)} %intensity.1.refs_0_), channel_id=1, source_target_pairs={{0,3},{1,2},{2,1},{3,0},{4,28},{5,29},{6,30},{7,31},{8,11},{9,10},... | collective-permute-start | bytes 196616 | tf_op jit(solution)/shard_map/ppermute | solution.py:298
  41.6 2.3 %collective-permute-start.15 = (f32[64,256]{1,0:T(8,128)S(1)}, f32[64,256]{1,0:T(8,128)S(1)}, u32[]{:S(2)}, u32[]{:S(2)}) collective-permute-start(f32[64,256]{1,0:T(8,128)S(1)} %intensity.1.refs_0_), channel_id=1, source_target_pairs={{0,24},{1,25},{2,26},{3,27},{4,7},{5,6},{6,5},{7,4},{8,16},{9,17},... | collective-permute-start | bytes 196616 | tf_op jit(solution)/shard_map/ppermute | solution.py:298
  44.0 0.7 %collective-permute-done.10.refs_1_ = f32[64,256]{1,0:T(8,128)S(1)} collective-permute-done((f32[64,256]{1,0:T(8,128)S(1)}, f32[64,256]{1,0:T(8,128)S(1)}, u32[]{:S(2)}, u32[]{:S(2)}) %collective-permute-start.10) | collective-permute-done | bytes 65568 | tf_op jit(solution)/shard_map/ppermute | solution.py:298
  44.7 2.6 %collective-permute-start.11 = (f32[64,256]{1,0:T(8,128)S(1)}, f32[64,256]{1,0:T(8,128)S(1)}, u32[]{:S(2)}, u32[]{:S(2)}) collective-permute-start(f32[64,256]{1,0:T(8,128)S(1)} %collective-permute-done.10.refs_1_), channel_id=1, source_target_pairs={{0,24},{1,25},{2,26},{3,27},{4,7},{5,6},{6,5},{7,4},{8,16},{9,17},... | collective-permute-start | bytes 196616 | tf_op jit(solution)/shard_map/ppermute | solution.py:298
  47.3 0.5 collective-permute-start.16
  47.8 2.0 %collective-permute-done.11.refs_5_ = f32[64,256]{1,0:T(8,128)S(1)} collective-permute-done((f32[64,256]{1,0:T(8,128)S(1)}, f32[64,256]{1,0:T(8,128)S(1)}, u32[]{:S(2)}, u32[]{:S(2)}) %collective-permute-start.11) | collective-permute-done | bytes 65568 | tf_op jit(solution)/shard_map/ppermute | solution.py:298
  49.9 1.0 %unfold.1.before = f32[512,256]{1,0:T(8,128)} custom-call(f32[64,256]{1,0:T(8,128)S(1)} %intensity.1.refs_0_, f32[64,256]{1,0:T(8,128)S(1)} %collective-permute-done.10.refs_1_, f32[64,256]{1,0:T(8,128)S(1)} %collective-permute-done.13.refs_2_, f32[64,256]{1,0:T(8,128)S(1)} %collective-permute-done.14.refs_3_, ...), custom_call_target="tpu_custom_call" | custom-call | flops 10000000000 | bytes 1 | tf_op jit(solution)/shard_map/unfold/pallas_call | solution.py:285
  51.1 0.7 %last.1 = f32[512,256]{1,0:T(8,128)} custom-call(f32[64,256]{1,0:T(8,128)S(1)} %collective-permute-done.12.ref, f32[512,256]{1,0:T(8,128)} %unfold.1.before), custom_call_target="tpu_custom_call", output_to_operand_aliasing={{}: (1, {})} | custom-call | tf_op jit(solution)/shard_map/last/pallas_call | solution.py:342
  (34 shorter events, 1.6 us)
Async XLA Ops:
  0.0 8.6 %copy-start.3 = (s32[128]{0:T(128)S(1)}, s32[128]{0:T(128)}, u32[]{:S(2)}) copy-start(s32[128]{0:T(128)} %param.15) | copy-start | bytes 1540
  0.0 8.6 %copy-start.2 = (s32[128,1]{0,1:T(1,128)S(1)}, s32[128,1]{0,1:T(1,128)}, u32[]{:S(2)}) copy-start(s32[128,1]{0,1:T(1,128)} %param.14) | copy-start | bytes 1540
  0.0 8.6 %copy-start.1 = (s32[2]{0:T(128)S(1)}, s32[2]{0:T(128)}, u32[]{:S(2)}) copy-start(s32[2]{0:T(128)} %param.13) | copy-start | bytes 28
  0.0 8.7 %copy-start = (f32[3600]{0:T(1024)S(1)}, f32[3600]{0:T(1024)}, u32[]{:S(2)}) copy-start(f32[3600]{0:T(1024)} %lorentz.1) | copy-start | bytes 43204
  9.0 6.0 %collective-permute-start = (f32[136,256]{1,0:T(8,128)S(1)}, f32[136,256]{1,0:T(8,128)S(1)}, u32[]{:S(2)}, u32[]{:S(2)}) collective-permute-start(f32[136,256]{1,0:T(8,128)S(1)} %get-tuple-element.27.first), channel_id=1, source_target_pairs={{0,8},{1,9},{2,10},{3,11},{4,5},{5,4},{6,7},{7,6},{8,0},{9,1},{10,... | collective-permute-start | bytes 417800 | tf_op jit(solution)/shard_map/ppermute | solution.py:298
  12.0 5.2 %collective-permute-start.2 = (f32[128,256]{1,0:T(8,128)S(1)}, f32[128,256]{1,0:T(8,128)S(1)}, u32[]{:S(2)}, u32[]{:S(2)}) collective-permute-start(f32[128,256]{1,0:T(8,128)S(1)} %get-tuple-element.30.first), channel_id=1, source_target_pairs={{0,8},{1,9},{2,10},{3,11},{4,5},{5,4},{6,7},{7,6},{8,0},{9,1},{10,... | collective-permute-start | bytes 393224 | tf_op jit(solution)/shard_map/ppermute | solution.py:298
  15.1 6.7 %collective-permute-start.1 = (f32[272,256]{1,0:T(8,128)S(1)}, f32[272,256]{1,0:T(8,128)S(1)}, u32[]{:S(2)}, u32[]{:S(2)}) collective-permute-start(f32[272,256]{1,0:T(8,128)S(1)} %join.2.names.payload.rest_0_), channel_id=1, source_target_pairs={{0,1},{1,0},{2,3},{3,2},{4,12},{5,13},{6,14},{7,15},{8,9},{9,8},{1... | collective-permute-start | bytes 835592 | tf_op jit(solution)/shard_map/ppermute | solution.py:298
  17.2 7.3 %collective-permute-start.6 = (f32[256,256]{1,0:T(8,128)S(1)}, f32[256,256]{1,0:T(8,128)S(1)}, u32[]{:S(2)}, u32[]{:S(2)}) collective-permute-start(f32[256,256]{1,0:T(8,128)S(1)} %join.3.payload), channel_id=1, source_target_pairs={{0,1},{1,0},{2,3},{3,2},{4,12},{5,13},{6,14},{7,15},{8,9},{9,8},{1... | collective-permute-start | bytes 786440 | tf_op jit(solution)/shard_map/ppermute | solution.py:298
  22.1 2.9 %collective-permute-start.3 = (f32[256,256]{1,0:T(8,128)S(1)}, f32[256,256]{1,0:T(8,128)S(1)}, u32[]{:S(2)}, u32[]{:S(2)}) collective-permute-start(f32[256,256]{1,0:T(8,128)S(1)} %get-tuple-element.33), channel_id=1, source_target_pairs={{0,4},{1,5},{2,6},{3,7},{4,0},{5,1},{6,2},{7,3},{8,12},{9,13},{10,... | collective-permute-start | bytes 786440 | tf_op jit(solution)/shard_map/ppermute | solution.py:298
  24.9 2.2 %collective-permute-start.7 = (f32[256,256]{1,0:T(8,128)S(1)}, f32[256,256]{1,0:T(8,128)S(1)}, u32[]{:S(2)}, u32[]{:S(2)}) collective-permute-start(f32[256,256]{1,0:T(8,128)S(1)} %get-tuple-element.40), channel_id=1, source_target_pairs={{0,4},{1,5},{2,6},{3,7},{4,0},{5,1},{6,2},{7,3},{8,12},{9,13},{10,... | collective-permute-start | bytes 786440 | tf_op jit(solution)/shard_map/ppermute | solution.py:298
  25.0 5.0 %collective-permute-start.4 = (f32[128,256]{1,0:T(8,128)S(1)}, f32[128,256]{1,0:T(8,128)S(1)}, u32[]{:S(2)}, u32[]{:S(2)}) collective-permute-start(f32[128,256]{1,0:T(8,128)S(1)} %get-tuple-element.35), channel_id=1, source_target_pairs={{0,16},{1,17},{2,18},{3,19},{4,6},{5,7},{6,4},{7,5},{8,24},{9,25},... | collective-permute-start | bytes 393224 | tf_op jit(solution)/shard_map/ppermute | solution.py:298
  27.1 6.1 %collective-permute-start.8 = (f32[128,256]{1,0:T(8,128)S(1)}, f32[128,256]{1,0:T(8,128)S(1)}, u32[]{:S(2)}, u32[]{:S(2)}) collective-permute-start(f32[128,256]{1,0:T(8,128)S(1)} %get-tuple-element.42), channel_id=1, source_target_pairs={{0,16},{1,17},{2,18},{3,19},{4,6},{5,7},{6,4},{7,5},{8,24},{9,25},... | collective-permute-start | bytes 393224 | tf_op jit(solution)/shard_map/ppermute | solution.py:298
  30.1 5.7 %collective-permute-start.5 = (f32[64,256]{1,0:T(8,128)S(1)}, f32[64,256]{1,0:T(8,128)S(1)}, u32[]{:S(2)}, u32[]{:S(2)}) collective-permute-start(f32[64,256]{1,0:T(8,128)S(1)} %get-tuple-element.37), channel_id=1, source_target_pairs={{0,2},{1,3},{2,0},{3,1},{4,20},{5,21},{6,22},{7,23},{8,10},{9,11},... | collective-permute-start | bytes 196616 | tf_op jit(solution)/shard_map/ppermute | solution.py:298
  33.2 5.2 %collective-permute-start.9 = (f32[64,256]{1,0:T(8,128)S(1)}, f32[64,256]{1,0:T(8,128)S(1)}, u32[]{:S(2)}, u32[]{:S(2)}) collective-permute-start(f32[64,256]{1,0:T(8,128)S(1)} %get-tuple-element.44), channel_id=1, source_target_pairs={{0,2},{1,3},{2,0},{3,1},{4,20},{5,21},{6,22},{7,23},{8,10},{9,11},... | collective-permute-start | bytes 196616 | tf_op jit(solution)/shard_map/ppermute | solution.py:298
  38.5 6.2 %collective-permute-start.10 = (f32[64,256]{1,0:T(8,128)S(1)}, f32[64,256]{1,0:T(8,128)S(1)}, u32[]{:S(2)}, u32[]{:S(2)}) collective-permute-start(f32[64,256]{1,0:T(8,128)S(1)} %intensity.1.refs_0_), channel_id=1, source_target_pairs={{0,3},{1,2},{2,1},{3,0},{4,28},{5,29},{6,30},{7,31},{8,11},{9,10},... | collective-permute-start | bytes 196616 | tf_op jit(solution)/shard_map/ppermute | solution.py:298
  41.6 5.7 %collective-permute-start.15 = (f32[64,256]{1,0:T(8,128)S(1)}, f32[64,256]{1,0:T(8,128)S(1)}, u32[]{:S(2)}, u32[]{:S(2)}) collective-permute-start(f32[64,256]{1,0:T(8,128)S(1)} %intensity.1.refs_0_), channel_id=1, source_target_pairs={{0,24},{1,25},{2,26},{3,27},{4,7},{5,6},{6,5},{7,4},{8,16},{9,17},... | collective-permute-start | bytes 196616 | tf_op jit(solution)/shard_map/ppermute | solution.py:298
  44.7 5.2 %collective-permute-start.11 = (f32[64,256]{1,0:T(8,128)S(1)}, f32[64,256]{1,0:T(8,128)S(1)}, u32[]{:S(2)}, u32[]{:S(2)}) collective-permute-start(f32[64,256]{1,0:T(8,128)S(1)} %collective-permute-done.10.refs_1_), channel_id=1, source_target_pairs={{0,24},{1,25},{2,26},{3,27},{4,7},{5,6},{6,5},{7,4},{8,16},{9,17},... | collective-permute-start | bytes 196616 | tf_op jit(solution)/shard_map/ppermute | solution.py:298
  47.3 2.5 %collective-permute-start.13 = (f32[64,256]{1,0:T(8,128)S(1)}, f32[64,256]{1,0:T(8,128)S(1)}, u32[]{:S(2)}, u32[]{:S(2)}) collective-permute-start(f32[64,256]{1,0:T(8,128)S(1)} %intensity.1.refs_0_), channel_id=1, source_target_pairs={{0,4},{1,5},{2,6},{3,7},{4,0},{5,1},{6,2},{7,3},{8,12},{9,13},{10,... | collective-permute-start | bytes 196616 | tf_op jit(solution)/shard_map/ppermute | solution.py:298
  47.3 2.5 %collective-permute-start.16 = (f32[64,256]{1,0:T(8,128)S(1)}, f32[64,256]{1,0:T(8,128)S(1)}, u32[]{:S(2)}, u32[]{:S(2)}) collective-permute-start(f32[64,256]{1,0:T(8,128)S(1)} %collective-permute-done.15.refs_4_), channel_id=1, source_target_pairs={{0,4},{1,5},{2,6},{3,7},{4,0},{5,1},{6,2},{7,3},{8,12},{9,13},{10,... | collective-permute-start | bytes 196616 | tf_op jit(solution)/shard_map/ppermute | solution.py:298
  47.8 2.0 %collective-permute-start.14 = (f32[64,256]{1,0:T(8,128)S(1)}, f32[64,256]{1,0:T(8,128)S(1)}, u32[]{:S(2)}, u32[]{:S(2)}) collective-permute-start(f32[64,256]{1,0:T(8,128)S(1)} %collective-permute-done.10.refs_1_), channel_id=1, source_target_pairs={{0,4},{1,5},{2,6},{3,7},{4,0},{5,1},{6,2},{7,3},{8,12},{9,13},{10,... | collective-permute-start | bytes 196616 | tf_op jit(solution)/shard_map/ppermute | solution.py:298
  49.9 1.3 %collective-permute-start.12 = (f32[64,256]{1,0:T(8,128)S(1)}, f32[64,256]{1,0:T(8,128)S(1)}, u32[]{:S(2)}, u32[]{:S(2)}) collective-permute-start(f32[64,256]{1,0:T(8,128)S(1)} %collective-permute-done.11.refs_5_), channel_id=1, source_target_pairs={{0,4},{1,5},{2,6},{3,7},{4,0},{5,1},{6,2},{7,3},{8,12},{9,13},{10,... | collective-permute-start | bytes 196616 | tf_op jit(solution)/shard_map/ppermute | solution.py:298

commit v6 on v4

--- a/solution.py
+++ b/solution.py
@@ -45,7 +45,7 @@
 
     def steps(self):
         row = self.sy * self.sz
-        return (row, 1), (2 * row, 2)
+        return (1, row), (2 * row, 2)
 
     def box_row(self, place):
         (gather_a, gather_b), (first, second) = self.steps()

time: 52.2 us -> 52.2 us (level)
  no operation moved by 1% of the time
where the time goes in v6:
time: 52.2 us; the launch traced here: 52 us
  starting transfers between devices  23.7 us (45%)
  waiting for transfers between devices  16 us (31%)
  Pallas kernels  12.1 us (23%)
    ppermute x17, starting transfers between devices, swap(): return lax.ppermute(array, AXES, pairs)  23.7 us
    ppermute x17, waiting for transfers between devices, swap(): return lax.ppermute(array, AXES, pairs)  16 us
    pallas_call x1, Pallas kernels, accumulate(): pl.pallas_call(accumulate_kernel, in_specs=[pl.BlockSpec(memory_space=pl....  8.61 us
    pallas_call x13, Pallas kernels, small_call(): pl.pallas_call(kernel, out_shape=[jax.ShapeDtypeStruct(shape, jnp.float32...  2.46 us
  transfers between devices with their start and end apart: 17, of which 9 were waited for; matrix products, arithmetic and copies ran while one was open for 0% of the time, Pallas kernels for 5%

profile of v6, /device:TPU:0, one launch (start us, length us, event | category | flops | bytes accessed | tf_op | source)
XLA Modules:
  0.0 52.0 jit_solution(10125184002127216735)
XLA Ops:
  0.0 8.6 %tile_sums.1 = (f32[128,256]{1,0:T(8,128)S(1)}, f32[128,256]{1,0:T(8,128)S(1)}) custom-call(bf16[2,64,128,128]{3,2,1,0:T(8,128)(2,1)} %counts.1, bf16[2,64,128,256]{3,2,1,0:T(8,128)(2,1)} %rows.1, bf16[2,64,128,256]{3,2,1,0:T(8,128)(2,1)} %cols.1, bf16[64,128,128]{2,1,0:T(8,128)(2,1)} %seen.1), custom_call_target="tpu_custom_call" | custom-call | flops 2147483648 | bytes 23068672 | tf_op jit(solution)/shard_map/tile_sums/pallas_call | solution.py:140
  8.7 0.3 payload.1
  9.0 3.1 %collective-permute-start = (f32[136,256]{1,0:T(8,128)S(1)}, f32[136,256]{1,0:T(8,128)S(1)}, u32[]{:S(2)}, u32[]{:S(2)}) collective-permute-start(f32[136,256]{1,0:T(8,128)S(1)} %get-tuple-element.27.first), channel_id=1, source_target_pairs={{0,1},{1,0},{2,3},{3,2},{4,12},{5,13},{6,14},{7,15},{8,9},{9,8},{1... | collective-permute-start | bytes 417800 | tf_op jit(solution)/shard_map/ppermute | solution.py:299
  12.2 3.0 %collective-permute-done.second = f32[136,256]{1,0:T(8,128)S(1)} collective-permute-done((f32[136,256]{1,0:T(8,128)S(1)}, f32[136,256]{1,0:T(8,128)S(1)}, u32[]{:S(2)}, u32[]{:S(2)}) %collective-permute-start) | collective-permute-done | bytes 139296 | tf_op jit(solution)/shard_map/ppermute | solution.py:299
  15.1 2.0 %collective-permute-start.1 = (f32[272,256]{1,0:T(8,128)S(1)}, f32[272,256]{1,0:T(8,128)S(1)}, u32[]{:S(2)}, u32[]{:S(2)}) collective-permute-start(f32[272,256]{1,0:T(8,128)S(1)} %join.2.payload.rest_0_), channel_id=1, source_target_pairs={{0,8},{1,9},{2,10},{3,11},{4,5},{5,4},{6,7},{7,6},{8,0},{9,1},{10,... | collective-permute-start | bytes 835592 | tf_op jit(solution)/shard_map/ppermute | solution.py:299
  17.2 1.5 %collective-permute-start.6 = (f32[272,256]{1,0:T(8,128)S(1)}, f32[272,256]{1,0:T(8,128)S(1)}, u32[]{:S(2)}, u32[]{:S(2)}) collective-permute-start(f32[272,256]{1,0:T(8,128)S(1)} %join.3.payload), channel_id=1, source_target_pairs={{0,8},{1,9},{2,10},{3,11},{4,5},{5,4},{6,7},{7,6},{8,0},{9,1},{10,... | collective-permute-start | bytes 835592 | tf_op jit(solution)/shard_map/ppermute | solution.py:299
  19.4 2.4 %collective-permute-done.1.payload = f32[272,256]{1,0:T(8,128)S(1)} collective-permute-done((f32[272,256]{1,0:T(8,128)S(1)}, f32[272,256]{1,0:T(8,128)S(1)}, u32[]{:S(2)}, u32[]{:S(2)}) %collective-permute-start.1) | collective-permute-done | bytes 278560 | tf_op jit(solution)/shard_map/ppermute | solution.py:299
  21.8 0.3 box_sums.6
  22.2 2.6 %collective-permute-done.6.payload = f32[272,256]{1,0:T(8,128)S(1)} collective-permute-done((f32[272,256]{1,0:T(8,128)S(1)}, f32[272,256]{1,0:T(8,128)S(1)}, u32[]{:S(2)}, u32[]{:S(2)}) %collective-permute-start.6) | collective-permute-done | bytes 278560 | tf_op jit(solution)/shard_map/ppermute | solution.py:299
  25.2 2.0 %collective-permute-start.4 = (f32[128,256]{1,0:T(8,128)S(1)}, f32[128,256]{1,0:T(8,128)S(1)}, u32[]{:S(2)}, u32[]{:S(2)}) collective-permute-start(f32[128,256]{1,0:T(8,128)S(1)} %get-tuple-element.35), channel_id=1, source_target_pairs={{0,16},{1,17},{2,18},{3,19},{4,6},{5,7},{6,4},{7,5},{8,24},{9,25},... | collective-permute-start | bytes 393224 | tf_op jit(solution)/shard_map/ppermute | solution.py:299
  27.3 1.5 %collective-permute-start.8 = (f32[128,256]{1,0:T(8,128)S(1)}, f32[128,256]{1,0:T(8,128)S(1)}, u32[]{:S(2)}, u32[]{:S(2)}) collective-permute-start(f32[128,256]{1,0:T(8,128)S(1)} %get-tuple-element.42), channel_id=1, source_target_pairs={{0,16},{1,17},{2,18},{3,19},{4,6},{5,7},{6,4},{7,5},{8,24},{9,25},... | collective-permute-start | bytes 393224 | tf_op jit(solution)/shard_map/ppermute | solution.py:299
  28.7 1.5 %collective-permute-done.4.refs_1_ = f32[128,256]{1,0:T(8,128)S(1)} collective-permute-done((f32[128,256]{1,0:T(8,128)S(1)}, f32[128,256]{1,0:T(8,128)S(1)}, u32[]{:S(2)}, u32[]{:S(2)}) %collective-permute-start.4) | collective-permute-done | bytes 131104 | tf_op jit(solution)/shard_map/ppermute | solution.py:299
  30.2 3.1 %collective-permute-start.5 = (f32[64,256]{1,0:T(8,128)S(1)}, f32[64,256]{1,0:T(8,128)S(1)}, u32[]{:S(2)}, u32[]{:S(2)}) collective-permute-start(f32[64,256]{1,0:T(8,128)S(1)} %get-tuple-element.37), channel_id=1, source_target_pairs={{0,2},{1,3},{2,0},{3,1},{4,20},{5,21},{6,22},{7,23},{8,10},{9,11},... | collective-permute-start | bytes 196616 | tf_op jit(solution)/shard_map/ppermute | solution.py:299
  33.4 1.6 %collective-permute-start.9 = (f32[64,256]{1,0:T(8,128)S(1)}, f32[64,256]{1,0:T(8,128)S(1)}, u32[]{:S(2)}, u32[]{:S(2)}) collective-permute-start(f32[64,256]{1,0:T(8,128)S(1)} %get-tuple-element.44), channel_id=1, source_target_pairs={{0,2},{1,3},{2,0},{3,1},{4,20},{5,21},{6,22},{7,23},{8,10},{9,11},... | collective-permute-start | bytes 196616 | tf_op jit(solution)/shard_map/ppermute | solution.py:299
  35.0 1.0 %collective-permute-done.5.refs_1_ = f32[64,256]{1,0:T(8,128)S(1)} collective-permute-done((f32[64,256]{1,0:T(8,128)S(1)}, f32[64,256]{1,0:T(8,128)S(1)}, u32[]{:S(2)}, u32[]{:S(2)}) %collective-permute-start.5) | collective-permute-done | bytes 65568 | tf_op jit(solution)/shard_map/ppermute | solution.py:299
  36.0 2.6 %collective-permute-done.9.refs_1_ = f32[64,256]{1,0:T(8,128)S(1)} collective-permute-done((f32[64,256]{1,0:T(8,128)S(1)}, f32[64,256]{1,0:T(8,128)S(1)}, u32[]{:S(2)}, u32[]{:S(2)}) %collective-permute-start.9) | collective-permute-done | bytes 65568 | tf_op jit(solution)/shard_map/ppermute | solution.py:299
  38.6 3.2 %collective-permute-start.10 = (f32[64,256]{1,0:T(8,128)S(1)}, f32[64,256]{1,0:T(8,128)S(1)}, u32[]{:S(2)}, u32[]{:S(2)}) collective-permute-start(f32[64,256]{1,0:T(8,128)S(1)} %intensity.1.refs_0_), channel_id=1, source_target_pairs={{0,3},{1,2},{2,1},{3,0},{4,28},{5,29},{6,30},{7,31},{8,11},{9,10},... | collective-permute-start | bytes 196616 | tf_op jit(solution)/shard_map/ppermute | solution.py:299
  41.8 2.3 %collective-permute-start.15 = (f32[64,256]{1,0:T(8,128)S(1)}, f32[64,256]{1,0:T(8,128)S(1)}, u32[]{:S(2)}, u32[]{:S(2)}) collective-permute-start(f32[64,256]{1,0:T(8,128)S(1)} %intensity.1.refs_0_), channel_id=1, source_target_pairs={{0,24},{1,25},{2,26},{3,27},{4,7},{5,6},{6,5},{7,4},{8,16},{9,17},... | collective-permute-start | bytes 196616 | tf_op jit(solution)/shard_map/ppermute | solution.py:299
  44.2 0.7 %collective-permute-done.10.refs_1_ = f32[64,256]{1,0:T(8,128)S(1)} collective-permute-done((f32[64,256]{1,0:T(8,128)S(1)}, f32[64,256]{1,0:T(8,128)S(1)}, u32[]{:S(2)}, u32[]{:S(2)}) %collective-permute-start.10) | collective-permute-done | bytes 65568 | tf_op jit(solution)/shard_map/ppermute | solution.py:299
  44.9 2.6 %collective-permute-start.11 = (f32[64,256]{1,0:T(8,128)S(1)}, f32[64,256]{1,0:T(8,128)S(1)}, u32[]{:S(2)}, u32[]{:S(2)}) collective-permute-start(f32[64,256]{1,0:T(8,128)S(1)} %collective-permute-done.10.refs_1_), channel_id=1, source_target_pairs={{0,24},{1,25},{2,26},{3,27},{4,7},{5,6},{6,5},{7,4},{8,16},{9,17},... | collective-permute-start | bytes 196616 | tf_op jit(solution)/shard_map/ppermute | solution.py:299
  47.5 0.5 collective-permute-start.16
  48.0 2.0 %collective-permute-done.11.refs_5_ = f32[64,256]{1,0:T(8,128)S(1)} collective-permute-done((f32[64,256]{1,0:T(8,128)S(1)}, f32[64,256]{1,0:T(8,128)S(1)}, u32[]{:S(2)}, u32[]{:S(2)}) %collective-permute-start.11) | collective-permute-done | bytes 65568 | tf_op jit(solution)/shard_map/ppermute | solution.py:299
  50.1 1.0 %unfold.1.before = f32[512,256]{1,0:T(8,128)} custom-call(f32[64,256]{1,0:T(8,128)S(1)} %intensity.1.refs_0_, f32[64,256]{1,0:T(8,128)S(1)} %collective-permute-done.10.refs_1_, f32[64,256]{1,0:T(8,128)S(1)} %collective-permute-done.13.refs_2_, f32[64,256]{1,0:T(8,128)S(1)} %collective-permute-done.14.refs_3_, ...), custom_call_target="tpu_custom_call" | custom-call | flops 10000000000 | bytes 1 | tf_op jit(solution)/shard_map/unfold/pallas_call | solution.py:286
  51.3 0.7 %last.1 = f32[512,256]{1,0:T(8,128)} custom-call(f32[64,256]{1,0:T(8,128)S(1)} %collective-permute-done.12.ref, f32[512,256]{1,0:T(8,128)} %unfold.1.before), custom_call_target="tpu_custom_call", output_to_operand_aliasing={{}: (1, {})} | custom-call | tf_op jit(solution)/shard_map/last/pallas_call | solution.py:343
  (34 shorter events, 1.6 us)
Async XLA Ops:
  0.0 8.6 %copy-start.3 = (s32[128]{0:T(128)S(1)}, s32[128]{0:T(128)}, u32[]{:S(2)}) copy-start(s32[128]{0:T(128)} %param.15) | copy-start | bytes 1540
  0.0 8.6 %copy-start.2 = (s32[128,1]{0,1:T(1,128)S(1)}, s32[128,1]{0,1:T(1,128)}, u32[]{:S(2)}) copy-start(s32[128,1]{0,1:T(1,128)} %param.14) | copy-start | bytes 1540
  0.0 8.6 %copy-start.1 = (s32[2]{0:T(128)S(1)}, s32[2]{0:T(128)}, u32[]{:S(2)}) copy-start(s32[2]{0:T(128)} %param.13) | copy-start | bytes 28
  0.0 8.7 %copy-start = (f32[3600]{0:T(1024)S(1)}, f32[3600]{0:T(1024)}, u32[]{:S(2)}) copy-start(f32[3600]{0:T(1024)} %lorentz.1) | copy-start | bytes 43204
  9.0 6.1 %collective-permute-start = (f32[136,256]{1,0:T(8,128)S(1)}, f32[136,256]{1,0:T(8,128)S(1)}, u32[]{:S(2)}, u32[]{:S(2)}) collective-permute-start(f32[136,256]{1,0:T(8,128)S(1)} %get-tuple-element.27.first), channel_id=1, source_target_pairs={{0,1},{1,0},{2,3},{3,2},{4,12},{5,13},{6,14},{7,15},{8,9},{9,8},{1... | collective-permute-start | bytes 417800 | tf_op jit(solution)/shard_map/ppermute | solution.py:299
  12.1 5.1 %collective-permute-start.2 = (f32[136,256]{1,0:T(8,128)S(1)}, f32[136,256]{1,0:T(8,128)S(1)}, u32[]{:S(2)}, u32[]{:S(2)}) collective-permute-start(f32[136,256]{1,0:T(8,128)S(1)} %get-tuple-element.30.first), channel_id=1, source_target_pairs={{0,1},{1,0},{2,3},{3,2},{4,12},{5,13},{6,14},{7,15},{8,9},{9,8},{1... | collective-permute-start | bytes 417800 | tf_op jit(solution)/shard_map/ppermute | solution.py:299
  15.1 6.6 %collective-permute-start.1 = (f32[272,256]{1,0:T(8,128)S(1)}, f32[272,256]{1,0:T(8,128)S(1)}, u32[]{:S(2)}, u32[]{:S(2)}) collective-permute-start(f32[272,256]{1,0:T(8,128)S(1)} %join.2.payload.rest_0_), channel_id=1, source_target_pairs={{0,8},{1,9},{2,10},{3,11},{4,5},{5,4},{6,7},{7,6},{8,0},{9,1},{10,... | collective-permute-start | bytes 835592 | tf_op jit(solution)/shard_map/ppermute | solution.py:299
  17.2 7.6 %collective-permute-start.6 = (f32[272,256]{1,0:T(8,128)S(1)}, f32[272,256]{1,0:T(8,128)S(1)}, u32[]{:S(2)}, u32[]{:S(2)}) collective-permute-start(f32[272,256]{1,0:T(8,128)S(1)} %join.3.payload), channel_id=1, source_target_pairs={{0,8},{1,9},{2,10},{3,11},{4,5},{5,4},{6,7},{7,6},{8,0},{9,1},{10,... | collective-permute-start | bytes 835592 | tf_op jit(solution)/shard_map/ppermute | solution.py:299
  22.1 3.1 %collective-permute-start.3 = (f32[256,256]{1,0:T(8,128)S(1)}, f32[256,256]{1,0:T(8,128)S(1)}, u32[]{:S(2)}, u32[]{:S(2)}) collective-permute-start(f32[256,256]{1,0:T(8,128)S(1)} %get-tuple-element.33), channel_id=1, source_target_pairs={{0,4},{1,5},{2,6},{3,7},{4,0},{5,1},{6,2},{7,3},{8,12},{9,13},{10,... | collective-permute-start | bytes 786440 | tf_op jit(solution)/shard_map/ppermute | solution.py:299
  25.1 2.2 %collective-permute-start.7 = (f32[256,256]{1,0:T(8,128)S(1)}, f32[256,256]{1,0:T(8,128)S(1)}, u32[]{:S(2)}, u32[]{:S(2)}) collective-permute-start(f32[256,256]{1,0:T(8,128)S(1)} %get-tuple-element.40), channel_id=1, source_target_pairs={{0,4},{1,5},{2,6},{3,7},{4,0},{5,1},{6,2},{7,3},{8,12},{9,13},{10,... | collective-permute-start | bytes 786440 | tf_op jit(solution)/shard_map/ppermute | solution.py:299
  25.2 5.0 %collective-permute-start.4 = (f32[128,256]{1,0:T(8,128)S(1)}, f32[128,256]{1,0:T(8,128)S(1)}, u32[]{:S(2)}, u32[]{:S(2)}) collective-permute-start(f32[128,256]{1,0:T(8,128)S(1)} %get-tuple-element.35), channel_id=1, source_target_pairs={{0,16},{1,17},{2,18},{3,19},{4,6},{5,7},{6,4},{7,5},{8,24},{9,25},... | collective-permute-start | bytes 393224 | tf_op jit(solution)/shard_map/ppermute | solution.py:299
  27.3 6.1 %collective-permute-start.8 = (f32[128,256]{1,0:T(8,128)S(1)}, f32[128,256]{1,0:T(8,128)S(1)}, u32[]{:S(2)}, u32[]{:S(2)}) collective-permute-start(f32[128,256]{1,0:T(8,128)S(1)} %get-tuple-element.42), channel_id=1, source_target_pairs={{0,16},{1,17},{2,18},{3,19},{4,6},{5,7},{6,4},{7,5},{8,24},{9,25},... | collective-permute-start | bytes 393224 | tf_op jit(solution)/shard_map/ppermute | solution.py:299
  30.2 5.7 %collective-permute-start.5 = (f32[64,256]{1,0:T(8,128)S(1)}, f32[64,256]{1,0:T(8,128)S(1)}, u32[]{:S(2)}, u32[]{:S(2)}) collective-permute-start(f32[64,256]{1,0:T(8,128)S(1)} %get-tuple-element.37), channel_id=1, source_target_pairs={{0,2},{1,3},{2,0},{3,1},{4,20},{5,21},{6,22},{7,23},{8,10},{9,11},... | collective-permute-start | bytes 196616 | tf_op jit(solution)/shard_map/ppermute | solution.py:299
  33.4 5.2 %collective-permute-start.9 = (f32[64,256]{1,0:T(8,128)S(1)}, f32[64,256]{1,0:T(8,128)S(1)}, u32[]{:S(2)}, u32[]{:S(2)}) collective-permute-start(f32[64,256]{1,0:T(8,128)S(1)} %get-tuple-element.44), channel_id=1, source_target_pairs={{0,2},{1,3},{2,0},{3,1},{4,20},{5,21},{6,22},{7,23},{8,10},{9,11},... | collective-permute-start | bytes 196616 | tf_op jit(solution)/shard_map/ppermute | solution.py:299
  38.6 6.2 %collective-permute-start.10 = (f32[64,256]{1,0:T(8,128)S(1)}, f32[64,256]{1,0:T(8,128)S(1)}, u32[]{:S(2)}, u32[]{:S(2)}) collective-permute-start(f32[64,256]{1,0:T(8,128)S(1)} %intensity.1.refs_0_), channel_id=1, source_target_pairs={{0,3},{1,2},{2,1},{3,0},{4,28},{5,29},{6,30},{7,31},{8,11},{9,10},... | collective-permute-start | bytes 196616 | tf_op jit(solution)/shard_map/ppermute | solution.py:299
  41.8 5.7 %collective-permute-start.15 = (f32[64,256]{1,0:T(8,128)S(1)}, f32[64,256]{1,0:T(8,128)S(1)}, u32[]{:S(2)}, u32[]{:S(2)}) collective-permute-start(f32[64,256]{1,0:T(8,128)S(1)} %intensity.1.refs_0_), channel_id=1, source_target_pairs={{0,24},{1,25},{2,26},{3,27},{4,7},{5,6},{6,5},{7,4},{8,16},{9,17},... | collective-permute-start | bytes 196616 | tf_op jit(solution)/shard_map/ppermute | solution.py:299
  44.9 5.2 %collective-permute-start.11 = (f32[64,256]{1,0:T(8,128)S(1)}, f32[64,256]{1,0:T(8,128)S(1)}, u32[]{:S(2)}, u32[]{:S(2)}) collective-permute-start(f32[64,256]{1,0:T(8,128)S(1)} %collective-permute-done.10.refs_1_), channel_id=1, source_target_pairs={{0,24},{1,25},{2,26},{3,27},{4,7},{5,6},{6,5},{7,4},{8,16},{9,17},... | collective-permute-start | bytes 196616 | tf_op jit(solution)/shard_map/ppermute | solution.py:299
  47.5 2.5 %collective-permute-start.13 = (f32[64,256]{1,0:T(8,128)S(1)}, f32[64,256]{1,0:T(8,128)S(1)}, u32[]{:S(2)}, u32[]{:S(2)}) collective-permute-start(f32[64,256]{1,0:T(8,128)S(1)} %intensity.1.refs_0_), channel_id=1, source_target_pairs={{0,4},{1,5},{2,6},{3,7},{4,0},{5,1},{6,2},{7,3},{8,12},{9,13},{10,... | collective-permute-start | bytes 196616 | tf_op jit(solution)/shard_map/ppermute | solution.py:299
  47.5 2.5 %collective-permute-start.16 = (f32[64,256]{1,0:T(8,128)S(1)}, f32[64,256]{1,0:T(8,128)S(1)}, u32[]{:S(2)}, u32[]{:S(2)}) collective-permute-start(f32[64,256]{1,0:T(8,128)S(1)} %collective-permute-done.15.refs_4_), channel_id=1, source_target_pairs={{0,4},{1,5},{2,6},{3,7},{4,0},{5,1},{6,2},{7,3},{8,12},{9,13},{10,... | collective-permute-start | bytes 196616 | tf_op jit(solution)/shard_map/ppermute | solution.py:299
  48.0 2.0 %collective-permute-start.14 = (f32[64,256]{1,0:T(8,128)S(1)}, f32[64,256]{1,0:T(8,128)S(1)}, u32[]{:S(2)}, u32[]{:S(2)}) collective-permute-start(f32[64,256]{1,0:T(8,128)S(1)} %collective-permute-done.10.refs_1_), channel_id=1, source_target_pairs={{0,4},{1,5},{2,6},{3,7},{4,0},{5,1},{6,2},{7,3},{8,12},{9,13},{10,... | collective-permute-start | bytes 196616 | tf_op jit(solution)/shard_map/ppermute | solution.py:299
  50.0 1.3 %collective-permute-start.12 = (f32[64,256]{1,0:T(8,128)S(1)}, f32[64,256]{1,0:T(8,128)S(1)}, u32[]{:S(2)}, u32[]{:S(2)}) collective-permute-start(f32[64,256]{1,0:T(8,128)S(1)} %collective-permute-done.11.refs_5_), channel_id=1, source_target_pairs={{0,4},{1,5},{2,6},{3,7},{4,0},{5,1},{6,2},{7,3},{8,12},{9,13},{10,... | collective-permute-start | bytes 196616 | tf_op jit(solution)/shard_map/ppermute | solution.py:299
